TPU v7x, 32 devices: a whole 2x2x4 slice. The times are simulated.
32 devices in a mesh: groups: 2 (over y), ctx: 4 (over z), head: 2 (over x), sub: 2 (over core).
Axes of the slice: x: 2, y: 2, z: 4, core: 2. Of those that a mesh axis runs over, the one named last changes fastest.
Arguments:
- queries: bfloat16 [4096, 4096], P(('groups', 'ctx'), ('head', 'sub')), parts along dimension 0, may hold values from -6 to 6
- keys: bfloat16 [4096, 2, 4096], P(('groups', 'ctx'), None, ('head', 'sub')), parts along dimension 0, may hold values from -6 to 6
- values: bfloat16 [4096, 2, 4096], P(('groups', 'ctx'), None, ('head', 'sub')), parts along dimension 0, may hold values from -0.59765625 to 0.59765625
- betas: float32 [4096, 2, 32], P(('groups', 'ctx'), None, ('head', 'sub')), parts along dimension 0, may hold values from 0.3 to 2
- log_decay: float32 [4096, 32], P(('groups', 'ctx'), ('head', 'sub')), parts along dimension 0, may hold values from -1.5 to 0, as said below
- attn_queries: bfloat16 [4096, 4096], P(('groups', 'ctx'), ('head', 'sub')), parts along dimension 0, may hold values from -24 to 24
- attn_keys: bfloat16 [4096, 4096], P(('groups', 'ctx'), ('head', 'sub')), parts along dimension 0, may hold values from -24 to 24
Outputs:
- retained: bfloat16 [4096, 4096], P(('groups', 'ctx'), ('head', 'sub')), parts along dimension 0
- attended: bfloat16 [4096, 4096], P(('groups', 'ctx'), ('head', 'sub')), parts along dimension 0
There are 2 independent parts, one for each index of `groups`. A program takes and returns all parts, laid end to end along the dimension named above; each array names one. Nothing has to cross between parts.
Inputs may be any that keep to these rules, and one draw needn't show every extreme that they name: `log_decay`: logarithms of decays; a few tokens of each head take sudden drops, which may fall on the same token.
All inputs are finite; a program needn't handle non-finite values.
Results may differ from a plain program's by a relative error of at most 0.0057.
Values may be sent and summed in bfloat16 or wider, within the bound.
No kernel may reach another device: no remote copies, remote signals or barrier semaphores. Data moves between devices by JAX's collectives and lax.ppermute only.
A program may use at most 128 MiB of HBM per device.

v0:
```python
import jax
import jax.numpy as jnp
from jax import lax
from jax.sharding import PartitionSpec as P

NREF = 2
SPAN = 32


highest = lax.Precision.HIGHEST


def from_behind(array, axis, by):
    length = lax.axis_size(axis)
    pairs = [(i, i + by) for i in range(length) if 0 <= i + by < length]
    return lax.ppermute(array, axis, pairs)


def unit_rows(matrix):
    return matrix * lax.rsqrt(jnp.sum(matrix * matrix, axis=-1, keepdims=True) + 1e-06)


def arrange(block_queries, block_keys, block_values, block_betas, segment_forgetting):
    count = block_queries.shape[0]
    heads = block_betas.shape[2]
    width = block_queries.shape[1] // heads
    query_heads = block_queries.reshape(count, heads, width).transpose(1, 0, 2).astype(jnp.float32)
    key_heads = (
        block_keys.reshape(count, NREF, heads, width)
        .transpose(2, 0, 1, 3)
        .reshape(heads, count * NREF, width)
        .astype(jnp.float32)
    )
    value_heads = (
        block_values.reshape(count, NREF, heads, width)
        .transpose(2, 0, 1, 3)
        .reshape(heads, count * NREF, width)
        .astype(jnp.float32)
    )
    beta_heads = block_betas.transpose(2, 0, 1).reshape(heads, count * NREF)
    stepped = jnp.concatenate(
        [
            segment_forgetting[:, None, :],
            jnp.zeros((count, NREF - 1, heads), segment_forgetting.dtype),
        ],
        axis=1,
    )
    decay_heads = stepped.transpose(2, 0, 1).reshape(heads, count * NREF)
    return (unit_rows(query_heads), unit_rows(key_heads), value_heads, beta_heads, decay_heads)


def span_factors(key_rows, value_rows, beta_rows, decay_rows):
    size = key_rows.shape[0]
    width = key_rows.shape[1]
    level = jnp.cumsum(decay_rows)
    gram = jnp.dot(key_rows, key_rows.T, precision=highest)
    spread = jnp.minimum(level[:, None] - level[None, :], 0.0)
    below = jnp.arange(size)[:, None] > jnp.arange(size)[None, :]
    mixing = jnp.where(below, beta_rows[:, None] * jnp.exp(spread) * gram, 0.0) + jnp.eye(
        size, dtype=key_rows.dtype
    )
    sides = jnp.concatenate(
        [beta_rows[:, None] * value_rows, (beta_rows * jnp.exp(level))[:, None] * key_rows], axis=1
    )
    solved = jax.scipy.linalg.solve_triangular(mixing, sides, lower=True, unit_diagonal=True)
    written = solved[:, :width]
    carried = solved[:, width:]
    trailing = jnp.exp(level[-1] - level)
    transition = jnp.exp(level[-1]) * jnp.eye(width, dtype=key_rows.dtype) - jnp.dot(
        (trailing[:, None] * carried).T, key_rows, precision=highest
    )
    addition = jnp.dot((trailing[:, None] * written).T, key_rows, precision=highest)
    return (written, carried, level, transition, addition)


def span_outputs(state, query_rows, key_rows, written, carried, level):
    count = query_rows.shape[0]
    size = key_rows.shape[0]
    fresh = written - jnp.dot(carried, state.T, precision=highest)
    reached = level[NREF - 1 :: NREF]
    spread = jnp.minimum(reached[:, None] - level[None, :], 0.0)
    visible = jnp.arange(size)[None, :] <= NREF * jnp.arange(count)[:, None] + NREF - 1
    weights = jnp.where(
        visible, jnp.exp(spread) * jnp.dot(query_rows, key_rows.T, precision=highest), 0.0
    )
    return jnp.exp(reached)[:, None] * jnp.dot(query_rows, state.T, precision=highest) + jnp.dot(
        weights, fresh, precision=highest
    )


def compose(earlier, later):
    joined = jnp.einsum("hab,hbc->hac", earlier[0], later[0], precision=highest)
    carried = jnp.einsum("hab,hbc->hac", earlier[1], later[0], precision=highest) + later[1]
    return (joined, carried)


def block_attention(block_queries, block_keys, block_values, earlier_ok, heads):
    count = block_queries.shape[0]
    width = block_queries.shape[1] // heads
    query_heads = block_queries.reshape(count, heads, width)
    key_heads = block_keys.reshape(2 * count, heads, width)
    value_heads = block_values.reshape(2 * count, heads, width)
    attention_scores = jnp.einsum(
        "qhd,khd->hqk", query_heads, key_heads, preferred_element_type=jnp.float32
    ) * width ** (-0.5)
    position = jnp.arange(2 * count)[None, :]
    ownrow = jnp.arange(count)[:, None]
    allowed = jnp.where(position >= count, position - count <= ownrow, earlier_ok)
    attention_scores = jnp.where(allowed[None], attention_scores, -1e30)
    largest = jnp.max(attention_scores, axis=2, keepdims=True)
    expanded = jnp.exp(attention_scores - largest)
    weights = (expanded / jnp.sum(expanded, axis=2, keepdims=True)).astype(jnp.bfloat16)
    mixed = jnp.einsum("hqk,khd->qhd", weights, value_heads, preferred_element_type=jnp.float32)
    return mixed.reshape(count, heads * width).astype(jnp.bfloat16)


def per_device(queries, keys, values, betas, log_decay, attn_queries, attn_keys):
    heads = betas.shape[2]
    width = queries.shape[1] // heads
    tokens_here = queries.shape[0]
    blocks = tokens_here // SPAN
    query_heads, key_heads, value_heads, beta_heads, decay_heads = jax.vmap(arrange)(
        queries.reshape(blocks, SPAN, heads * width),
        keys.reshape(blocks, SPAN, NREF, heads * width),
        values.reshape(blocks, SPAN, NREF, heads * width),
        betas.reshape(blocks, SPAN, NREF, heads),
        log_decay.reshape(blocks, SPAN, heads),
    )
    written, carried, level, transition, addition = jax.vmap(jax.vmap(span_factors))(
        key_heads, value_heads, beta_heads, decay_heads
    )
    identity = jnp.broadcast_to(jnp.eye(width, dtype=jnp.float32), (heads, width, width))
    nothing = jnp.zeros((heads, width, width), jnp.float32)

    def gather_pair(partial_state_pair, span_pair):
        return (compose(partial_state_pair, span_pair), None)

    (whole_transition, whole_addition), unused = lax.scan(
        gather_pair, (identity, nothing), (transition, addition)
    )

    def relay(counter, arriving):
        leaving = (
            jnp.einsum("hab,hbc->hac", arriving, whole_transition, precision=highest)
            + whole_addition
        )
        return from_behind(leaving, "ctx", 1)

    incoming = lax.fori_loop(0, lax.axis_size("ctx") - 1, relay, nothing)

    def advance(state, pieces):
        (
            span_queries,
            span_keys,
            span_written,
            span_carried,
            span_level,
            span_transition,
            span_addition,
        ) = pieces
        produced = jax.vmap(span_outputs)(
            state, span_queries, span_keys, span_written, span_carried, span_level
        )
        following = (
            jnp.einsum("hab,hbc->hac", state, span_transition, precision=highest) + span_addition
        )
        return (following, produced)

    closing_memory_matrix, produced = lax.scan(
        advance, incoming, (query_heads, key_heads, written, carried, level, transition, addition)
    )
    retained = (
        produced.transpose(0, 2, 1, 3).reshape(tokens_here, heads * width).astype(jnp.bfloat16)
    )
    earlier_keys, earlier_values = from_behind((attn_keys, retained), "ctx", 1)
    joined_keys = jnp.concatenate([earlier_keys, attn_keys], axis=0)
    joined_values = jnp.concatenate([earlier_values, retained], axis=0)
    attended = block_attention(
        attn_queries, joined_keys, joined_values, lax.axis_index("ctx") > 0, heads
    )
    return (retained, attended)


def solution(mesh):
    return jax.shard_map(
        per_device,
        mesh=mesh,
        in_specs=(
            P(("groups", "ctx"), ("head", "sub")),
            P(("groups", "ctx"), None, ("head", "sub")),
            P(("groups", "ctx"), None, ("head", "sub")),
            P(("groups", "ctx"), None, ("head", "sub")),
            P(("groups", "ctx"), ("head", "sub")),
            P(("groups", "ctx"), ("head", "sub")),
            P(("groups", "ctx"), ("head", "sub")),
        ),
        out_specs=(P(("groups", "ctx"), ("head", "sub")), P(("groups", "ctx"), ("head", "sub"))),
        check_vma=False,
    )
```

profile of v0, /device:TPU:16, one launch (start us, length us, event | category | flops | bytes accessed | tf_op | source)
XLA Modules:
  0.0 1073.7 jit_solution(3387656800160925149)
XLA Ops:
  1.8 3.5 reduce_window_sum.11
  6.9 4.6 reshape.169
  11.6 4.2 convert_multiply_fusion
  15.7 6.4 mul.150
  22.1 3.6 reduce_sum.27
  26.3 4.4 copy.81
  30.9 3.9 broadcast_multiply_fusion
  36.7 8.8 add_bitcast_fusion
  45.4 630.6 %custom-call.4 = f32[16,8,1,64,64]{3,4,2,1,0:T(8,128)} custom-call(f32[16,8,1,64,64]{4,3,2,1,0:T(8,128)} %add_bitcast_fusion), custom_call_target="InvertDiagBlocksLowerTriangular" | custom-call | tf_op jit(solution)/shard_map/vmap(vmap(jit(_solve_triangular)))/triangular_solve | solution.py:65
  676.0 4.7 reshape.170
  680.7 4.4 copy.85
  685.2 2.6 broadcast_multiply_fusion.1
  687.8 11.7 %fusion.26 = f32[16,8,64,256]{3,2,1,0:T(8,128)S(1)} fusion(f32[16,8,64,128]{3,2,1,0:T(8,128)} %get-tuple-element.373, f32[16,8,64,128]{3,2,1,0:T(8,128)} %broadcast_multiply_fusion.1, f32[16,8,1,64,64]{3,4,2,1,0:T(8,128)} %custom-call.4), kind=kOutput, calls=%fused_computation.42 | convolution fusion | flops 1612709888 | bytes 18874368 | tf_op jit(solution)/shard_map/vmap(vmap(jit(_solve_triangular)))/triangular_solve | solution.py:65
  699.6 4.8 fusion.59
  706.4 17.0 %fusion.35 = f32[16,8,128,128]{2,3,1,0:T(8,128)} fusion(f32[16,8,64,128]{3,2,1,0:T(8,128)S(1)} %copy-done.2, f32[16,8,64]{2,1,0:T(8,128)S(1)} %get-tuple-element.377, f32[16,8,64,256]{3,2,1,0:T(8,128)S(1)} %fusion.26), kind=kOutput, calls=%fused_computation.52 | convolution fusion | flops 1611661312 | bytes 16842752 | tf_op jit(solution)/shard_map/vmap(vmap())/dot_general | solution.py:72
  723.5 20.3 %multiply_subtract_fusion = f32[16,8,128,128]{3,2,1,0:T(8,128)} fusion(f32[128,128]{1,0:T(8,128)S(1)} %fusion.51, f32[16,8]{1,0:T(8,128)S(1)} %copy.77, f32[16,8,64,128]{3,2,1,0:T(8,128)} %copy-done.1, f32[16,8,64]{2,1,0:T(8,128)S(1)} %get-tuple-element.377, f32[16,8,64,256]{3,2,1,0:T(8,128)} %copy-done.3), kind=kOutput, calls=%fused_computation.48 | convolution fusion | flops 1615855616 | bytes 16876032 | tf_op jit(solution)/shard_map/vmap(vmap())/dot_general | solution.py:69
  743.8 9.2 copy.88
  753.1 58.9 %while.41 = (s32[]{:T(128)}, f32[8,128,128]{1,2,0:T(8,128)S(1)}, f32[8,128,128]{1,2,0:T(8,128)S(1)}, f32[16,8,128,128]{2,3,1,0:T(8,128)}, f32[16,8,128,128]{2,3,1,0:T(8,128)}, /*index=5*/s32[]{:T(128)}, s32[]{:T(128)}) while((s32[]{:T(128)}, f32[8,128,128]{1,2,0:T(8,128)S(1)}, f32[8,128,128]{1,2,0:T(8,128)S(1)}, ...), condition=%wide.region_3.4_spmd.clone, body=%wide.region_2.0_spmd.clone.sunk | while | flops 402915328 | bytes 5768791 | solution.py:138
  812.4 46.1 %while.39 = (s32[]{:T(128)}, f32[8,128,128]{2,1,0:T(8,128)S(1)}, f32[8,128,128]{2,1,0:T(8,128)S(1)}, f32[8,128,128]{2,1,0:T(8,128)S(1)}, s32[]{:T(128)}) while((s32[]{:T(128)}, f32[8,128,128]{2,1,0:T(8,128)S(1)}, f32[8,128,128]{2,1,0:T(8,128)S(1)}, f32[8,128,128]{2,1,0:T(8,128)S(1)}, s32[]{:T(128)}) %tuple.89), condition=%wide.region_5.6_spmd, body=%wide.region_4.5_spmd.sunk | while | flops 201457664 | bytes 4194405 | solution.py:149
  813.1 3.5 collective-permute-start
  816.6 12.1 %collective-permute-done = f32[8,128,128]{2,1,0:T(8,128)S(1)} collective-permute-done((f32[8,128,128]{2,1,0:T(8,128)S(1)}, f32[8,128,128]{2,1,0:T(8,128)S(1)}, u32[]{:S(2)}, u32[]{:S(2)}) %collective-permute-start) | collective-permute-done | bytes 524320 | tf_op jit(solution)/shard_map/while/body/eval_jaxpr/ppermute | solution.py:16
  829.3 3.5 collective-permute-start
  832.8 11.2 %collective-permute-done = f32[8,128,128]{2,1,0:T(8,128)S(1)} collective-permute-done((f32[8,128,128]{2,1,0:T(8,128)S(1)}, f32[8,128,128]{2,1,0:T(8,128)S(1)}, u32[]{:S(2)}, u32[]{:S(2)}) %collective-permute-start) | collective-permute-done | bytes 524320 | tf_op jit(solution)/shard_map/while/body/eval_jaxpr/ppermute | solution.py:16
  844.6 3.5 collective-permute-start
  848.1 10.2 collective-permute-done
  863.3 123.4 %while.40 = (s32[]{:T(128)}, f32[8,128,128]{1,2,0:T(8,128)S(1)}, bf16[16,8,32,128]{3,2,1,0:T(8,128)(2,1)}, f32[16,8,128,128]{2,3,1,0:T(8,128)}, f32[16,8,128,128...) while((s32[]{:T(128)}, f32[8,128,128]{1,2,0:T(8,128)S(1)}, ...), condition=%wide.region_8.9_spmd, body=%wide.region_7.8_spmd.sunk | while | flops 402982976 | bytes 6573429 | solution.py:169
  988.8 3.5 collective-permute-start.1
  997.1 19.8 %collective-permute-done.1 = bf16[512,1024]{1,0:T(8,128)(2,1)} collective-permute-done((bf16[512,1024]{1,0:T(8,128)(2,1)S(1)}, bf16[512,1024]{1,0:T(8,128)(2,1)}, u32[]{:S(2)}, u32[]{:S(2)}) %collective-permute-start.1) | collective-permute-done | bytes 1048608 | tf_op jit(solution)/shard_map/ppermute | solution.py:16
  1021.2 14.3 %collective-permute-done.2 = bf16[512,1024]{0,1:T(8,128)(2,1)} collective-permute-done((bf16[512,1024]{0,1:T(8,128)(2,1)}, bf16[512,1024]{0,1:T(8,128)(2,1)}, u32[]{:S(2)}, u32[]{:S(2)}) %collective-permute-start.2) | collective-permute-done | bytes 1048608 | tf_op jit(solution)/shard_map/ppermute | solution.py:16
  1037.2 8.1 fusion.48
  1045.3 17.9 %fusion.60 = (f32[8,512]{1,0:T(8,128)S(1)}, f32[8,512,1024]{1,2,0:T(8,128)}) fusion(f32[8,1024,512]{2,1,0:T(8,128)} %fusion.48, pred[512,1024]{0,1:T(8,128)(4,1)} %fusion.46), kind=kOutput, calls=%fused_computation.100 | output fusion | flops 25166848 | bytes 34095104 | tf_op jit(solution)/shard_map/sub | solution.py:111
  1063.2 8.0 fusion.47
  (316 shorter events, 210.0 us)
Async XLA Ops:
  0.6 1036.6 %copy-start = (bf16[512,1024]{1,0:T(8,128)(2,1)S(1)}, bf16[512,1024]{1,0:T(8,128)(2,1)}, u32[]{:S(2)}) copy-start(bf16[512,1024]{1,0:T(8,128)(2,1)} %param.18) | copy-start | bytes 3145732
  34.7 1.9 copy-start.1
  699.6 6.8 copy-start.3
  699.6 6.8 copy-start.2
  813.1 15.6 %collective-permute-start = (f32[8,128,128]{2,1,0:T(8,128)S(1)}, f32[8,128,128]{2,1,0:T(8,128)S(1)}, u32[]{:S(2)}, u32[]{:S(2)}) collective-permute-start(f32[8,128,128]{2,1,0:T(8,128)S(1)} %convolution_add_fusion.3), channel_id=1, source_target_pairs={{0,4},{4,8},{8,12},{1,5},{5,9},{9,13},{2,6},{6,10},{10,14},{3,7},{... | collective-permute-start | bytes 1572872 | tf_op jit(solution)/shard_map/while/body/eval_jaxpr/ppermute | solution.py:16
  829.3 14.7 %collective-permute-start = (f32[8,128,128]{2,1,0:T(8,128)S(1)}, f32[8,128,128]{2,1,0:T(8,128)S(1)}, u32[]{:S(2)}, u32[]{:S(2)}) collective-permute-start(f32[8,128,128]{2,1,0:T(8,128)S(1)} %convolution_add_fusion.3), channel_id=1, source_target_pairs={{0,4},{4,8},{8,12},{1,5},{5,9},{9,13},{2,6},{6,10},{10,14},{3,7},{... | collective-permute-start | bytes 1572872 | tf_op jit(solution)/shard_map/while/body/eval_jaxpr/ppermute | solution.py:16
  844.6 13.8 %collective-permute-start = (f32[8,128,128]{2,1,0:T(8,128)S(1)}, f32[8,128,128]{2,1,0:T(8,128)S(1)}, u32[]{:S(2)}, u32[]{:S(2)}) collective-permute-start(f32[8,128,128]{2,1,0:T(8,128)S(1)} %convolution_add_fusion.3), channel_id=1, source_target_pairs={{0,4},{4,8},{8,12},{1,5},{5,9},{9,13},{2,6},{6,10},{10,14},{3,7},{... | collective-permute-start | bytes 1572872 | tf_op jit(solution)/shard_map/while/body/eval_jaxpr/ppermute | solution.py:16
  986.7 5.6 copy-start.6
  988.8 8.3 copy-start.4
  988.8 28.1 %collective-permute-start.1 = (bf16[512,1024]{1,0:T(8,128)(2,1)S(1)}, bf16[512,1024]{1,0:T(8,128)(2,1)}, u32[]{:S(2)}, u32[]{:S(2)}) collective-permute-start(bf16[512,1024]{1,0:T(8,128)(2,1)S(1)} %bitcast.189), channel_id=1, source_target_pairs={{0,4},{4,8},{8,12},{1,5},{5,9},{9,13},{2,6},{6,10},{10,14},{3,7},{... | collective-permute-start | bytes 3145736 | tf_op jit(solution)/shard_map/ppermute | solution.py:16
  993.7 41.8 %collective-permute-start.2 = (bf16[512,1024]{0,1:T(8,128)(2,1)}, bf16[512,1024]{0,1:T(8,128)(2,1)}, u32[]{:S(2)}, u32[]{:S(2)}) collective-permute-start(bf16[512,1024]{0,1:T(8,128)(2,1)} %copy.98), channel_id=1, source_target_pairs={{0,4},{4,8},{8,12},{1,5},{5,9},{9,13},{2,6},{6,10},{10,14},{3,7},{... | collective-permute-start | bytes 3145736 | tf_op jit(solution)/shard_map/ppermute | solution.py:16
  1045.3 17.9 %copy-start.5 = (bf16[1024,1024]{0,1:T(8,128)(2,1)S(1)}, bf16[1024,1024]{0,1:T(8,128)(2,1)}, u32[]{:S(2)}) copy-start(bf16[1024,1024]{0,1:T(8,128)(2,1)} %copy.97) | copy-start | bytes 6291460
where the time goes:
time: 1090 us; the launch traced here: 1070 us
  other arithmetic  677 us (62%)
  matrix products  237 us (22%)
  local copies, waits for them, and re-layouts  73.2 us (7%)
  waiting for transfers between devices  67.5 us (6%)
  starting transfers between devices  15.9 us (1%)
    another operation x2, other arithmetic, span_factors(): jax.scipy.linalg.solve_triangular(mixing, sides, lower=True, unit_diagona...  631 us
    ppermute x5, waiting for transfers between devices, from_behind(): return lax.ppermute(array, axis, pairs)  67.5 us
    dot_general x16, matrix products, compose(): jnp.einsum('hab,hbc->hac', earlier[1], later[0], precision=highest)  29.6 us
    dot_general x16, matrix products, advance(): jnp.einsum('hab,hbc->hac', state, span_transition, precision=highest)  29.5 us
    dot_general x16, matrix products, compose(): joined = jnp.einsum('hab,hbc->hac', earlier[0], later[0], precision=highest)  27.4 us
    dot_general x16, matrix products, span_outputs(): fresh = written - jnp.dot(carried, state.T, precision=highest)  26 us
    dot_general x16, matrix products, span_outputs(): jnp.dot(query_rows, key_rows.T, precision=highest)  23.5 us
  transfers between devices with their start and end apart: 5, of which 5 were waited for; matrix products, arithmetic and copies ran while one was open for 1% of the time, Pallas kernels for 0%

commit v1 on v0

v1 whole, which is shorter than its diff:
```python
import functools
import math

import jax
import jax.numpy as jnp
from jax import lax
from jax.experimental import pallas as pl
from jax.experimental.pallas import tpu as pltpu
from jax.sharding import PartitionSpec as P

f32=jnp.float32; bf16=jnp.bfloat16
def dot(a,b): return lax.dot_general(a,b,(((1,),(0,)),((),())),preferred_element_type=f32)
def dot_nt(a,b): return lax.dot_general(a,b,(((1,),(1,)),((),())),preferred_element_type=f32)
def dot_tn(a,b): return lax.dot_general(a,b,(((0,),(0,)),((),())),preferred_element_type=f32)
def split(x):
    hi=x.astype(bf16); return hi,(x-hi.astype(f32)).astype(bf16)
def masks(C):
    i=lax.broadcasted_iota(jnp.int32,(C,C),0); j=lax.broadcasted_iota(jnp.int32,(C,C),1)
    ms=[((i//8)==(j//8)).astype(bf16)]
    s=8
    while s<C:
        ms.append((((i//(2*s))==(j//(2*s))) & ((i//s)!=(j//s))).astype(bf16)); s*=2
    eye=(i==j).astype(f32)
    return ms,eye
def inverse(A,ms,eye,mode):
    if mode=="f32":
        out=[]
        for a in A:
            out.append(jax.scipy.linalg.solve_triangular(a+eye,eye,lower=True,unit_diagonal=True))
        return out
    if mode.startswith("bf"):
        Ab=[a.astype(bf16) for a in A]
        A8=[a*ms[0] for a in Ab]
        P=[dot(a,a).astype(bf16) for a in A8]
        IA=[(eye.astype(bf16)-a) for a in A8]
        X1=[x.astype(f32)+dot(x,p) for x,p in zip(IA,P)]
        P2=[dot(p,p).astype(bf16) for p in P]
        X=[x+dot(x.astype(bf16),p) for x,p in zip(X1,P2)]
        for m in ms[1:]:
            Xb=[x.astype(bf16) for x in X]
            B=[dot(a*m,x).astype(bf16) for a,x in zip(Ab,Xb)]
            X=[x-dot(xb,b) for x,xb,b in zip(X,Xb,B)]
        nref=int(mode[2:])
        for r in range(nref):
            X0=[x.astype(bf16) for x in X]
            if r==0: As=[jnp.concatenate(split(a),axis=1) for a in A]
            if r==0 or True:
                E=[(eye-x.astype(f32))-dot(a,jnp.concatenate([x,x],axis=0)) for a,x in zip(As,X0)]
            X=[x.astype(f32)+dot(x,e.astype(bf16)) for x,e in zip(X0,E)]
        return X
def chunk(Y,k,q,v,Lr,Lc,br,bc,Lq,ms,eye,mode="bf1",opt=()):
    C=k[0].shape[0]; T=q[0].shape[0]; d=k[0].shape[1]; n=len(k)
    i=lax.broadcasted_iota(jnp.int32,(C+T,C),0); j=lax.broadcasted_iota(jnp.int32,(C+T,C),1)
    lim=jnp.where(i<C,i-1,2*(i-C)+1)
    mask=j<=lim
    H=range(n)
    G=[dot_nt(jnp.concatenate([k[h],q[h]],0),k[h]) for h in H]
    Gd=[G[h][:C]*eye for h in H]
    nr=[lax.rsqrt(jnp.sum(Gd[h],axis=0,keepdims=True)+1e-6) for h in H]
    nc=[lax.rsqrt(jnp.sum(Gd[h],axis=1,keepdims=True)+1e-6) for h in H]
    qn=[lax.rsqrt(jnp.sum(jnp.square(q[h].astype(f32)),axis=1,keepdims=True)+1e-6) for h in H]
    lev=[jnp.concatenate([Lc[h],Lq[h]],0) for h in H]
    rs=[jnp.concatenate([bc[h]*nc[h]*nc[h],qn[h]],0) for h in H]
    M=[jnp.where(mask,jnp.exp(jnp.minimum(lev[h]-Lr[h],0.0))*G[h]*rs[h],0.0) for h in H]
    A=[M[h][:C] for h in H]; wt=[M[h][C:].astype(bf16) for h in H]
    X=inverse(A,ms,eye,mode)
    bn=[br[h]*nr[h] for h in H]
    Xb=[jnp.concatenate(split(X[h]*bn[h]),1) for h in H]
    Xu=[jnp.concatenate(split(X[h]*(bn[h]*nr[h]*jnp.exp(Lr[h]))),1) for h in H]
    W=[dot(Xb[h],jnp.concatenate([v[h],v[h]],0)) for h in H]
    U=[dot(Xu[h],jnp.concatenate([k[h],k[h]],0)) for h in H]
    Us=[split(U[h]) for h in H]
    Ys=[split(Y[h]) for h in H]
    def dup(x): return jnp.concatenate([x,x],1)
    R1=[dot(dup(jnp.concatenate([Us[h][0],Us[h][1],q[h]],0)),jnp.concatenate(Ys[h],0)) for h in H]
    F=[jnp.concatenate([W[h],jnp.zeros_like(W[h])],1)-(R1[h][:C]+R1[h][C:2*C]) for h in H]
    last=[Lr[h][:,C-1:C] for h in H]
    kt=[split(jnp.transpose(k[h].astype(f32))*jnp.exp(last[h]-Lr[h])) for h in H]
    Fs=[split(F[h]) for h in H]
    ws=[split(M[h][C:]) for h in H]
    R2=[dot(dup(jnp.concatenate([kt[h][0],kt[h][1],ws[h][0],ws[h][1]],0)),jnp.concatenate(Fs[h],0)) for h in H]
    Yn=[Y[h]*jnp.exp(last[h])+(R2[h][:d]+R2[h][d:2*d]) for h in H]
    o=[(qn[h]*jnp.exp(Lq[h]))*R1[h][2*C:]+(R2[h][2*d:2*d+T]+R2[h][2*d+T:]) for h in H]
    return Yn,o


def k1_body(q_ref,k_ref,v_ref,s_ref,o_ref,qe_ref,yo_ref,y_ref,*,HB,mode):
    c=pl.program_id(1); C=k_ref.shape[0]; T=q_ref.shape[0]; d=128
    @pl.when(c==0)
    def _():
        i=lax.broadcasted_iota(jnp.int32,(d,2*d),0); j=lax.broadcasted_iota(jnp.int32,(d,2*d),1)
        y0=(j==i+d).astype(f32)
        for h in range(HB): y_ref[h]=y0
    ms,eye=masks(C)
    rows=s_ref[0]
    cols=jnp.transpose(rows)
    H=range(HB)
    sl=lambda r: [r[:,h*d:(h+1)*d] for h in H]
    P=rows.shape[0]//3
    Yn,o=chunk([y_ref[h] for h in H],sl(k_ref),sl(q_ref),sl(v_ref),
        [rows[h:h+1] for h in H],[cols[:,h:h+1] for h in H],
        [rows[P+h:P+h+1] for h in H],[cols[:,P+h:P+h+1] for h in H],
        [cols[:T,2*P+h:2*P+h+1] for h in H],ms,eye,mode)
    for h in H:
        y_ref[h]=Yn[h]
        o_ref[:,h*d:(h+1)*d]=o[h][:,:d]
        qe_ref[:,h*d:(h+1)*d]=o[h][:,d:].astype(bf16)
    @pl.when(c==pl.num_programs(1)-1)
    def _():
        for h in H: yo_ref[h]=Yn[h]
def small(betas,log_decay,HB,T=64):
    n,heads=log_decay.shape
    ch=n//T
    L=jnp.cumsum(log_decay.reshape(ch,T,heads),axis=1).transpose(0,2,1)
    L2=jnp.repeat(L,2,axis=2)
    b=betas.reshape(ch,2*T,heads).transpose(0,2,1)
    Lp=jnp.concatenate([L,jnp.zeros_like(L)],axis=2)
    P=max(HB,8)
    out=jnp.stack([L2,b,Lp],1)
    g=heads//HB
    out=out.reshape(ch,3,g,HB,2*T).transpose(2,0,1,3,4)
    if HB<8: out=jnp.concatenate([out,jnp.zeros((g,ch,3,8-HB,2*T),f32)],3)
    return out.reshape(g*ch,3*P,2*T)
def k1(queries,keys2,values2,sm,HB,mode="bf1",T=64):
    n=queries.shape[0]; heads=queries.shape[1]//128; ch=n//T; g=heads//HB; w=HB*128
    return pl.pallas_call(functools.partial(k1_body,HB=HB,mode=mode),
        grid=(g,ch),
        in_specs=[pl.BlockSpec((T,w),lambda i,c:(c,i)),pl.BlockSpec((2*T,w),lambda i,c:(c,i)),pl.BlockSpec((2*T,w),lambda i,c:(c,i)),
                  pl.BlockSpec((1,)+sm.shape[1:],lambda i,c:(i*ch+c,0,0))],
        out_specs=[pl.BlockSpec((T,w),lambda i,c:(c,i)),pl.BlockSpec((T,w),lambda i,c:(c,i)),pl.BlockSpec((HB,128,256),lambda i,c:(i,0,0))],
        out_shape=[jax.ShapeDtypeStruct((n,heads*128),f32),jax.ShapeDtypeStruct((n,heads*128),bf16),jax.ShapeDtypeStruct((heads,128,256),f32)],
        scratch_shapes=[pltpu.VMEM((HB,128,256),f32)],
        compiler_params=pltpu.CompilerParams(vmem_limit_bytes=50*2**20),
        name="local_chunks",
    )(queries,keys2,values2,sm)


def attend_body(q_ref, kp_ref, ko_ref, vp_ref, vo_ref, out_ref, *, HB, axis, R):
    n = q_ref.shape[0]
    d = 128
    bias = jnp.where(lax.axis_index(axis) > 0, 0.0, -1e30).astype(f32)
    scale = d ** -0.5 * math.log2(math.e)
    ones = jnp.ones((n, d), bf16)
    tri = lax.broadcasted_iota(jnp.int32, (R, R), 1) <= lax.broadcasted_iota(jnp.int32, (R, R), 0)
    for h in range(HB):
        s = slice(h * d, h * d + d)
        vp = jnp.concatenate([vp_ref[:, s], ones], 1)
        vo = jnp.concatenate([vo_ref[:, s], ones], 1)
        for i in range(n // R):
            q = q_ref[i * R:(i + 1) * R, s]
            sp = dot_nt(q, kp_ref[:, s]) + bias
            so = dot_nt(q, ko_ref[: (i + 1) * R, s])
            diag = jnp.where(tri, so[:, i * R:], -1e30)
            so = diag if i == 0 else jnp.concatenate([so[:, : i * R], diag], 1)
            m = jnp.maximum(jnp.max(sp, 1, keepdims=True), jnp.max(so, 1, keepdims=True))
            ep = jnp.exp2((sp - m) * scale).astype(bf16)
            eo = jnp.exp2((so - m) * scale).astype(bf16)
            r = dot(ep, vp) + dot(eo, vo[: (i + 1) * R])
            out_ref[i * R:(i + 1) * R, s] = (r[:, :d] / r[:, d:]).astype(bf16)

def attend(q, kp, ko, vp, vo, HB=1, R=256, axis="ctx"):
    n, w = q.shape
    spec = pl.BlockSpec((n, HB * 128), lambda h: (0, h))
    return pl.pallas_call(
        functools.partial(attend_body, HB=HB, axis=axis, R=R), grid=(w // (HB * 128),),
        in_specs=[spec] * 5, out_specs=spec, out_shape=jax.ShapeDtypeStruct((n, w), bf16),
        compiler_params=pltpu.CompilerParams(vmem_limit_bytes=50 * 2**20), name="attend")(q, kp, ko, vp, vo)

def finish_body(o_ref, qe_ref, z_ref, out_ref, *, HB):
    d = 128
    for h in range(HB):
        s = slice(h * d, h * d + d)
        out_ref[:, s] = (o_ref[:, s] + dot(qe_ref[:, s], z_ref[h])).astype(bf16)

def finish(o, qe, z, B=128):
    n, w = o.shape
    spec = pl.BlockSpec((B, w), lambda i: (i, 0))
    return pl.pallas_call(
        functools.partial(finish_body, HB=w // 128), grid=(n // B,),
        in_specs=[spec, spec, pl.BlockSpec(z.shape, lambda i: (0, 0, 0))], out_specs=spec,
        out_shape=jax.ShapeDtypeStruct((n, w), bf16), name="finish")(o, qe, z)

def hop_body(y_ref, z_ref, out_ref):
    d = 128
    for h in range(y_ref.shape[0]):
        y = y_ref[h]
        hi, lo = split(y[:, d:])
        z = z_ref[h]
        out_ref[h] = (y[:, :d] + dot(jnp.concatenate([hi, lo], 1), jnp.concatenate([z, z], 0))).astype(bf16)

def hop(y, z):
    return pl.pallas_call(hop_body, out_shape=jax.ShapeDtypeStruct(z.shape, bf16), name="hop")(y, z)


def from_behind(array, axis, by):
    n = lax.axis_size(axis)
    return lax.ppermute(array, axis, [(i, i + by) for i in range(n) if 0 <= i + by < n])
def per_device(queries, keys, values, betas, log_decay, attn_queries, attn_keys):
    n, w = queries.shape
    ak_prev = from_behind(attn_keys, "ctx", 1)
    HB = min(8, w // 128)
    sm = small(betas, log_decay, HB)
    o, qe, y = k1(queries, keys.reshape(2 * n, w), values.reshape(2 * n, w), sm, HB)
    z = y[:, :, :128].astype(bf16)
    z = from_behind(z, "ctx", 1)
    for _ in range(lax.axis_size("ctx") - 2):
        z = from_behind(hop(y, z), "ctx", 1)
    ret = finish(o, qe, z)
    rp = from_behind(ret, "ctx", 1)
    return ret, attend(attn_queries, ak_prev, attn_keys, rp, ret)


def solution(mesh):
    rows, cols = ("groups", "ctx"), ("head", "sub")
    flat, paired = P(rows, cols), P(rows, None, cols)
    return jax.shard_map(
        per_device,
        mesh=mesh,
        in_specs=(flat, paired, paired, paired, flat, flat, flat),
        out_specs=(flat, flat),
        check_vma=False,
    )
```

time: 1090 us -> 146 us (0.13); the launches traced: 1070 us -> 145 us
  other arithmetic: 677 us -> 6.34 us
  matrix products: 237 us -> 0 us
  local copies, waits for them, and re-layouts: 73.2 us -> 12.4 us
  Pallas kernels: 0 us -> 58.1 us
  waiting for transfers between devices: 67.5 us -> 51.5 us
    another operation x3 -> x2, other arithmetic: 634 us -> 6.34 us  [the longest x1 6.33 us: small(): L = jnp.cumsum(log_decay.reshape(ch, T, heads), axis=1).transpose(0, 2, 1)]
    dot_general x120 -> x0, matrix products: 225 us -> none  [the longest x16 29.6 us: compose(): jnp.einsum('hab,hbc->hac', earlier[1], later[0], precision=highest)]
    pallas_call x0 -> x5, Pallas kernels: none -> 58.1 us  [the longest x1 37.2 us: k1(): pl.pallas_call(functools.partial(k1_body, HB=HB, mode=mode), grid=(g, ch)...]
    convert_element_type x6 -> x0, local copies, waits for them, and re-layouts: 20.1 us -> none  [the longest x2 9.13 us: arrange(): value_heads = block_values.reshape(count, NREF, heads, width).transpose(2...]
    sub x18 -> x0, other arithmetic: 18 us -> none  [the longest x1 17.9 us: block_attention(): expanded = jnp.exp(attention_scores - largest)]
    ppermute x5, waiting for transfers between devices: 67.5 us -> 51.5 us  [from_behind(): lax.ppermute(array, axis, [(i, i + by) for i in range(n) if 0 <= i + by <...]
    dynamic_slice x16 -> x0, local copies, waits for them, and re-layouts: 14.7 us -> none  [per_device(): lax.scan(advance, incoming, (query_heads, key_heads, written, carried, le...]
    unnamed x19 -> x23, local copies, waits for them, and re-layouts: 17.5 us -> 4.36 us
  transfers between devices with their start and end apart: 5 -> 5, of which waited for: 5 -> 5; matrix products, arithmetic and copies ran while one was open for 1% -> 0% of each run, Pallas kernels for 0% -> 3%
where the time goes in v1:
time: 146 us; the launch traced here: 145 us
  Pallas kernels  58.1 us (40%)
  waiting for transfers between devices  51.5 us (35%)
  starting transfers between devices  16.2 us (11%)
  local copies, waits for them, and re-layouts  12.4 us (8%)
  other arithmetic  6.34 us (4%)
    ppermute x5, waiting for transfers between devices, from_behind(): lax.ppermute(array, axis, [(i, i + by) for i in range(n) if 0 <= i + by <...  51.5 us
    pallas_call x1, Pallas kernels, k1(): pl.pallas_call(functools.partial(k1_body, HB=HB, mode=mode), grid=(g, ch)...  37.2 us
    ppermute x5, starting transfers between devices, from_behind(): lax.ppermute(array, axis, [(i, i + by) for i in range(n) if 0 <= i + by <...  16.2 us
    pallas_call x1, Pallas kernels, attend(): pl.pallas_call(functools.partial(attend_body, HB=HB, axis=axis, R=R), gri...  12 us
    another operation x1, other arithmetic, small(): L = jnp.cumsum(log_decay.reshape(ch, T, heads), axis=1).transpose(0, 2, 1)  6.33 us
    pallas_call x2, Pallas kernels, hop(): pl.pallas_call(hop_body, out_shape=jax.ShapeDtypeStruct(z.shape, bf16), n...  4.53 us
    unnamed x23, local copies, waits for them, and re-layouts  4.36 us
    pallas_call x1, Pallas kernels, finish(): pl.pallas_call(functools.partial(finish_body, HB=w // 128), grid=(n // B,...  4.29 us
  transfers between devices with their start and end apart: 5, of which 5 were waited for; matrix products, arithmetic and copies ran while one was open for 0% of the time, Pallas kernels for 3%

profile of v1, /device:TPU:16, one launch (start us, length us, event | category | flops | bytes accessed | tf_op | source)
XLA Modules:
  0.0 145.2 jit_solution(5940812221262583956)
XLA Ops:
  0.6 0.0 copy-start.10
  0.6 0.8 reshape.18
  1.4 0.2 copy.20
  1.6 0.0 copy-start.5
  1.6 6.3 %reduce-window_bitcast_fusion = f32[8,8,64]{1,0,2:T(8,128)S(1)} fusion(f32[8,64,8]{2,0,1:T(8,128)S(1)} %copy.20), kind=kOutput, calls=%fused_computation | output fusion | flops 258048 | bytes 32768 | tf_op jit(solution)/shard_map/jit(cumsum)/reduce_window_sum | solution.py:114
  8.0 0.2 copy.22
  8.2 0.2 copy.24
  8.4 0.3 copy.21
  8.7 0.2 copy.23
  8.9 2.2 %reshape.16.k_ref = bf16[1024,1024]{1,0:T(8,128)(2,1)} reshape(bf16[512,2,1024]{2,1,0:T(2,128)(2,1)S(1)} %copy-done.5) | data formatting | bytes 4194304 | tf_op jit(solution)/shard_map/reshape | solution.py:203
  11.1 4.2 %reshape.17.v_ref = bf16[1024,1024]{1,0:T(8,128)(2,1)} reshape(bf16[512,2,1024]{2,1,0:T(2,128)(2,1)} %param.9) | data formatting | bytes 4194304 | tf_op jit(solution)/shard_map/reshape | solution.py:203
  15.3 37.2 %local_chunks.1 = (f32[512,1024]{1,0:T(8,128)}, bf16[512,1024]{1,0:T(8,128)(2,1)S(1)}, f32[8,128,256]{2,1,0:T(8,128)S(1)}) custom-call(bf16[512,1024]{1,0:T(8,128)(2,1)S(1)} %copy-done.2, bf16[1024,1024]{1,0:T(8,128)(2,1)} %reshape.16.k_ref, bf16[1024,1024]{1,0:T(8,128)(2,1)} %reshape.17.v_ref, f32[8,24,128]{2,1,0:T(8,128)S(1)} %maximum_bitcast_fusion.s_ref), custom_call_target="tpu_custom_call" | custom-call | tf_op jit(solution)/shard_map/local_chunks/pallas_call | solution.py:126
  52.5 1.0 copy-done.1
  53.5 3.6 %collective-permute-start = (bf16[8,128,128]{2,1,0:T(8,128)(2,1)S(1)}, bf16[8,128,128]{2,1,0:T(8,128)(2,1)S(1)}, u32[]{:S(2)}, u32[]{:S(2)}) collective-permute-start(bf16[8,128,128]{2,1,0:T(8,128)(2,1)S(1)} %slice.7), channel_id=1, source_target_pairs={{0,4},{4,8},{8,12},{1,5},{5,9},{9,13},{2,6},{6,10},{10,14},{3,7},{... | collective-permute-start | bytes 786440 | tf_op jit(solution)/shard_map/ppermute | solution.py:197
  57.1 6.4 %collective-permute-done.z_ref = bf16[8,128,128]{2,1,0:T(8,128)(2,1)S(1)} collective-permute-done((bf16[8,128,128]{2,1,0:T(8,128)(2,1)S(1)}, bf16[8,128,128]{2,1,0:T(8,128)(2,1)S(1)}, u32[]{:S(2)}, u32[]{:S(2)}) %collective-permute-start) | collective-permute-done | bytes 262176 | tf_op jit(solution)/shard_map/ppermute | solution.py:197
  63.6 0.0 copy-done
  63.6 0.7 copy-done.9
  64.3 2.3 %hop.2 = bf16[8,128,128]{2,1,0:T(8,128)(2,1)} custom-call(f32[8,128,256]{2,1,0:T(8,128)} %copy-done, bf16[8,128,128]{2,1,0:T(8,128)(2,1)} %copy-done.9), custom_call_target="tpu_custom_call" | custom-call | tf_op jit(solution)/shard_map/hop/pallas_call | solution.py:192
  66.6 3.5 %collective-permute-start.1 = (bf16[8,128,128]{2,1,0:T(8,128)(2,1)}, bf16[8,128,128]{2,1,0:T(8,128)(2,1)S(1)}, u32[]{:S(2)}, u32[]{:S(2)}) collective-permute-start(bf16[8,128,128]{2,1,0:T(8,128)(2,1)} %hop.2), channel_id=1, source_target_pairs={{0,4},{4,8},{8,12},{1,5},{5,9},{9,13},{2,6},{6,10},{10,14},{3,7},{... | collective-permute-start | bytes 786440 | tf_op jit(solution)/shard_map/ppermute | solution.py:197
  70.1 5.8 %collective-permute-done.1.z_ref = bf16[8,128,128]{2,1,0:T(8,128)(2,1)S(1)} collective-permute-done((bf16[8,128,128]{2,1,0:T(8,128)(2,1)}, bf16[8,128,128]{2,1,0:T(8,128)(2,1)S(1)}, u32[]{:S(2)}, u32[]{:S(2)}) %collective-permute-start.1) | collective-permute-done | bytes 262176 | tf_op jit(solution)/shard_map/ppermute | solution.py:197
  75.8 0.7 copy-done.8
  76.5 2.3 %hop.3 = bf16[8,128,128]{2,1,0:T(8,128)(2,1)} custom-call(f32[8,128,256]{2,1,0:T(8,128)} %copy-done, bf16[8,128,128]{2,1,0:T(8,128)(2,1)} %copy-done.8), custom_call_target="tpu_custom_call" | custom-call | tf_op jit(solution)/shard_map/hop/pallas_call | solution.py:192
  78.8 3.5 %collective-permute-start.2 = (bf16[8,128,128]{2,1,0:T(8,128)(2,1)}, bf16[8,128,128]{2,1,0:T(8,128)(2,1)S(1)}, u32[]{:S(2)}, u32[]{:S(2)}) collective-permute-start(bf16[8,128,128]{2,1,0:T(8,128)(2,1)} %hop.3), channel_id=1, source_target_pairs={{0,4},{4,8},{8,12},{1,5},{5,9},{9,13},{2,6},{6,10},{10,14},{3,7},{... | collective-permute-start | bytes 786440 | tf_op jit(solution)/shard_map/ppermute | solution.py:197
  82.3 1.9 %collective-permute-start.3 = (bf16[512,1024]{1,0:T(8,128)(2,1)S(1)}, bf16[512,1024]{1,0:T(8,128)(2,1)S(1)}, u32[]{:S(2)}, u32[]{:S(2)}) collective-permute-start(bf16[512,1024]{1,0:T(8,128)(2,1)S(1)} %copy-done.4), channel_id=1, source_target_pairs={{0,4},{4,8},{8,12},{1,5},{5,9},{9,13},{2,6},{6,10},{10,14},{3,7},{... | collective-permute-start | bytes 3145736 | tf_op jit(solution)/shard_map/ppermute | solution.py:197
  84.2 5.7 %collective-permute-done.2.z_ref = bf16[8,128,128]{2,1,0:T(8,128)(2,1)S(1)} collective-permute-done((bf16[8,128,128]{2,1,0:T(8,128)(2,1)}, bf16[8,128,128]{2,1,0:T(8,128)(2,1)S(1)}, u32[]{:S(2)}, u32[]{:S(2)}) %collective-permute-start.2) | collective-permute-done | bytes 262176 | tf_op jit(solution)/shard_map/ppermute | solution.py:197
  90.0 0.7 copy-done.7
  90.7 4.3 %finish.1.vo_ref = bf16[512,1024]{1,0:T(8,128)(2,1)} custom-call(f32[512,1024]{1,0:T(8,128)} %get-tuple-element.5.o_ref, bf16[512,1024]{1,0:T(8,128)(2,1)} %copy-done.1, bf16[8,128,128]{2,1,0:T(8,128)(2,1)} %copy-done.7), custom_call_target="tpu_custom_call" | custom-call | tf_op jit(solution)/shard_map/finish/pallas_call | solution.py:178
  95.0 3.7 %collective-permute-start.4 = (bf16[512,1024]{1,0:T(8,128)(2,1)}, bf16[512,1024]{1,0:T(8,128)(2,1)S(1)}, u32[]{:S(2)}, u32[]{:S(2)}) collective-permute-start(bf16[512,1024]{1,0:T(8,128)(2,1)} %finish.1.vo_ref), channel_id=1, source_target_pairs={{0,4},{4,8},{8,12},{1,5},{5,9},{9,13},{2,6},{6,10},{10,14},{3,7},{... | collective-permute-start | bytes 3145736 | tf_op jit(solution)/shard_map/ppermute | solution.py:197
  98.6 13.8 %collective-permute-done.3.kp_ref = bf16[512,1024]{1,0:T(8,128)(2,1)S(1)} collective-permute-done((bf16[512,1024]{1,0:T(8,128)(2,1)S(1)}, bf16[512,1024]{1,0:T(8,128)(2,1)S(1)}, u32[]{:S(2)}, u32[]{:S(2)}) %collective-permute-start.3) | collective-permute-done | bytes 1048608 | tf_op jit(solution)/shard_map/ppermute | solution.py:197
  112.4 19.8 %collective-permute-done.4.vp_ref = bf16[512,1024]{1,0:T(8,128)(2,1)S(1)} collective-permute-done((bf16[512,1024]{1,0:T(8,128)(2,1)}, bf16[512,1024]{1,0:T(8,128)(2,1)S(1)}, u32[]{:S(2)}, u32[]{:S(2)}) %collective-permute-start.4) | collective-permute-done | bytes 1048608 | tf_op jit(solution)/shard_map/ppermute | solution.py:197
  132.2 1.0 copy-done.6
  133.2 12.0 %attend.1 = bf16[512,1024]{1,0:T(8,128)(2,1)} custom-call(bf16[512,1024]{1,0:T(8,128)(2,1)S(1)} %copy-done.3, bf16[512,1024]{1,0:T(8,128)(2,1)S(1)} %collective-permute-done.3.kp_ref, bf16[512,1024]{1,0:T(8,128)(2,1)S(1)} %copy-done.4, bf16[512,1024]{1,0:T(8,128)(2,1)} %copy-done.6, bf16[512,1024]{1,0:T(8,128)(2,1)} %finish.1.vo_ref), custom_call_target="tpu_custom_call" | custom-call | tf_op jit(solution)/shard_map/attend/pallas_call | solution.py:164
  (18 shorter events, 0.1 us)
Async XLA Ops:
  0.6 7.8 %copy-start.10 = (f32[512,2,8]{0,2,1:T(8,128)S(1)}, f32[512,2,8]{0,2,1:T(8,128)}, u32[]{:S(2)}) copy-start(f32[512,2,8]{0,2,1:T(8,128)} %param.10) | copy-start | bytes 98308
  1.6 7.3 %copy-start.5 = (bf16[512,2,1024]{2,1,0:T(2,128)(2,1)S(1)}, bf16[512,2,1024]{2,1,0:T(2,128)(2,1)}, u32[]{:S(2)}) copy-start(bf16[512,2,1024]{2,1,0:T(2,128)(2,1)} %param.8) | copy-start | bytes 6291460
  11.1 4.2 %copy-start.2 = (bf16[512,1024]{1,0:T(8,128)(2,1)S(1)}, bf16[512,1024]{1,0:T(8,128)(2,1)}, u32[]{:S(2)}) copy-start(bf16[512,1024]{1,0:T(8,128)(2,1)} %q_ref.2) | copy-start | bytes 3145732
  52.5 1.0 copy-start.1
  53.5 10.1 %copy-start = (f32[8,128,256]{2,1,0:T(8,128)}, f32[8,128,256]{2,1,0:T(8,128)S(1)}, u32[]{:S(2)}) copy-start(f32[8,128,256]{2,1,0:T(8,128)S(1)} %get-tuple-element.7.y_ref) | copy-start | bytes 3145732
  53.5 28.8 %copy-start.4 = (bf16[512,1024]{1,0:T(8,128)(2,1)S(1)}, bf16[512,1024]{1,0:T(8,128)(2,1)}, u32[]{:S(2)}) copy-start(bf16[512,1024]{1,0:T(8,128)(2,1)} %ko_ref.1) | copy-start | bytes 3145732
  53.5 10.1 %collective-permute-start = (bf16[8,128,128]{2,1,0:T(8,128)(2,1)S(1)}, bf16[8,128,128]{2,1,0:T(8,128)(2,1)S(1)}, u32[]{:S(2)}, u32[]{:S(2)}) collective-permute-start(bf16[8,128,128]{2,1,0:T(8,128)(2,1)S(1)} %slice.7), channel_id=1, source_target_pairs={{0,4},{4,8},{8,12},{1,5},{5,9},{9,13},{2,6},{6,10},{10,14},{3,7},{... | collective-permute-start | bytes 786440 | tf_op jit(solution)/shard_map/ppermute | solution.py:197
  63.6 0.7 copy-start.9
  66.6 9.3 %collective-permute-start.1 = (bf16[8,128,128]{2,1,0:T(8,128)(2,1)}, bf16[8,128,128]{2,1,0:T(8,128)(2,1)S(1)}, u32[]{:S(2)}, u32[]{:S(2)}) collective-permute-start(bf16[8,128,128]{2,1,0:T(8,128)(2,1)} %hop.2), channel_id=1, source_target_pairs={{0,4},{4,8},{8,12},{1,5},{5,9},{9,13},{2,6},{6,10},{10,14},{3,7},{... | collective-permute-start | bytes 786440 | tf_op jit(solution)/shard_map/ppermute | solution.py:197
  75.8 0.7 copy-start.8
  78.8 11.2 %collective-permute-start.2 = (bf16[8,128,128]{2,1,0:T(8,128)(2,1)}, bf16[8,128,128]{2,1,0:T(8,128)(2,1)S(1)}, u32[]{:S(2)}, u32[]{:S(2)}) collective-permute-start(bf16[8,128,128]{2,1,0:T(8,128)(2,1)} %hop.3), channel_id=1, source_target_pairs={{0,4},{4,8},{8,12},{1,5},{5,9},{9,13},{2,6},{6,10},{10,14},{3,7},{... | collective-permute-start | bytes 786440 | tf_op jit(solution)/shard_map/ppermute | solution.py:197
  82.3 30.1 %collective-permute-start.3 = (bf16[512,1024]{1,0:T(8,128)(2,1)S(1)}, bf16[512,1024]{1,0:T(8,128)(2,1)S(1)}, u32[]{:S(2)}, u32[]{:S(2)}) collective-permute-start(bf16[512,1024]{1,0:T(8,128)(2,1)S(1)} %copy-done.4), channel_id=1, source_target_pairs={{0,4},{4,8},{8,12},{1,5},{5,9},{9,13},{2,6},{6,10},{10,14},{3,7},{... | collective-permute-start | bytes 3145736 | tf_op jit(solution)/shard_map/ppermute | solution.py:197
  90.0 0.7 copy-start.7
  90.7 42.5 %copy-start.3 = (bf16[512,1024]{1,0:T(8,128)(2,1)S(1)}, bf16[512,1024]{1,0:T(8,128)(2,1)}, u32[]{:S(2)}) copy-start(bf16[512,1024]{1,0:T(8,128)(2,1)} %q_ref.3) | copy-start | bytes 3145732
  95.0 37.2 %collective-permute-start.4 = (bf16[512,1024]{1,0:T(8,128)(2,1)}, bf16[512,1024]{1,0:T(8,128)(2,1)S(1)}, u32[]{:S(2)}, u32[]{:S(2)}) collective-permute-start(bf16[512,1024]{1,0:T(8,128)(2,1)} %finish.1.vo_ref), channel_id=1, source_target_pairs={{0,4},{4,8},{8,12},{1,5},{5,9},{9,13},{2,6},{6,10},{10,14},{3,7},{... | collective-permute-start | bytes 3145736 | tf_op jit(solution)/shard_map/ppermute | solution.py:197
  132.2 1.0 copy-start.6

commit v2 on v0

v2 whole, which is shorter than its diff:
```python
import functools
import math

import jax
import jax.numpy as jnp
from jax import lax
from jax.experimental import pallas as pl
from jax.experimental.pallas import tpu as pltpu
from jax.sharding import PartitionSpec as P

f32 = jnp.float32
bf16 = jnp.bfloat16


def dot(a, b):
    return lax.dot_general(a, b, (((1,), (0,)), ((), ())), preferred_element_type=f32)


def dot_nt(a, b):
    return lax.dot_general(a, b, (((1,), (1,)), ((), ())), preferred_element_type=f32)


def cat(parts, axis):
    return jnp.concatenate(parts, axis)


def split(x):
    hi = x.astype(bf16)
    return hi, (x - hi.astype(f32)).astype(bf16)


def product(a, b):
    n = b[0].shape[1]
    row = cat(b, 1)
    r = dot(cat(a, 1), cat([row, row], 0))
    return r[:, :n] + r[:, n:]


def odd(x, s):
    return cat([x[b * s:(b + 1) * s] for b in range(1, x.shape[0] // s, 2)], 0)


def weave(even, o, s):
    out = []
    for b in range(o.shape[0] // s):
        out.append(jnp.zeros((s, o.shape[1]), o.dtype) if even is None else even[2 * b * s:(2 * b + 1) * s])
        out.append(o[b * s:(b + 1) * s])
    return cat(out, 0)


def block_masks(C):
    i = lax.broadcasted_iota(jnp.int32, (C, C), 0)
    j = lax.broadcasted_iota(jnp.int32, (C, C), 1)
    masks = {0: ((i // 4) == (j // 4)).astype(bf16)}
    s = 4
    while s < C:
        masks[s] = (((i // (2 * s)) == (j // (2 * s))) & ((i // s) != (j // s))).astype(bf16)
        s *= 2
    return masks, (i == j).astype(f32)


def inverses(A, masks, eye):
    C = eye.shape[0]
    eb = eye.astype(bf16)
    As = [split(a) for a in A]
    small = [(a[0] * masks[0], a[1] * masks[0]) for a in As]
    square = [split(product(a, a)) for a in small]
    start = [(eb - a[0], -a[1]) for a in small]
    X = [t[0].astype(f32) + t[1].astype(f32) + product(t, p) for t, p in zip(start, square)]
    Xs = [split(x) for x in X]
    s = 4
    while s < C:
        if s < 16:
            m = masks[s]
            B = [split(product((a[0] * m, a[1] * m), x)) for a, x in zip(As, Xs)]
            X = [x - product(xs, b) for x, xs, b in zip(X, Xs, B)]
            Xs = [split(x) for x in X]
        else:
            m = odd(masks[s], s)
            B = [split(product((odd(a[0], s) * m, odd(a[1], s) * m), x)) for a, x in zip(As, Xs)]
            B = [(weave(None, b[0], s), weave(None, b[1], s)) for b in B]
            Xo = [odd(x, s) - product((odd(xs[0], s), odd(xs[1], s)), b) for x, xs, b in zip(X, Xs, B)]
            X = [weave(x, o, s) for x, o in zip(X, Xo)]
            if 2 * s < C:
                So = [split(o) for o in Xo]
                Xs = [(weave(x[0], o[0], s), weave(x[1], o[1], s)) for x, o in zip(Xs, So)]
        s *= 2
    return X


def two(parts):
    x = cat(parts, 0)
    return cat([x, x], 1)


def factors(kq, k, q, v, Lr, Lc, br, bc, Lq, masks, eye):
    C, d = k[0].shape
    T = q[0].shape[0]
    H = range(len(k))
    i = lax.broadcasted_iota(jnp.int32, (C + T, C), 0)
    j = lax.broadcasted_iota(jnp.int32, (C + T, C), 1)
    visible = j <= jnp.where(i < C, i - 1, 2 * (i - C) + 1)
    nil = jnp.zeros((C, d), bf16)
    G = []
    for p, both in enumerate(kq):
        a, b = k[2 * p], k[2 * p + 1]
        r = dot_nt(both, cat([cat([a, nil], 1), cat([nil, b], 1)], 0))
        G += [r[:, :C], r[:, C:]]
    Gd = [G[h][:C] * eye for h in H]
    nr = [lax.rsqrt(jnp.sum(Gd[h], axis=0, keepdims=True) + 1e-6) for h in H]
    nc = [lax.rsqrt(jnp.sum(Gd[h], axis=1, keepdims=True) + 1e-6) for h in H]
    qn = [lax.rsqrt(jnp.sum(jnp.square(q[h].astype(f32)), axis=1, keepdims=True) + 1e-6) for h in H]
    lev = [cat([Lc[h], Lq[h]], 0) for h in H]
    rs = [cat([bc[h] * nc[h] * nc[h], qn[h]], 0) for h in H]
    M = [jnp.where(visible, jnp.exp(jnp.minimum(lev[h] - Lr[h], 0.0)) * G[h] * rs[h], 0.0) for h in H]
    X = inverses([M[h][:C] for h in H], masks, eye)
    bn = [br[h] * nr[h] for h in H]
    W = [dot(cat(split(X[h] * bn[h]), 1), cat([v[h], v[h]], 0)) for h in H]
    U = [dot(cat(split(X[h] * (bn[h] * nr[h] * jnp.exp(Lr[h]))), 1), cat([k[h], k[h]], 0)) for h in H]
    last = [Lr[h][:, C - 1:C] for h in H]
    kt = [split(jnp.transpose(k[h].astype(f32)) * jnp.exp(last[h] - Lr[h])) for h in H]
    ws = [split(M[h][C:]) for h in H]
    right = [split(cat([U[h], W[h]], 1)) for h in H]
    R = [dot(two([kt[h][0], ws[h][0], kt[h][1], ws[h][1]]), cat(right[h], 0)) for h in H]
    R = [r[:d + T] + r[d + T:] for r in R]
    left = [split(cat([R[h][:d, :d], (qn[h] * jnp.exp(Lq[h])) * q[h].astype(f32) - R[h][d:, :d]], 0)) for h in H]
    return left, [R[h][:, d:] for h in H], [jnp.exp(last[h]) for h in H]


def advance(Y, left, add, decay):
    H = range(len(Y))
    d = Y[0].shape[0]
    n = left[0][0].shape[0]
    R = [dot(two(left[h]), cat(split(Y[h]), 0)) for h in H]
    R = [r[:n] + r[n:] for r in R]
    nil = jnp.zeros_like(add[0])
    own = [cat([a, nil], 1) for a in add]
    return [Y[h] * decay[h] + own[h][:d] - R[h][:d] for h in H], [own[h][d:] + R[h][d:] for h in H]


D = 128


def params(mib):
    return pltpu.CompilerParams(vmem_limit_bytes=mib * 2**20)


def cost(us):
    return pl.CostEstimate(flops=int(us * 10**9), bytes_accessed=10**6, transcendentals=0)


def local_body(q_ref, k_ref, v_ref, b_ref, l_ref, o_ref, qe_ref, yo_ref, a_ref, y_ref, r_ref, *, HB, NC, first):
    c = pl.program_id(0)
    T = q_ref.shape[0] // NC
    C = 2 * T
    d = D
    H = range(HB)
    heads = l_ref.shape[0]

    @pl.when(c == 0)
    def _():
        i = lax.broadcasted_iota(jnp.int32, (d, 2 * d), 0)
        j = lax.broadcasted_iota(jnp.int32, (d, 2 * d), 1)
        for h in H:
            y_ref[h] = (j == i + d).astype(f32)

        def pick(x, m):
            a = x.astype(bf16)
            r = dot(cat([a, *split(x - a.astype(f32))], 0), m.astype(bf16))
            return r[:heads] + r[heads:2 * heads] + r[2 * heads:]

        def full(x):
            return x if heads == 8 else cat([x, jnp.zeros((8 - heads, C), f32)], 0)

        ld, b0, b1 = l_ref[...], b_ref[0], b_ref[1]
        t = lax.broadcasted_iota(jnp.int32, (l_ref.shape[1], C), 0)
        i = lax.broadcasted_iota(jnp.int32, (l_ref.shape[1], C), 1)
        for s in range(r_ref.shape[0]):
            u = t - s * T
            r_ref[s, 0:8] = full(pick(ld, (u >= 0) & (u <= i // 2)))
            r_ref[s, 8:16] = full(pick(b0, 2 * u == i) + pick(b1, 2 * u + 1 == i))
            r_ref[s, 16:24] = full(pick(ld, (u >= 0) & (u <= i)))

    masks, eye = block_masks(C)
    kq, k, q, v, Lr, Lc, br, bc, Lq = ([] for _ in range(9))
    for s in range(NC):
        rows = r_ref[c * NC + s]
        cols = jnp.transpose(cat([rows, jnp.zeros((C - 24, C), f32)], 0))
        ks = k_ref[s * T:(s + 1) * T].reshape(C, HB * d)
        vs = v_ref[s * T:(s + 1) * T].reshape(C, HB * d)
        qs = q_ref[s * T:(s + 1) * T]
        both = cat([ks, qs], 0)
        kq += [both[:, p * d:(p + 2) * d] for p in range(0, HB, 2)]
        for h in H:
            at = first + h
            k.append(ks[:, h * d:(h + 1) * d])
            v.append(vs[:, h * d:(h + 1) * d])
            q.append(qs[:, h * d:(h + 1) * d])
            Lr.append(rows[at:at + 1])
            br.append(rows[8 + at:9 + at])
            Lc.append(cols[:, at:at + 1])
            bc.append(cols[:, 8 + at:9 + at])
            Lq.append(cols[:T, 16 + at:17 + at])
    left, add, decay = factors(kq, k, q, v, Lr, Lc, br, bc, Lq, masks, eye)
    Y = [y_ref[h] for h in H]
    for s in range(NC):
        now = slice(s * HB, (s + 1) * HB)
        Y, o = advance(Y, left[now], add[now], decay[now])
        for h in H:
            o_ref[s * T:(s + 1) * T, h * d:(h + 1) * d] = o[h][:, :d]
            qe_ref[s * T:(s + 1) * T, h * d:(h + 1) * d] = o[h][:, d:].astype(bf16)
    for h in H:
        y_ref[h] = Y[h]

    @pl.when(c == pl.num_programs(0) - 1)
    def _():
        for h in H:
            yo_ref[h] = Y[h]
            a_ref[h] = Y[h][:, :d].astype(bf16)


def local(queries, keys, values, betas, decay, g, HB, NC, T=64):
    n, w = queries.shape
    heads = w // D
    wg = HB * D
    B = NC * T
    flat = pl.BlockSpec((B, wg), lambda c: (c, g))
    pair = pl.BlockSpec((B, 2, wg), lambda c: (c, 0, g))
    out = pl.BlockSpec((B, wg), lambda c: (c, 0))
    whole = lambda *s: pl.BlockSpec(s, lambda c: (0,) * len(s))
    return pl.pallas_call(
        functools.partial(local_body, HB=HB, NC=NC, first=g * HB),
        grid=(n // B,),
        in_specs=[flat, pair, pair, whole(2, heads, n), whole(heads, n)],
        out_specs=[out, out, whole(HB, D, 2 * D), whole(HB, D, D)],
        out_shape=[jax.ShapeDtypeStruct((n, wg), f32), jax.ShapeDtypeStruct((n, wg), bf16), jax.ShapeDtypeStruct((HB, D, 2 * D), f32), jax.ShapeDtypeStruct((HB, D, D), bf16)],
        scratch_shapes=[pltpu.VMEM((HB, D, 2 * D), f32), pltpu.VMEM((n // T, 24, 2 * T), f32)],
        cost_estimate=cost(HB * 5), name="local", compiler_params=params(52),
    )(queries, keys, values, betas, decay)


VMEM = pl.BlockSpec(memory_space=pltpu.VMEM)


def hop_body(y_ref, z_ref, out_ref):
    for h in range(y_ref.shape[0]):
        hi, lo = split(y_ref[h, :, D:])
        z = z_ref[h]
        out_ref[h] = (y_ref[h, :, :D] + dot(cat([hi, lo], 1), cat([z, z], 0))).astype(bf16)


def hop(y, z):
    return pl.pallas_call(
        hop_body, in_specs=[VMEM, VMEM], out_specs=VMEM, out_shape=jax.ShapeDtypeStruct(z.shape, bf16),
        cost_estimate=cost(1), name="hop", compiler_params=params(8))(y, z)


def finish_body(o_ref, qe_ref, z_ref, out_ref):
    for h in range(z_ref.shape[0]):
        s = slice(h * D, h * D + D)
        out_ref[:, s] = (o_ref[:, s] + dot(qe_ref[:, s], z_ref[h])).astype(bf16)


def finish(o, qe, z, B=256):
    n, w = o.shape
    spec = pl.BlockSpec((B, w), lambda i: (i, 0))
    return pl.pallas_call(
        finish_body, grid=(n // B,), in_specs=[spec, spec, VMEM], out_specs=spec,
        out_shape=jax.ShapeDtypeStruct((n, w), bf16), cost_estimate=cost(2), name="finish", compiler_params=params(8))(o, qe, z)


def attend_body(q_ref, kp_ref, ko_ref, vp_ref, o_ref, qe_ref, z_ref, *refs, axis, R, first):
    ret_ref, out_ref = refs[-2:]
    n = q_ref.shape[0]
    h = pl.program_id(0)
    bias = jnp.where(lax.axis_index(axis) > 0, 0.0, -1e30).astype(f32)
    scale = D ** -0.5 * math.log2(math.e)
    ones = jnp.ones((n, D), bf16)
    tri = lax.broadcasted_iota(jnp.int32, (R, R), 1) <= lax.broadcasted_iota(jnp.int32, (R, R), 0)
    ret = (o_ref[...] + dot(qe_ref[...], z_ref[h])).astype(bf16)
    ret_ref[...] = ret
    kp = kp_ref[:, pl.ds(pl.multiple_of(h * D, D), D)]
    vp = cat([vp_ref[:, pl.ds(pl.multiple_of(h * D, D), D)], ones], 1)
    vo = cat([ret, ones], 1)
    for i in range(n // R):
        q = q_ref[i * R:(i + 1) * R]
        sp = dot_nt(q, kp) + bias
        so = dot_nt(q, ko_ref[:(i + 1) * R])
        diag = jnp.where(tri, so[:, i * R:], -1e30)
        so = diag if i == 0 else cat([so[:, :i * R], diag], 1)
        m = jnp.maximum(jnp.max(sp, 1, keepdims=True), jnp.max(so, 1, keepdims=True))
        ep = jnp.exp2((sp - m) * scale).astype(bf16)
        eo = jnp.exp2((so - m) * scale).astype(bf16)
        r = dot(ep, vp) + dot(eo, vo[:(i + 1) * R])
        out_ref[i * R:(i + 1) * R] = (r[:, :D] / r[:, D:]).astype(bf16)


def attend(q, kp, ko, vp, o, qe, z, carry, g, HB, R=256, axis="ctx"):
    n, w = q.shape
    flat = pl.BlockSpec((n, D), lambda h: (0, g * HB + h))
    part = pl.BlockSpec((n, D), lambda h: (0, h))
    held = [pl.BlockSpec(memory_space=pl.ANY)] * len(carry)
    return pl.pallas_call(
        functools.partial(attend_body, axis=axis, R=R, first=g * HB), grid=(HB,),
        in_specs=[flat, VMEM, flat, VMEM, part, part, VMEM] + held, out_specs=[flat, flat],
        out_shape=[jax.ShapeDtypeStruct((n, w), bf16)] * 2,
        input_output_aliases={7 + i: i for i in range(len(carry))},
        cost_estimate=cost(HB * 1.3), name="attend", compiler_params=params(24))(q, kp, ko, vp, o, qe, z, *carry)


def from_behind(array, axis):
    n = lax.axis_size(axis)
    return lax.ppermute(array, axis, [(i, i + 1) for i in range(n - 1)])


GROUPS = 2


def per_device(queries, keys, values, betas, log_decay, attn_queries, attn_keys):
    n, w = queries.shape
    HB = w // D // GROUPS
    hops = lax.axis_size("ctx") - 1
    G = range(GROUPS)
    beta_rows = betas.transpose(1, 2, 0)
    decay_rows = log_decay.transpose(1, 0)
    keys_behind = []
    parts = []
    for g in G:
        if g:
            decay_rows, keys_behind[-1] = lax.optimization_barrier((decay_rows, keys_behind[-1]))
        keys_behind.append(from_behind(attn_keys[:, g * HB * D:(g + 1) * HB * D], "ctx"))
        parts.append(local(queries, keys, values, beta_rows, decay_rows, g, HB, math.gcd(16 // HB, n // 64)))
    z = [jnp.zeros_like(p[3]) for p in parts]
    behind = [None] * GROUPS
    for k in range(hops):
        for g in G:
            o, qe, y, a = parts[g]
            if k == 1 and g < GROUPS - 1:
                z[g], parts[-1], keys_behind[-1] = lax.optimization_barrier((z[g], parts[-1], keys_behind[-1]))
                o, qe, y, a = parts[g]
            sent = a if k == 0 else hop(y, z[g])
            if k == hops - 1:
                ret = finish(o, qe, z[g])
            z[g] = from_behind(sent, "ctx")
            if k == hops - 1:
                behind[g] = from_behind(ret, "ctx")
    carry = ()
    for g in G:
        o, qe, y, a = parts[g]
        carry = attend(attn_queries, keys_behind[g], attn_keys, behind[g], o, qe, z[g], carry, g, HB)
    return tuple(carry)


def solution(mesh):
    rows, cols = ("groups", "ctx"), ("head", "sub")
    flat, paired = P(rows, cols), P(rows, None, cols)
    return jax.shard_map(
        per_device,
        mesh=mesh,
        in_specs=(flat, paired, paired, paired, flat, flat, flat),
        out_specs=(flat, flat),
        check_vma=False,
    )
```

time: 1090 us -> 99.4 us (0.09)
  the two profiles are of different devices: /device:TPU:16 before, /device:TPU:0 now
where the time goes in v2:
time: 99.4 us; the launch traced here: 98.9 us
  Pallas kernels  53.8 us (54%)
  starting transfers between devices  31.8 us (32%)
  waiting for transfers between devices  11.1 us (11%)
  local copies, waits for them, and re-layouts  1.31 us (1%)
    pallas_call x2, Pallas kernels, local(): pl.pallas_call(functools.partial(local_body, HB=HB, NC=NC, first=g * HB),...  40.2 us
    ppermute x10, starting transfers between devices, from_behind(): return lax.ppermute(array, axis, [(i, i + 1) for i in range(n - 1)])  31.8 us
    pallas_call x2, Pallas kernels, attend(): pl.pallas_call(functools.partial(attend_body, axis=axis, R=R, first=g * H...  11.9 us
    ppermute x10, waiting for transfers between devices, from_behind(): return lax.ppermute(array, axis, [(i, i + 1) for i in range(n - 1)])  11.1 us
  transfers between devices with their start and end apart: 10, of which 3 were waited for; matrix products, arithmetic and copies ran while one was open for 0% of the time, Pallas kernels for 48%

profile of v2, /device:TPU:0, one launch (start us, length us, event | category | flops | bytes accessed | tf_op | source)
XLA Modules:
  0.0 98.9 jit_solution(12160034061841551365)
XLA Ops:
  0.6 1.3 %fusion = (bf16[512,512]{1,0:T(8,128)(2,1)S(1)}, bf16[512,512]{1,0:T(8,128)(2,1)S(1)}) fusion(bf16[512,1024]{1,0:T(8,128)(2,1)} %ko_ref.3), kind=kLoop, calls=%fused_computation | loop fusion | bytes 2097152 | tf_op jit(solution)/shard_map/slice | solution.py:331
  1.9 5.0 %collective-permute-start.2 = (bf16[512,512]{1,0:T(8,128)(2,1)S(1)}, bf16[512,512]{1,0:T(8,128)(2,1)S(1)}, u32[]{:S(2)}, u32[]{:S(2)}) collective-permute-start(bf16[512,512]{1,0:T(8,128)(2,1)S(1)} %get-tuple-element.36), channel_id=1, source_target_pairs={{0,4},{4,8},{8,12},{1,5},{5,9},{9,13},{2,6},{6,10},{10,14},{3,7},{... | collective-permute-start | bytes 1572872 | tf_op jit(solution)/shard_map/ppermute | solution.py:313
  6.9 3.5 %collective-permute-start.1 = (bf16[512,512]{1,0:T(8,128)(2,1)S(1)}, bf16[512,512]{1,0:T(8,128)(2,1)S(1)}, u32[]{:S(2)}, u32[]{:S(2)}) collective-permute-start(bf16[512,512]{1,0:T(8,128)(2,1)S(1)} %get-tuple-element.37), channel_id=1, source_target_pairs={{0,4},{4,8},{8,12},{1,5},{5,9},{9,13},{2,6},{6,10},{10,14},{3,7},{... | collective-permute-start | bytes 1572872 | tf_op jit(solution)/shard_map/ppermute | solution.py:313
  10.4 20.1 %local.2 = (f32[512,512]{1,0:T(8,128)}, bf16[512,512]{1,0:T(8,128)(2,1)S(1)}, f32[4,128,256]{2,1,0:T(8,128)S(1)}, bf16[4,128,128]{2,1,0:T(8,128)(2,1)S(1)}) custom-call(bf16[512,1024]{1,0:T(8,128)(2,1)} %q_ref.5, bf16[512,2,1024]{2,1,0:T(2,128)(2,1)} %k_ref.3, bf16[512,2,1024]{2,1,0:T(2,128)(2,1)} %v_ref.3, f32[2,8,512]{2,1,0:T(8,128)S(1)} %bitcast.2, ...), custom_call_target="tpu_custom_call" | custom-call | flops 20000000000 | bytes 1000000 | tf_op jit(solution)/shard_map/local/pallas_call | solution.py:231
  30.5 3.6 %collective-permute-start = (bf16[4,128,128]{2,1,0:T(8,128)(2,1)S(1)}, bf16[4,128,128]{2,1,0:T(8,128)(2,1)S(1)}, u32[]{:S(2)}, u32[]{:S(2)}) collective-permute-start(bf16[4,128,128]{2,1,0:T(8,128)(2,1)S(1)} %get-tuple-element.19), channel_id=1, source_target_pairs={{0,4},{4,8},{8,12},{1,5},{5,9},{9,13},{2,6},{6,10},{10,14},{3,7},{... | collective-permute-start | bytes 393224 | tf_op jit(solution)/shard_map/ppermute | solution.py:313
  34.1 0.0 collective-permute-done.1.kp_ref
  34.1 20.1 %local.3 = (f32[512,512]{1,0:T(8,128)}, bf16[512,512]{1,0:T(8,128)(2,1)S(1)}, f32[4,128,256]{2,1,0:T(8,128)S(1)}, bf16[4,128,128]{2,1,0:T(8,128)(2,1)S(1)}) custom-call(bf16[512,1024]{1,0:T(8,128)(2,1)} %q_ref.5, bf16[512,2,1024]{2,1,0:T(2,128)(2,1)} %k_ref.3, bf16[512,2,1024]{2,1,0:T(2,128)(2,1)} %v_ref.3, f32[2,8,512]{2,1,0:T(8,128)S(1)} %bitcast.3, ...), custom_call_target="tpu_custom_call" | custom-call | flops 20000000000 | bytes 1000000 | tf_op jit(solution)/shard_map/local/pallas_call | solution.py:231
  54.2 0.0 collective-permute-done.z_ref
  54.2 0.2 hop.6
  54.5 2.1 %collective-permute-start.7 = (bf16[4,128,128]{2,1,0:T(8,128)(2,1)S(1)}, bf16[4,128,128]{2,1,0:T(8,128)(2,1)S(1)}, u32[]{:S(2)}, u32[]{:S(2)}) collective-permute-start(bf16[4,128,128]{2,1,0:T(8,128)(2,1)S(1)} %hop.6), channel_id=1, source_target_pairs={{0,4},{4,8},{8,12},{1,5},{5,9},{9,13},{2,6},{6,10},{10,14},{3,7},{... | collective-permute-start | bytes 393224 | tf_op jit(solution)/shard_map/ppermute | solution.py:313
  56.5 1.9 %collective-permute-start.3 = (bf16[4,128,128]{2,1,0:T(8,128)(2,1)S(1)}, bf16[4,128,128]{2,1,0:T(8,128)(2,1)S(1)}, u32[]{:S(2)}, u32[]{:S(2)}) collective-permute-start(bf16[4,128,128]{2,1,0:T(8,128)(2,1)S(1)} %get-tuple-element.24), channel_id=1, source_target_pairs={{0,4},{4,8},{8,12},{1,5},{5,9},{9,13},{2,6},{6,10},{10,14},{3,7},{... | collective-permute-start | bytes 393224 | tf_op jit(solution)/shard_map/ppermute | solution.py:313
  58.5 1.7 %collective-permute-done.7.z_ref = bf16[4,128,128]{2,1,0:T(8,128)(2,1)S(1)} collective-permute-done((bf16[4,128,128]{2,1,0:T(8,128)(2,1)S(1)}, bf16[4,128,128]{2,1,0:T(8,128)(2,1)S(1)}, u32[]{:S(2)}, u32[]{:S(2)}) %collective-permute-start.7) | collective-permute-done | bytes 131104 | tf_op jit(solution)/shard_map/ppermute | solution.py:313
  60.2 0.5 finish.3
  60.6 4.4 %collective-permute-start.8 = (bf16[512,512]{1,0:T(8,128)(2,1)S(1)}, bf16[512,512]{1,0:T(8,128)(2,1)S(1)}, u32[]{:S(2)}, u32[]{:S(2)}) collective-permute-start(bf16[512,512]{1,0:T(8,128)(2,1)S(1)} %finish.3), channel_id=1, source_target_pairs={{0,4},{4,8},{8,12},{1,5},{5,9},{9,13},{2,6},{6,10},{10,14},{3,7},{... | collective-permute-start | bytes 1572872 | tf_op jit(solution)/shard_map/ppermute | solution.py:313
  65.1 0.2 hop.4
  65.3 0.0 copy-start.4
  65.3 2.0 %collective-permute-start.4 = (bf16[4,128,128]{2,1,0:T(8,128)(2,1)S(1)}, bf16[4,128,128]{2,1,0:T(8,128)(2,1)S(1)}, u32[]{:S(2)}, u32[]{:S(2)}) collective-permute-start(bf16[4,128,128]{2,1,0:T(8,128)(2,1)S(1)} %hop.4), channel_id=1, source_target_pairs={{0,4},{4,8},{8,12},{1,5},{5,9},{9,13},{2,6},{6,10},{10,14},{3,7},{... | collective-permute-start | bytes 393224 | tf_op jit(solution)/shard_map/ppermute | solution.py:313
  67.3 0.2 hop.7
  67.6 2.8 %collective-permute-start.9 = (bf16[4,128,128]{2,1,0:T(8,128)(2,1)S(1)}, bf16[4,128,128]{2,1,0:T(8,128)(2,1)S(1)}, u32[]{:S(2)}, u32[]{:S(2)}) collective-permute-start(bf16[4,128,128]{2,1,0:T(8,128)(2,1)S(1)} %hop.7), channel_id=1, source_target_pairs={{0,4},{4,8},{8,12},{1,5},{5,9},{9,13},{2,6},{6,10},{10,14},{3,7},{... | collective-permute-start | bytes 393224 | tf_op jit(solution)/shard_map/ppermute | solution.py:313
  70.3 7.4 %collective-permute-done.4.z_ref = bf16[4,128,128]{2,1,0:T(8,128)(2,1)S(1)} collective-permute-done((bf16[4,128,128]{2,1,0:T(8,128)(2,1)S(1)}, bf16[4,128,128]{2,1,0:T(8,128)(2,1)S(1)}, u32[]{:S(2)}, u32[]{:S(2)}) %collective-permute-start.4) | collective-permute-done | bytes 131104 | tf_op jit(solution)/shard_map/ppermute | solution.py:313
  77.7 0.5 finish.2
  78.2 0.0 copy-start
  78.2 0.0 copy-start.1
  78.2 4.5 %collective-permute-start.5 = (bf16[512,512]{1,0:T(8,128)(2,1)S(1)}, bf16[512,512]{1,0:T(8,128)(2,1)S(1)}, u32[]{:S(2)}, u32[]{:S(2)}) collective-permute-start(bf16[512,512]{1,0:T(8,128)(2,1)S(1)} %finish.2), channel_id=1, source_target_pairs={{0,4},{4,8},{8,12},{1,5},{5,9},{9,13},{2,6},{6,10},{10,14},{3,7},{... | collective-permute-start | bytes 1572872 | tf_op jit(solution)/shard_map/ppermute | solution.py:313
  82.8 0.2 hop.5
  83.0 2.0 %collective-permute-start.6 = (bf16[4,128,128]{2,1,0:T(8,128)(2,1)S(1)}, bf16[4,128,128]{2,1,0:T(8,128)(2,1)S(1)}, u32[]{:S(2)}, u32[]{:S(2)}) collective-permute-start(bf16[4,128,128]{2,1,0:T(8,128)(2,1)S(1)} %hop.5), channel_id=1, source_target_pairs={{0,4},{4,8},{8,12},{1,5},{5,9},{9,13},{2,6},{6,10},{10,14},{3,7},{... | collective-permute-start | bytes 393224 | tf_op jit(solution)/shard_map/ppermute | solution.py:313
  85.0 0.0 collective-permute-done.9.z_ref
  85.0 0.0 collective-permute-done.8.vp_ref
  85.0 6.0 %attend.2 = (bf16[512,1024]{1,0:T(8,128)(2,1)}, bf16[512,1024]{1,0:T(8,128)(2,1)}) custom-call(bf16[512,1024]{1,0:T(8,128)(2,1)S(1)} %copy-done.1, bf16[512,512]{1,0:T(8,128)(2,1)S(1)} %collective-permute-done.1.kp_ref, bf16[512,1024]{1,0:T(8,128)(2,1)S(1)} %copy-done, bf16[512,512]{1,0:T(8,128)(2,1)S(1)} %collective-permute-done.8.vp_ref, ...), custom_call_target="tpu_custom_call" | custom-call | flops 5200000000 | bytes 1000000 | tf_op jit(solution)/shard_map/attend/pallas_call | solution.py:303
  91.0 2.0 %collective-permute-done.6.z_ref = bf16[4,128,128]{2,1,0:T(8,128)(2,1)S(1)} collective-permute-done((bf16[4,128,128]{2,1,0:T(8,128)(2,1)S(1)}, bf16[4,128,128]{2,1,0:T(8,128)(2,1)S(1)}, u32[]{:S(2)}, u32[]{:S(2)}) %collective-permute-start.6) | collective-permute-done | bytes 131104 | tf_op jit(solution)/shard_map/ppermute | solution.py:313
  93.0 0.0 collective-permute-done.5.vp_ref
  93.0 6.0 %attend.3 = (bf16[512,1024]{1,0:T(8,128)(2,1)}, bf16[512,1024]{1,0:T(8,128)(2,1)}) custom-call(bf16[512,1024]{1,0:T(8,128)(2,1)S(1)} %copy-done.1, bf16[512,512]{1,0:T(8,128)(2,1)S(1)} %collective-permute-done.2.kp_ref, bf16[512,1024]{1,0:T(8,128)(2,1)S(1)} %copy-done, ...), custom_call_target="tpu_custom_call", output_to_operand_aliasing={{0}: (7, {}), {1}: (8, {})} | custom-call | flops 5200000000 | bytes 1000000 | tf_op jit(solution)/shard_map/attend/pallas_call | solution.py:303
  (11 shorter events, 0.0 us)
Async XLA Ops:
  0.6 9.8 %copy-start.3 = (f32[512,8]{0,1:T(8,128)S(1)}, f32[512,8]{0,1:T(8,128)}, u32[]{:S(2)}) copy-start(f32[512,8]{0,1:T(8,128)} %param.11) | copy-start | bytes 49156
  0.6 9.8 %copy-start.2 = (f32[512,2,8]{0,2,1:T(8,128)S(1)}, f32[512,2,8]{0,2,1:T(8,128)}, u32[]{:S(2)}) copy-start(f32[512,2,8]{0,2,1:T(8,128)} %param.10) | copy-start | bytes 98308
  1.9 52.3 %collective-permute-start.2 = (bf16[512,512]{1,0:T(8,128)(2,1)S(1)}, bf16[512,512]{1,0:T(8,128)(2,1)S(1)}, u32[]{:S(2)}, u32[]{:S(2)}) collective-permute-start(bf16[512,512]{1,0:T(8,128)(2,1)S(1)} %get-tuple-element.36), channel_id=1, source_target_pairs={{0,4},{4,8},{8,12},{1,5},{5,9},{9,13},{2,6},{6,10},{10,14},{3,7},{... | collective-permute-start | bytes 1572872 | tf_op jit(solution)/shard_map/ppermute | solution.py:313
  6.9 27.2 %collective-permute-start.1 = (bf16[512,512]{1,0:T(8,128)(2,1)S(1)}, bf16[512,512]{1,0:T(8,128)(2,1)S(1)}, u32[]{:S(2)}, u32[]{:S(2)}) collective-permute-start(bf16[512,512]{1,0:T(8,128)(2,1)S(1)} %get-tuple-element.37), channel_id=1, source_target_pairs={{0,4},{4,8},{8,12},{1,5},{5,9},{9,13},{2,6},{6,10},{10,14},{3,7},{... | collective-permute-start | bytes 1572872 | tf_op jit(solution)/shard_map/ppermute | solution.py:313
  30.5 23.7 %collective-permute-start = (bf16[4,128,128]{2,1,0:T(8,128)(2,1)S(1)}, bf16[4,128,128]{2,1,0:T(8,128)(2,1)S(1)}, u32[]{:S(2)}, u32[]{:S(2)}) collective-permute-start(bf16[4,128,128]{2,1,0:T(8,128)(2,1)S(1)} %get-tuple-element.19), channel_id=1, source_target_pairs={{0,4},{4,8},{8,12},{1,5},{5,9},{9,13},{2,6},{6,10},{10,14},{3,7},{... | collective-permute-start | bytes 393224 | tf_op jit(solution)/shard_map/ppermute | solution.py:313
  54.2 5.9 %copy-start.5 = (f32[512,512]{1,0:T(8,128)S(1)}, f32[512,512]{1,0:T(8,128)}, u32[]{:S(2)}) copy-start(f32[512,512]{1,0:T(8,128)} %get-tuple-element.30.o_ref) | copy-start | bytes 3145732
  54.5 5.7 %collective-permute-start.7 = (bf16[4,128,128]{2,1,0:T(8,128)(2,1)S(1)}, bf16[4,128,128]{2,1,0:T(8,128)(2,1)S(1)}, u32[]{:S(2)}, u32[]{:S(2)}) collective-permute-start(bf16[4,128,128]{2,1,0:T(8,128)(2,1)S(1)} %hop.6), channel_id=1, source_target_pairs={{0,4},{4,8},{8,12},{1,5},{5,9},{9,13},{2,6},{6,10},{10,14},{3,7},{... | collective-permute-start | bytes 393224 | tf_op jit(solution)/shard_map/ppermute | solution.py:313
  56.5 8.5 %collective-permute-start.3 = (bf16[4,128,128]{2,1,0:T(8,128)(2,1)S(1)}, bf16[4,128,128]{2,1,0:T(8,128)(2,1)S(1)}, u32[]{:S(2)}, u32[]{:S(2)}) collective-permute-start(bf16[4,128,128]{2,1,0:T(8,128)(2,1)S(1)} %get-tuple-element.24), channel_id=1, source_target_pairs={{0,4},{4,8},{8,12},{1,5},{5,9},{9,13},{2,6},{6,10},{10,14},{3,7},{... | collective-permute-start | bytes 393224 | tf_op jit(solution)/shard_map/ppermute | solution.py:313
  60.6 24.4 %collective-permute-start.8 = (bf16[512,512]{1,0:T(8,128)(2,1)S(1)}, bf16[512,512]{1,0:T(8,128)(2,1)S(1)}, u32[]{:S(2)}, u32[]{:S(2)}) collective-permute-start(bf16[512,512]{1,0:T(8,128)(2,1)S(1)} %finish.3), channel_id=1, source_target_pairs={{0,4},{4,8},{8,12},{1,5},{5,9},{9,13},{2,6},{6,10},{10,14},{3,7},{... | collective-permute-start | bytes 1572872 | tf_op jit(solution)/shard_map/ppermute | solution.py:313
  65.3 12.4 %copy-start.4 = (f32[512,512]{1,0:T(8,128)S(1)}, f32[512,512]{1,0:T(8,128)}, u32[]{:S(2)}) copy-start(f32[512,512]{1,0:T(8,128)} %get-tuple-element.26.o_ref) | copy-start | bytes 3145732
  65.3 12.4 %collective-permute-start.4 = (bf16[4,128,128]{2,1,0:T(8,128)(2,1)S(1)}, bf16[4,128,128]{2,1,0:T(8,128)(2,1)S(1)}, u32[]{:S(2)}, u32[]{:S(2)}) collective-permute-start(bf16[4,128,128]{2,1,0:T(8,128)(2,1)S(1)} %hop.4), channel_id=1, source_target_pairs={{0,4},{4,8},{8,12},{1,5},{5,9},{9,13},{2,6},{6,10},{10,14},{3,7},{... | collective-permute-start | bytes 393224 | tf_op jit(solution)/shard_map/ppermute | solution.py:313
  67.6 17.4 %collective-permute-start.9 = (bf16[4,128,128]{2,1,0:T(8,128)(2,1)S(1)}, bf16[4,128,128]{2,1,0:T(8,128)(2,1)S(1)}, u32[]{:S(2)}, u32[]{:S(2)}) collective-permute-start(bf16[4,128,128]{2,1,0:T(8,128)(2,1)S(1)} %hop.7), channel_id=1, source_target_pairs={{0,4},{4,8},{8,12},{1,5},{5,9},{9,13},{2,6},{6,10},{10,14},{3,7},{... | collective-permute-start | bytes 393224 | tf_op jit(solution)/shard_map/ppermute | solution.py:313
  78.2 6.8 %copy-start = (bf16[512,1024]{1,0:T(8,128)(2,1)S(1)}, bf16[512,1024]{1,0:T(8,128)(2,1)}, u32[]{:S(2)}) copy-start(bf16[512,1024]{1,0:T(8,128)(2,1)} %ko_ref.3) | copy-start | bytes 3145732
  78.2 6.8 %copy-start.1 = (bf16[512,1024]{1,0:T(8,128)(2,1)S(1)}, bf16[512,1024]{1,0:T(8,128)(2,1)}, u32[]{:S(2)}) copy-start(bf16[512,1024]{1,0:T(8,128)(2,1)} %q_ref.7) | copy-start | bytes 3145732
  78.2 14.8 %collective-permute-start.5 = (bf16[512,512]{1,0:T(8,128)(2,1)S(1)}, bf16[512,512]{1,0:T(8,128)(2,1)S(1)}, u32[]{:S(2)}, u32[]{:S(2)}) collective-permute-start(bf16[512,512]{1,0:T(8,128)(2,1)S(1)} %finish.2), channel_id=1, source_target_pairs={{0,4},{4,8},{8,12},{1,5},{5,9},{9,13},{2,6},{6,10},{10,14},{3,7},{... | collective-permute-start | bytes 1572872 | tf_op jit(solution)/shard_map/ppermute | solution.py:313
  83.0 10.0 %collective-permute-start.6 = (bf16[4,128,128]{2,1,0:T(8,128)(2,1)S(1)}, bf16[4,128,128]{2,1,0:T(8,128)(2,1)S(1)}, u32[]{:S(2)}, u32[]{:S(2)}) collective-permute-start(bf16[4,128,128]{2,1,0:T(8,128)(2,1)S(1)} %hop.5), channel_id=1, source_target_pairs={{0,4},{4,8},{8,12},{1,5},{5,9},{9,13},{2,6},{6,10},{10,14},{3,7},{... | collective-permute-start | bytes 393224 | tf_op jit(solution)/shard_map/ppermute | solution.py:313

commit v3 on v2

--- a/solution.py
+++ b/solution.py
@@ -51,39 +51,63 @@
 def block_masks(C):
     i = lax.broadcasted_iota(jnp.int32, (C, C), 0)
     j = lax.broadcasted_iota(jnp.int32, (C, C), 1)
-    masks = {0: ((i // 4) == (j // 4)).astype(bf16)}
-    s = 4
+    masks = {}
+    s = BASE
     while s < C:
         masks[s] = (((i // (2 * s)) == (j // (2 * s))) & ((i // s) != (j // s))).astype(bf16)
         s *= 2
     return masks, (i == j).astype(f32)
 
 
+BASE = 16
+
+
+def base_inverses(A):
+    C = A[0].shape[0]
+    i = lax.broadcasted_iota(jnp.int32, (C, C), 0)
+    j = lax.broadcasted_iota(jnp.int32, (C, C), 1)
+    place = (j // BASE - i // BASE) & (C // BASE - 1)
+    first = j & ~(BASE - 1)
+    zero = jnp.zeros((C, C), f32)
+    halves = lambda x: [x.reshape(C // BASE, BASE, C)[:, r:r + 8] for r in (0, 8)]
+    packs = []
+    for at in range(0, len(A), C // BASE):
+        packed = zero
+        for p, a in enumerate(A[at:at + C // BASE]):
+            packed = jnp.where(place == p, pltpu.roll(a, BASE * p, 1) if p else a, packed)
+        packs.append(packed)
+    start = halves(((j & (BASE - 1)) == (i & (BASE - 1))).astype(f32))
+    X = [list(start) for _ in packs]
+    for k in range(BASE - 1):
+        for x, packed in zip(X, packs):
+            lo, hi = halves(jnp.take_along_axis(packed, first + k, axis=1))
+            row = x[k // 8][:, k % 8:k % 8 + 1]
+            if k < 7:
+                x[0] = x[0] - lo * row
+            x[1] = x[1] - hi * row
+    out = []
+    for x, at in zip(X, range(0, len(A), C // BASE)):
+        whole = jnp.concatenate(x, axis=1).reshape(C, C)
+        for p in range(min(len(A) - at, C // BASE)):
+            out.append(jnp.where(place == 0, pltpu.roll(whole, C - BASE * p, 1) if p else whole, zero))
+    return out
+
+
 def inverses(A, masks, eye):
     C = eye.shape[0]
-    eb = eye.astype(bf16)
     As = [split(a) for a in A]
-    small = [(a[0] * masks[0], a[1] * masks[0]) for a in As]
-    square = [split(product(a, a)) for a in small]
-    start = [(eb - a[0], -a[1]) for a in small]
-    X = [t[0].astype(f32) + t[1].astype(f32) + product(t, p) for t, p in zip(start, square)]
+    X = base_inverses(A)
     Xs = [split(x) for x in X]
-    s = 4
+    s = BASE
     while s < C:
-        if s < 16:
-            m = masks[s]
-            B = [split(product((a[0] * m, a[1] * m), x)) for a, x in zip(As, Xs)]
-            X = [x - product(xs, b) for x, xs, b in zip(X, Xs, B)]
-            Xs = [split(x) for x in X]
-        else:
-            m = odd(masks[s], s)
-            B = [split(product((odd(a[0], s) * m, odd(a[1], s) * m), x)) for a, x in zip(As, Xs)]
-            B = [(weave(None, b[0], s), weave(None, b[1], s)) for b in B]
-            Xo = [odd(x, s) - product((odd(xs[0], s), odd(xs[1], s)), b) for x, xs, b in zip(X, Xs, B)]
-            X = [weave(x, o, s) for x, o in zip(X, Xo)]
-            if 2 * s < C:
-                So = [split(o) for o in Xo]
-                Xs = [(weave(x[0], o[0], s), weave(x[1], o[1], s)) for x, o in zip(Xs, So)]
+        m = odd(masks[s], s)
+        B = [split(product((odd(a[0], s) * m, odd(a[1], s) * m), x)) for a, x in zip(As, Xs)]
+        B = [(weave(None, b[0], s), weave(None, b[1], s)) for b in B]
+        Xo = [odd(x, s) - product((odd(xs[0], s), odd(xs[1], s)), b) for x, xs, b in zip(X, Xs, B)]
+        X = [weave(x, o, s) for x, o in zip(X, Xo)]
+        if 2 * s < C:
+            So = [split(o) for o in Xo]
+            Xs = [(weave(x[0], o[0], s), weave(x[1], o[1], s)) for x, o in zip(Xs, So)]
         s *= 2
     return X
 
@@ -139,6 +163,7 @@
 
 
 D = 128
+LOCAL = 1
 
 
 def params(mib):
@@ -149,7 +174,7 @@
     return pl.CostEstimate(flops=int(us * 10**9), bytes_accessed=10**6, transcendentals=0)
 
 
-def local_body(q_ref, k_ref, v_ref, b_ref, l_ref, o_ref, qe_ref, yo_ref, a_ref, y_ref, r_ref, *, HB, NC, first):
+def local_body(q_ref, k_ref, v_ref, b_ref, l_ref, o_ref, qe_ref, yo_ref, am_ref, a_ref, y_ref, r_ref, *, HB, NC, first):
     c = pl.program_id(0)
     T = q_ref.shape[0] // NC
     C = 2 * T
@@ -216,6 +241,7 @@
     def _():
         for h in H:
             yo_ref[h] = Y[h]
+            am_ref[h] = Y[h].astype(bf16)
             a_ref[h] = Y[h][:, :d].astype(bf16)
 
 
@@ -232,14 +258,25 @@
         functools.partial(local_body, HB=HB, NC=NC, first=g * HB),
         grid=(n // B,),
         in_specs=[flat, pair, pair, whole(2, heads, n), whole(heads, n)],
-        out_specs=[out, out, whole(HB, D, 2 * D), whole(HB, D, D)],
-        out_shape=[jax.ShapeDtypeStruct((n, wg), f32), jax.ShapeDtypeStruct((n, wg), bf16), jax.ShapeDtypeStruct((HB, D, 2 * D), f32), jax.ShapeDtypeStruct((HB, D, D), bf16)],
+        out_specs=[out, out, whole(HB, D, 2 * D), whole(HB, D, 2 * D), whole(HB, D, D)],
+        out_shape=[jax.ShapeDtypeStruct((n, wg), f32), jax.ShapeDtypeStruct((n, wg), bf16), jax.ShapeDtypeStruct((HB, D, 2 * D), f32), jax.ShapeDtypeStruct((HB, D, 2 * D), bf16), jax.ShapeDtypeStruct((HB, D, D), bf16)],
         scratch_shapes=[pltpu.VMEM((HB, D, 2 * D), f32), pltpu.VMEM((n // T, 24, 2 * T), f32)],
-        cost_estimate=cost(HB * 5), name="local", compiler_params=params(52),
+        cost_estimate=cost(HB * LOCAL), name="local", compiler_params=params(52),
     )(queries, keys, values, betas, decay)
 
 
 VMEM = pl.BlockSpec(memory_space=pltpu.VMEM)
+
+
+def meet_body(am_ref, a_ref, z_ref):
+    for h in range(z_ref.shape[0]):
+        z_ref[h] = (am_ref[h, :, :D].astype(f32) + dot(am_ref[h, :, D:], a_ref[h])).astype(bf16)
+
+
+def meet(am, a):
+    return pl.pallas_call(
+        meet_body, in_specs=[VMEM, VMEM], out_specs=VMEM, out_shape=jax.ShapeDtypeStruct(a.shape, bf16),
+        cost_estimate=cost(0.3), name="meet", compiler_params=params(8))(am, a)
 
 
 def hop_body(y_ref, z_ref, out_ref):
@@ -252,36 +289,33 @@
 def hop(y, z):
     return pl.pallas_call(
         hop_body, in_specs=[VMEM, VMEM], out_specs=VMEM, out_shape=jax.ShapeDtypeStruct(z.shape, bf16),
-        cost_estimate=cost(1), name="hop", compiler_params=params(8))(y, z)
-
-
-def finish_body(o_ref, qe_ref, z_ref, out_ref):
+        cost_estimate=cost(0.3), name="hop", compiler_params=params(8))(y, z)
+
+
+def leave_body(o_ref, qe_ref, y_ref, z_ref, out_ref):
+    n = o_ref.shape[0]
     for h in range(z_ref.shape[0]):
         s = slice(h * D, h * D + D)
-        out_ref[:, s] = (o_ref[:, s] + dot(qe_ref[:, s], z_ref[h])).astype(bf16)
-
-
-def finish(o, qe, z, B=256):
+        z = z_ref[h]
+        hi, lo = split(y_ref[h, :, D:])
+        out_ref[:n, s] = (o_ref[:, s] + dot(qe_ref[:, s], z)).astype(bf16)
+        out_ref[n:, s] = (y_ref[h, :, :D] + dot(cat([hi, lo], 1), cat([z, z], 0))).astype(bf16)
+
+
+def leave(o, qe, y, z):
     n, w = o.shape
-    spec = pl.BlockSpec((B, w), lambda i: (i, 0))
-    return pl.pallas_call(
-        finish_body, grid=(n // B,), in_specs=[spec, spec, VMEM], out_specs=spec,
-        out_shape=jax.ShapeDtypeStruct((n, w), bf16), cost_estimate=cost(2), name="finish", compiler_params=params(8))(o, qe, z)
-
-
-def attend_body(q_ref, kp_ref, ko_ref, vp_ref, o_ref, qe_ref, z_ref, *refs, axis, R, first):
-    ret_ref, out_ref = refs[-2:]
+    return pl.pallas_call(
+        leave_body, in_specs=[VMEM] * 4, out_specs=VMEM, out_shape=jax.ShapeDtypeStruct((n + D, w), bf16),
+        cost_estimate=cost(0.5), name="leave", compiler_params=params(8))(o, qe, y, z)
+
+
+def weigh_body(q_ref, kp_ref, ko_ref, p_ref, *, axis, R, first):
     n = q_ref.shape[0]
     h = pl.program_id(0)
     bias = jnp.where(lax.axis_index(axis) > 0, 0.0, -1e30).astype(f32)
     scale = D ** -0.5 * math.log2(math.e)
-    ones = jnp.ones((n, D), bf16)
     tri = lax.broadcasted_iota(jnp.int32, (R, R), 1) <= lax.broadcasted_iota(jnp.int32, (R, R), 0)
-    ret = (o_ref[...] + dot(qe_ref[...], z_ref[h])).astype(bf16)
-    ret_ref[...] = ret
-    kp = kp_ref[:, pl.ds(pl.multiple_of(h * D, D), D)]
-    vp = cat([vp_ref[:, pl.ds(pl.multiple_of(h * D, D), D)], ones], 1)
-    vo = cat([ret, ones], 1)
+    kp = kp_ref[:, pl.ds(pl.multiple_of((first + h) * D, D), D)]
     for i in range(n // R):
         q = q_ref[i * R:(i + 1) * R]
         sp = dot_nt(q, kp) + bias
@@ -289,28 +323,48 @@
         diag = jnp.where(tri, so[:, i * R:], -1e30)
         so = diag if i == 0 else cat([so[:, :i * R], diag], 1)
         m = jnp.maximum(jnp.max(sp, 1, keepdims=True), jnp.max(so, 1, keepdims=True))
-        ep = jnp.exp2((sp - m) * scale).astype(bf16)
-        eo = jnp.exp2((so - m) * scale).astype(bf16)
-        r = dot(ep, vp) + dot(eo, vo[:(i + 1) * R])
-        out_ref[i * R:(i + 1) * R] = (r[:, :D] / r[:, D:]).astype(bf16)
-
-
-def attend(q, kp, ko, vp, o, qe, z, carry, g, HB, R=256, axis="ctx"):
+        ep = jnp.exp2((sp - m) * scale)
+        eo = jnp.exp2((so - m) * scale)
+        inv = 1.0 / (jnp.sum(ep, 1, keepdims=True) + jnp.sum(eo, 1, keepdims=True))
+        p_ref[0, i * R:(i + 1) * R, :n] = (ep * inv).astype(bf16)
+        p_ref[0, i * R:(i + 1) * R, n:n + (i + 1) * R] = (eo * inv).astype(bf16)
+        if (i + 1) * R < n:
+            p_ref[0, i * R:(i + 1) * R, n + (i + 1) * R:] = jnp.zeros((R, n - (i + 1) * R), bf16)
+
+
+def weigh(q, kp, ko, g, HB, R=256, axis="ctx"):
     n, w = q.shape
     flat = pl.BlockSpec((n, D), lambda h: (0, g * HB + h))
+    return pl.pallas_call(
+        functools.partial(weigh_body, axis=axis, R=R, first=g * HB), grid=(HB,),
+        in_specs=[flat, VMEM, flat], out_specs=pl.BlockSpec((1, n, 2 * n), lambda h: (h, 0, 0)),
+        out_shape=jax.ShapeDtypeStruct((HB, n, 2 * n), bf16),
+        cost_estimate=cost(HB * 1.3), name="weigh", compiler_params=params(24))(q, kp, ko)
+
+
+def gather_body(o_ref, qe_ref, p_ref, vz_ref, *refs):
+    ret_ref, out_ref = refs[-2:]
+    n = o_ref.shape[0]
+    vz = vz_ref[:, pl.ds(pl.multiple_of(pl.program_id(0) * D, D), D)]
+    ret = (o_ref[...] + dot(qe_ref[...], vz[n:])).astype(bf16)
+    ret_ref[...] = ret
+    out_ref[...] = dot(p_ref[0], cat([vz[:n], ret], 0)).astype(bf16)
+
+
+def gather(o, qe, p, vz, carry, g, HB, w):
+    n = o.shape[0]
     part = pl.BlockSpec((n, D), lambda h: (0, h))
+    flat = pl.BlockSpec((n, D), lambda h: (0, g * HB + h))
     held = [pl.BlockSpec(memory_space=pl.ANY)] * len(carry)
     return pl.pallas_call(
-        functools.partial(attend_body, axis=axis, R=R, first=g * HB), grid=(HB,),
-        in_specs=[flat, VMEM, flat, VMEM, part, part, VMEM] + held, out_specs=[flat, flat],
-        out_shape=[jax.ShapeDtypeStruct((n, w), bf16)] * 2,
-        input_output_aliases={7 + i: i for i in range(len(carry))},
-        cost_estimate=cost(HB * 1.3), name="attend", compiler_params=params(24))(q, kp, ko, vp, o, qe, z, *carry)
-
-
-def from_behind(array, axis):
-    n = lax.axis_size(axis)
-    return lax.ppermute(array, axis, [(i, i + 1) for i in range(n - 1)])
+        gather_body, grid=(HB,), in_specs=[part, part, pl.BlockSpec((1, n, 2 * n), lambda h: (h, 0, 0)), VMEM] + held,
+        out_specs=[flat, flat], out_shape=[jax.ShapeDtypeStruct((n, w), bf16)] * 2,
+        input_output_aliases={4 + i: i for i in range(len(carry))},
+        cost_estimate=cost(HB * 0.5), name="gather", compiler_params=params(24))(o, qe, p, vz, *carry)
+
+
+def send(array, pairs):
+    return lax.ppermute(array, "ctx", pairs) if pairs else jnp.zeros_like(array)
 
 
 GROUPS = 2
@@ -319,36 +373,33 @@
 def per_device(queries, keys, values, betas, log_decay, attn_queries, attn_keys):
     n, w = queries.shape
     HB = w // D // GROUPS
-    hops = lax.axis_size("ctx") - 1
+    blocks = lax.axis_size("ctx")
+    every = [(i, i + 1) for i in range(blocks - 1)]
     G = range(GROUPS)
     beta_rows = betas.transpose(1, 2, 0)
     decay_rows = log_decay.transpose(1, 0)
-    keys_behind = []
-    parts = []
+    keys_behind = send(attn_keys, every)
+    parts, near, far, crossing = [], [], [], []
     for g in G:
-        if g:
-            decay_rows, keys_behind[-1] = lax.optimization_barrier((decay_rows, keys_behind[-1]))
-        keys_behind.append(from_behind(attn_keys[:, g * HB * D:(g + 1) * HB * D], "ctx"))
         parts.append(local(queries, keys, values, beta_rows, decay_rows, g, HB, math.gcd(16 // HB, n // 64)))
-    z = [jnp.zeros_like(p[3]) for p in parts]
-    behind = [None] * GROUPS
-    for k in range(hops):
-        for g in G:
-            o, qe, y, a = parts[g]
-            if k == 1 and g < GROUPS - 1:
-                z[g], parts[-1], keys_behind[-1] = lax.optimization_barrier((z[g], parts[-1], keys_behind[-1]))
-                o, qe, y, a = parts[g]
-            sent = a if k == 0 else hop(y, z[g])
-            if k == hops - 1:
-                ret = finish(o, qe, z[g])
-            z[g] = from_behind(sent, "ctx")
-            if k == hops - 1:
-                behind[g] = from_behind(ret, "ctx")
-    carry = ()
+        am, a = parts[g][3:]
+        near.append(send(am, every[:2]))
+        far.append(send(a, [(0, 2)] if blocks > 2 else []))
     for g in G:
-        o, qe, y, a = parts[g]
-        carry = attend(attn_queries, keys_behind[g], attn_keys, behind[g], o, qe, z[g], carry, g, HB)
-    return tuple(carry)
+        if g < GROUPS - 1:
+            near[g], far[g], parts[-1], keys_behind = lax.optimization_barrier((near[g], far[g], parts[-1], keys_behind))
+        else:
+            weights = [weigh(attn_queries, keys_behind, attn_keys, h, HB) for h in G]
+            near[g], far[g], weights = lax.optimization_barrier((near[g], far[g], weights))
+        z = meet(near[g], far[g])
+        o, qe, y = parts[g][:3]
+        for k in range(3, blocks - 1):
+            z = z + send(hop(y, z), [(k - 1, k)])
+        crossing.append(send(leave(o, qe, y, z), every))
+    done = ()
+    for g in G:
+        done = gather(*parts[g][:2], weights[g], crossing[g], done, g, HB, w)
+    return tuple(done)
 
 
 def solution(mesh):

time: 99.4 us -> 93 us (0.936)
  starting transfers between devices: 31.8 us -> 17.6 us
  waiting for transfers between devices: 11.1 us -> 20.4 us
  Pallas kernels: 53.8 us -> 52.3 us
    ppermute x10 -> x7, starting transfers between devices: 31.8 us -> 17.6 us  [send(): return lax.ppermute(array, 'ctx', pairs) if pairs else jnp.zeros_like(array)]
    ppermute x10 -> x7, waiting for transfers between devices: 11.1 us -> 20.4 us  [send(): return lax.ppermute(array, 'ctx', pairs) if pairs else jnp.zeros_like(array)]
    unnamed x12 -> x14, local copies, waits for them, and re-layouts: 0.03 us -> 1.5 us
    pallas_call x2, Pallas kernels: 40.2 us -> 38.8 us  [local(): pl.pallas_call(functools.partial(local_body, HB=HB, NC=NC, first=g * HB),...]
    slice x1 -> x0, local copies, waits for them, and re-layouts: 1.28 us -> none  [per_device(): attn_keys[:, g * HB * D:(g + 1) * HB * D]]
  transfers between devices with their start and end apart: 10 -> 7, of which waited for: 3 -> 2; matrix products, arithmetic and copies ran while one was open for 0% -> 0% of each run, Pallas kernels for 48% -> 53%
where the time goes in v3:
time: 93 us; the launch traced here: 92.6 us
  Pallas kernels  52.3 us (56%)
  waiting for transfers between devices  20.4 us (22%)
  starting transfers between devices  17.6 us (19%)
  local copies, waits for them, and re-layouts  1.5 us (2%)
    pallas_call x2, Pallas kernels, local(): pl.pallas_call(functools.partial(local_body, HB=HB, NC=NC, first=g * HB),...  38.8 us
    ppermute x7, waiting for transfers between devices, send(): return lax.ppermute(array, 'ctx', pairs) if pairs else jnp.zeros_like(array)  20.4 us
    ppermute x7, starting transfers between devices, send(): return lax.ppermute(array, 'ctx', pairs) if pairs else jnp.zeros_like(array)  17.6 us
    pallas_call x2, Pallas kernels, weigh(): pl.pallas_call(functools.partial(weigh_body, axis=axis, R=R, first=g * HB...  6.64 us
    pallas_call x2, Pallas kernels, gather(): pl.pallas_call(gather_body, grid=(HB,), in_specs=[part, part, pl.BlockSpe...  5.83 us
  transfers between devices with their start and end apart: 7, of which 2 were waited for; matrix products, arithmetic and copies ran while one was open for 0% of the time, Pallas kernels for 53%

profile of v3, /device:TPU:0, one launch (start us, length us, event | category | flops | bytes accessed | tf_op | source)
XLA Modules:
  0.0 92.6 jit_solution(5082721967195663861)
XLA Ops:
  0.6 5.0 %collective-permute-start.2 = (bf16[512,1024]{1,0:T(8,128)(2,1)}, bf16[512,1024]{1,0:T(8,128)(2,1)S(1)}, u32[]{:S(2)}, u32[]{:S(2)}) collective-permute-start(bf16[512,1024]{1,0:T(8,128)(2,1)} %ko_ref.3), channel_id=1, source_target_pairs={{0,4},{4,8},{8,12},{1,5},{5,9},{9,13},{2,6},{6,10},{10,14},{3,7},{... | collective-permute-start | bytes 3145736 | tf_op jit(solution)/shard_map/ppermute | solution.py:367
  5.6 0.0 copy-start.4
  5.6 0.7 copy-done.4
  6.4 0.7 copy-done.5
  7.1 19.3 %local.2 = (f32[512,512]{1,0:T(8,128)}, bf16[512,512]{1,0:T(8,128)(2,1)S(1)}, f32[4,128,256]{2,1,0:T(8,128)S(1)}, bf16[4,128,256]{2,1,0:T(8,128)(2,1)S(1)}, bf16[4,128,128]{2,1,0:T(8,128)(2,1)S(1)}) custom-call(bf16[512,1024]{1,0:T(8,128)(2,1)} %q_ref.5, bf16[512,2,1024]{2,1,0:T(2,128)(2,1)} %k_ref.3, bf16[512,2,1024]{2,1,0:T(2,128)(2,1)} %v_ref.3, ...), custom_call_target="tpu_custom_call" | custom-call | flops 4000000000 | bytes 1000000 | tf_op jit(solution)/shard_map/local/pallas_call | solution.py:257
  26.4 3.4 %collective-permute-start = (bf16[4,128,256]{2,1,0:T(8,128)(2,1)S(1)}, bf16[4,128,256]{2,1,0:T(8,128)(2,1)S(1)}, u32[]{:S(2)}, u32[]{:S(2)}) collective-permute-start(bf16[4,128,256]{2,1,0:T(8,128)(2,1)S(1)} %get-tuple-element.24), channel_id=1, source_target_pairs={{0,4},{4,8},{1,5},{5,9},{2,6},{6,10},{3,7},{7,11},{16,20},{20,24},... | collective-permute-start | bytes 786440 | tf_op jit(solution)/shard_map/ppermute | solution.py:367
  29.9 0.0 copy-start.1
  29.9 0.0 copy-start.2
  29.9 0.0 copy-start.3
  29.9 2.7 %collective-permute-start.1 = (bf16[4,128,128]{2,1,0:T(8,128)(2,1)S(1)}, bf16[4,128,128]{2,1,0:T(8,128)(2,1)S(1)}, u32[]{:S(2)}, u32[]{:S(2)}) collective-permute-start(bf16[4,128,128]{2,1,0:T(8,128)(2,1)S(1)} %get-tuple-element.25), channel_id=1, source_target_pairs={{0,8},{1,9},{2,10},{3,11},{16,24},{17,25},{18,26},{19,27}} | collective-permute-start | bytes 393224 | tf_op jit(solution)/shard_map/ppermute | solution.py:367
  32.7 19.4 %local.3 = (f32[512,512]{1,0:T(8,128)}, bf16[512,512]{1,0:T(8,128)(2,1)S(1)}, f32[4,128,256]{2,1,0:T(8,128)S(1)}, bf16[4,128,256]{2,1,0:T(8,128)(2,1)S(1)}, bf16[4,128,128]{2,1,0:T(8,128)(2,1)S(1)}) custom-call(bf16[512,1024]{1,0:T(8,128)(2,1)} %q_ref.5, bf16[512,2,1024]{2,1,0:T(2,128)(2,1)} %k_ref.3, bf16[512,2,1024]{2,1,0:T(2,128)(2,1)} %v_ref.3, ...), custom_call_target="tpu_custom_call" | custom-call | flops 4000000000 | bytes 1000000 | tf_op jit(solution)/shard_map/local/pallas_call | solution.py:257
  52.1 1.7 %collective-permute-start.3 = (bf16[4,128,256]{2,1,0:T(8,128)(2,1)S(1)}, bf16[4,128,256]{2,1,0:T(8,128)(2,1)S(1)}, u32[]{:S(2)}, u32[]{:S(2)}) collective-permute-start(bf16[4,128,256]{2,1,0:T(8,128)(2,1)S(1)} %get-tuple-element.29), channel_id=1, source_target_pairs={{0,4},{4,8},{1,5},{5,9},{2,6},{6,10},{3,7},{7,11},{16,20},{20,24},... | collective-permute-start | bytes 786440 | tf_op jit(solution)/shard_map/ppermute | solution.py:367
  53.8 1.3 %collective-permute-start.4 = (bf16[4,128,128]{2,1,0:T(8,128)(2,1)S(1)}, bf16[4,128,128]{2,1,0:T(8,128)(2,1)S(1)}, u32[]{:S(2)}, u32[]{:S(2)}) collective-permute-start(bf16[4,128,128]{2,1,0:T(8,128)(2,1)S(1)} %get-tuple-element.30), channel_id=1, source_target_pairs={{0,8},{1,9},{2,10},{3,11},{16,24},{17,25},{18,26},{19,27}} | collective-permute-start | bytes 393224 | tf_op jit(solution)/shard_map/ppermute | solution.py:367
  55.1 0.0 collective-permute-done.1.a_ref
  55.1 0.0 collective-permute-done.am_ref
  55.1 0.0 collective-permute-done.2.kp_ref
  55.1 0.2 meet.3.z_ref
  55.3 0.4 leave.3
  55.7 1.4 %collective-permute-start.6 = (bf16[640,512]{1,0:T(8,128)(2,1)S(1)}, bf16[640,512]{1,0:T(8,128)(2,1)S(1)}, u32[]{:S(2)}, u32[]{:S(2)}) collective-permute-start(bf16[640,512]{1,0:T(8,128)(2,1)S(1)} %leave.3), channel_id=1, source_target_pairs={{0,4},{4,8},{8,12},{1,5},{5,9},{9,13},{2,6},{6,10},{10,14},{3,7},{... | collective-permute-start | bytes 1966088 | tf_op jit(solution)/shard_map/ppermute | solution.py:367
  57.2 0.0 copy-done.2
  57.2 3.3 %weigh.2.p_ref = bf16[4,512,1024]{2,1,0:T(8,128)(2,1)S(1)} custom-call(bf16[512,1024]{1,0:T(8,128)(2,1)S(1)} %copy-done.2, bf16[512,1024]{1,0:T(8,128)(2,1)S(1)} %collective-permute-done.2.kp_ref, bf16[512,1024]{1,0:T(8,128)(2,1)S(1)} %copy-done.3), custom_call_target="tpu_custom_call" | custom-call | flops 5200000000 | bytes 1000000 | tf_op jit(solution)/shard_map/weigh/pallas_call | solution.py:338
  60.5 0.0 copy-start
  60.5 3.3 %weigh.3.p_ref = bf16[4,512,1024]{2,1,0:T(8,128)(2,1)S(1)} custom-call(bf16[512,1024]{1,0:T(8,128)(2,1)S(1)} %copy-done.2, bf16[512,1024]{1,0:T(8,128)(2,1)S(1)} %collective-permute-done.2.kp_ref, bf16[512,1024]{1,0:T(8,128)(2,1)S(1)} %copy-done.3), custom_call_target="tpu_custom_call" | custom-call | flops 5200000000 | bytes 1000000 | tf_op jit(solution)/shard_map/weigh/pallas_call | solution.py:338
  63.8 0.0 collective-permute-done.4.a_ref
  63.8 0.0 collective-permute-done.3.am_ref
  63.9 0.2 meet.2.z_ref
  64.0 0.4 leave.2
  64.4 2.0 %collective-permute-start.5 = (bf16[640,512]{1,0:T(8,128)(2,1)S(1)}, bf16[640,512]{1,0:T(8,128)(2,1)S(1)}, u32[]{:S(2)}, u32[]{:S(2)}) collective-permute-start(bf16[640,512]{1,0:T(8,128)(2,1)S(1)} %leave.2), channel_id=1, source_target_pairs={{0,4},{4,8},{8,12},{1,5},{5,9},{9,13},{2,6},{6,10},{10,14},{3,7},{... | collective-permute-start | bytes 1966088 | tf_op jit(solution)/shard_map/ppermute | solution.py:367
  66.4 11.0 %collective-permute-done.6.vz_ref = bf16[640,512]{1,0:T(8,128)(2,1)S(1)} collective-permute-done((bf16[640,512]{1,0:T(8,128)(2,1)S(1)}, bf16[640,512]{1,0:T(8,128)(2,1)S(1)}, u32[]{:S(2)}, u32[]{:S(2)}) %collective-permute-start.6) | collective-permute-done | bytes 655392 | tf_op jit(solution)/shard_map/ppermute | solution.py:367
  77.4 2.9 %gather.2 = (bf16[512,1024]{1,0:T(8,128)(2,1)}, bf16[512,1024]{1,0:T(8,128)(2,1)}) custom-call(f32[512,512]{1,0:T(8,128)S(1)} %copy-done.1, bf16[512,512]{1,0:T(8,128)(2,1)S(1)} %get-tuple-element.39.qe_ref, bf16[4,512,1024]{2,1,0:T(8,128)(2,1)S(1)} %weigh.2.p_ref, bf16[640,512]{1,0:T(8,128)(2,1)S(1)} %collective-permute-done.6.vz_ref), custom_call_target="tpu_custom_call" | custom-call | flops 2000000000 | bytes 1000000 | tf_op jit(solution)/shard_map/gather/pallas_call | solution.py:359
  80.3 9.4 %collective-permute-done.5.vz_ref = bf16[640,512]{1,0:T(8,128)(2,1)S(1)} collective-permute-done((bf16[640,512]{1,0:T(8,128)(2,1)S(1)}, bf16[640,512]{1,0:T(8,128)(2,1)S(1)}, u32[]{:S(2)}, u32[]{:S(2)}) %collective-permute-start.5) | collective-permute-done | bytes 655392 | tf_op jit(solution)/shard_map/ppermute | solution.py:367
  89.7 2.9 %gather.3 = (bf16[512,1024]{1,0:T(8,128)(2,1)}, bf16[512,1024]{1,0:T(8,128)(2,1)}) custom-call(f32[512,512]{1,0:T(8,128)S(1)} %copy-done, bf16[512,512]{1,0:T(8,128)(2,1)S(1)} %get-tuple-element.32.qe_ref, bf16[4,512,1024]{2,1,0:T(8,128)(2,1)S(1)} %weigh.3.p_ref, ...), custom_call_target="tpu_custom_call", output_to_operand_aliasing={{0}: (4, {}), {1}: (5, {})} | custom-call | flops 2000000000 | bytes 1000000 | tf_op jit(solution)/shard_map/gather/pallas_call | solution.py:359
  (6 shorter events, 0.0 us)
Async XLA Ops:
  0.6 54.5 %collective-permute-start.2 = (bf16[512,1024]{1,0:T(8,128)(2,1)}, bf16[512,1024]{1,0:T(8,128)(2,1)S(1)}, u32[]{:S(2)}, u32[]{:S(2)}) collective-permute-start(bf16[512,1024]{1,0:T(8,128)(2,1)} %ko_ref.3), channel_id=1, source_target_pairs={{0,4},{4,8},{8,12},{1,5},{5,9},{9,13},{2,6},{6,10},{10,14},{3,7},{... | collective-permute-start | bytes 3145736 | tf_op jit(solution)/shard_map/ppermute | solution.py:367
  5.6 0.8 copy-start.4
  6.4 0.7 copy-start.5
  7.1 25.6 %copy-start.6 = (f32[512,8]{0,1:T(8,128)S(1)}, f32[512,8]{0,1:T(8,128)}, u32[]{:S(2)}) copy-start(f32[512,8]{0,1:T(8,128)} %param.11) | copy-start | bytes 49156
  26.4 28.7 %collective-permute-start = (bf16[4,128,256]{2,1,0:T(8,128)(2,1)S(1)}, bf16[4,128,256]{2,1,0:T(8,128)(2,1)S(1)}, u32[]{:S(2)}, u32[]{:S(2)}) collective-permute-start(bf16[4,128,256]{2,1,0:T(8,128)(2,1)S(1)} %get-tuple-element.24), channel_id=1, source_target_pairs={{0,4},{4,8},{1,5},{5,9},{2,6},{6,10},{3,7},{7,11},{16,20},{20,24},... | collective-permute-start | bytes 786440 | tf_op jit(solution)/shard_map/ppermute | solution.py:367
  29.9 25.5 %copy-start.1 = (f32[512,512]{1,0:T(8,128)S(1)}, f32[512,512]{1,0:T(8,128)}, u32[]{:S(2)}) copy-start(f32[512,512]{1,0:T(8,128)} %get-tuple-element.38.o_ref) | copy-start | bytes 3145732
  29.9 27.3 %copy-start.2 = (bf16[512,1024]{1,0:T(8,128)(2,1)S(1)}, bf16[512,1024]{1,0:T(8,128)(2,1)}, u32[]{:S(2)}) copy-start(bf16[512,1024]{1,0:T(8,128)(2,1)} %q_ref.7) | copy-start | bytes 3145732
  29.9 27.3 %copy-start.3 = (bf16[512,1024]{1,0:T(8,128)(2,1)S(1)}, bf16[512,1024]{1,0:T(8,128)(2,1)}, u32[]{:S(2)}) copy-start(bf16[512,1024]{1,0:T(8,128)(2,1)} %ko_ref.3) | copy-start | bytes 3145732
  29.9 25.2 %collective-permute-start.1 = (bf16[4,128,128]{2,1,0:T(8,128)(2,1)S(1)}, bf16[4,128,128]{2,1,0:T(8,128)(2,1)S(1)}, u32[]{:S(2)}, u32[]{:S(2)}) collective-permute-start(bf16[4,128,128]{2,1,0:T(8,128)(2,1)S(1)} %get-tuple-element.25), channel_id=1, source_target_pairs={{0,8},{1,9},{2,10},{3,11},{16,24},{17,25},{18,26},{19,27}} | collective-permute-start | bytes 393224 | tf_op jit(solution)/shard_map/ppermute | solution.py:367
  52.1 11.7 %collective-permute-start.3 = (bf16[4,128,256]{2,1,0:T(8,128)(2,1)S(1)}, bf16[4,128,256]{2,1,0:T(8,128)(2,1)S(1)}, u32[]{:S(2)}, u32[]{:S(2)}) collective-permute-start(bf16[4,128,256]{2,1,0:T(8,128)(2,1)S(1)} %get-tuple-element.29), channel_id=1, source_target_pairs={{0,4},{4,8},{1,5},{5,9},{2,6},{6,10},{3,7},{7,11},{16,20},{20,24},... | collective-permute-start | bytes 786440 | tf_op jit(solution)/shard_map/ppermute | solution.py:367
  53.8 10.0 %collective-permute-start.4 = (bf16[4,128,128]{2,1,0:T(8,128)(2,1)S(1)}, bf16[4,128,128]{2,1,0:T(8,128)(2,1)S(1)}, u32[]{:S(2)}, u32[]{:S(2)}) collective-permute-start(bf16[4,128,128]{2,1,0:T(8,128)(2,1)S(1)} %get-tuple-element.30), channel_id=1, source_target_pairs={{0,8},{1,9},{2,10},{3,11},{16,24},{17,25},{18,26},{19,27}} | collective-permute-start | bytes 393224 | tf_op jit(solution)/shard_map/ppermute | solution.py:367
  55.7 21.7 %collective-permute-start.6 = (bf16[640,512]{1,0:T(8,128)(2,1)S(1)}, bf16[640,512]{1,0:T(8,128)(2,1)S(1)}, u32[]{:S(2)}, u32[]{:S(2)}) collective-permute-start(bf16[640,512]{1,0:T(8,128)(2,1)S(1)} %leave.3), channel_id=1, source_target_pairs={{0,4},{4,8},{8,12},{1,5},{5,9},{9,13},{2,6},{6,10},{10,14},{3,7},{... | collective-permute-start | bytes 1966088 | tf_op jit(solution)/shard_map/ppermute | solution.py:367
  60.5 3.6 %copy-start = (f32[512,512]{1,0:T(8,128)S(1)}, f32[512,512]{1,0:T(8,128)}, u32[]{:S(2)}) copy-start(f32[512,512]{1,0:T(8,128)} %get-tuple-element.31.o_ref) | copy-start | bytes 3145732
  64.4 25.3 %collective-permute-start.5 = (bf16[640,512]{1,0:T(8,128)(2,1)S(1)}, bf16[640,512]{1,0:T(8,128)(2,1)S(1)}, u32[]{:S(2)}, u32[]{:S(2)}) collective-permute-start(bf16[640,512]{1,0:T(8,128)(2,1)S(1)} %leave.2), channel_id=1, source_target_pairs={{0,4},{4,8},{8,12},{1,5},{5,9},{9,13},{2,6},{6,10},{10,14},{3,7},{... | collective-permute-start | bytes 1966088 | tf_op jit(solution)/shard_map/ppermute | solution.py:367

commit v4 on v3

--- a/solution.py
+++ b/solution.py
@@ -174,42 +174,62 @@
     return pl.CostEstimate(flops=int(us * 10**9), bytes_accessed=10**6, transcendentals=0)
 
 
-def local_body(q_ref, k_ref, v_ref, b_ref, l_ref, o_ref, qe_ref, yo_ref, am_ref, a_ref, y_ref, r_ref, *, HB, NC, first):
+def levels_body(b_ref, l_ref, r_ref, *, T):
+    C = 2 * T
+    heads = l_ref.shape[0]
+
+    def pick(x, m):
+        a = x.astype(bf16)
+        r = dot(cat([a, *split(x - a.astype(f32))], 0), m.astype(bf16))
+        return r[:heads] + r[heads:2 * heads] + r[2 * heads:]
+
+    def full(x):
+        return x if heads == 8 else cat([x, jnp.zeros((8 - heads, C), f32)], 0)
+
+    ld, b0, b1 = l_ref[...], b_ref[0], b_ref[1]
+    t = lax.broadcasted_iota(jnp.int32, (l_ref.shape[1], C), 0)
+    i = lax.broadcasted_iota(jnp.int32, (l_ref.shape[1], C), 1)
+    for s in range(r_ref.shape[0]):
+        u = t - s * T
+        r_ref[s, 0:8] = full(pick(ld, (u >= 0) & (u <= i // 2)))
+        r_ref[s, 8:16] = full(pick(b0, 2 * u == i) + pick(b1, 2 * u + 1 == i))
+        r_ref[s, 16:24] = full(pick(ld, (u >= 0) & (u <= i)))
+
+
+def local_body(*refs, HB, NC, first, start, fresh, last):
+    refs = list(refs)
+    q_ref, k_ref, v_ref = refs[:3]
+    y_ref = refs.pop()
     c = pl.program_id(0)
     T = q_ref.shape[0] // NC
     C = 2 * T
     d = D
     H = range(HB)
-    heads = l_ref.shape[0]
+    if fresh:
+        o_ref, qe_ref, r_ref, *out = refs[5:]
+    else:
+        r_ref, *more = refs[3:]
+        if start:
+            o_ref, qe_ref, *out = more[3:]
+        else:
+            o_ref, qe_ref, *out = more
 
     @pl.when(c == 0)
     def _():
-        i = lax.broadcasted_iota(jnp.int32, (d, 2 * d), 0)
-        j = lax.broadcasted_iota(jnp.int32, (d, 2 * d), 1)
-        for h in H:
-            y_ref[h] = (j == i + d).astype(f32)
-
-        def pick(x, m):
-            a = x.astype(bf16)
-            r = dot(cat([a, *split(x - a.astype(f32))], 0), m.astype(bf16))
-            return r[:heads] + r[heads:2 * heads] + r[2 * heads:]
-
-        def full(x):
-            return x if heads == 8 else cat([x, jnp.zeros((8 - heads, C), f32)], 0)
-
-        ld, b0, b1 = l_ref[...], b_ref[0], b_ref[1]
-        t = lax.broadcasted_iota(jnp.int32, (l_ref.shape[1], C), 0)
-        i = lax.broadcasted_iota(jnp.int32, (l_ref.shape[1], C), 1)
-        for s in range(r_ref.shape[0]):
-            u = t - s * T
-            r_ref[s, 0:8] = full(pick(ld, (u >= 0) & (u <= i // 2)))
-            r_ref[s, 8:16] = full(pick(b0, 2 * u == i) + pick(b1, 2 * u + 1 == i))
-            r_ref[s, 16:24] = full(pick(ld, (u >= 0) & (u <= i)))
+        if fresh:
+            levels_body(refs[3], refs[4], r_ref, T=T)
+        if start:
+            y_ref[...] = more[0][...]
+        else:
+            i = lax.broadcasted_iota(jnp.int32, (d, 2 * d), 0)
+            j = lax.broadcasted_iota(jnp.int32, (d, 2 * d), 1)
+            for h in H:
+                y_ref[h] = (j == i + d).astype(f32)
 
     masks, eye = block_masks(C)
     kq, k, q, v, Lr, Lc, br, bc, Lq = ([] for _ in range(9))
     for s in range(NC):
-        rows = r_ref[c * NC + s]
+        rows = r_ref[start + c * NC + s]
         cols = jnp.transpose(cat([rows, jnp.zeros((C - 24, C), f32)], 0))
         ks = k_ref[s * T:(s + 1) * T].reshape(C, HB * d)
         vs = v_ref[s * T:(s + 1) * T].reshape(C, HB * d)
@@ -240,29 +260,41 @@
     @pl.when(c == pl.num_programs(0) - 1)
     def _():
         for h in H:
-            yo_ref[h] = Y[h]
-            am_ref[h] = Y[h].astype(bf16)
-            a_ref[h] = Y[h][:, :d].astype(bf16)
-
-
-def local(queries, keys, values, betas, decay, g, HB, NC, T=64):
+            out[0][h] = Y[h]
+            if last:
+                out[1][h] = Y[h].astype(bf16)
+                out[2][h] = Y[h][:, :d].astype(bf16)
+
+
+def local(queries, keys, values, small, g, HB, start, stop, held=(), T=64):
     n, w = queries.shape
-    heads = w // D
     wg = HB * D
+    NC = math.gcd(16 // HB, stop - start)
     B = NC * T
-    flat = pl.BlockSpec((B, wg), lambda c: (c, g))
-    pair = pl.BlockSpec((B, 2, wg), lambda c: (c, 0, g))
-    out = pl.BlockSpec((B, wg), lambda c: (c, 0))
+    at = start // NC
+    fresh, last = len(small) == 2, stop == n // T
+    flat = pl.BlockSpec((B, wg), lambda c: (at + c, g))
+    pair = pl.BlockSpec((B, 2, wg), lambda c: (at + c, 0, g))
+    out = pl.BlockSpec((B, wg), lambda c: (at + c, 0))
     whole = lambda *s: pl.BlockSpec(s, lambda c: (0,) * len(s))
-    return pl.pallas_call(
-        functools.partial(local_body, HB=HB, NC=NC, first=g * HB),
-        grid=(n // B,),
-        in_specs=[flat, pair, pair, whole(2, heads, n), whole(heads, n)],
-        out_specs=[out, out, whole(HB, D, 2 * D), whole(HB, D, 2 * D), whole(HB, D, D)],
-        out_shape=[jax.ShapeDtypeStruct((n, wg), f32), jax.ShapeDtypeStruct((n, wg), bf16), jax.ShapeDtypeStruct((HB, D, 2 * D), f32), jax.ShapeDtypeStruct((HB, D, 2 * D), bf16), jax.ShapeDtypeStruct((HB, D, D), bf16)],
-        scratch_shapes=[pltpu.VMEM((HB, D, 2 * D), f32), pltpu.VMEM((n // T, 24, 2 * T), f32)],
+    rows = (n // T, 24, 2 * T)
+    any_ = pl.BlockSpec(memory_space=pl.ANY)
+    outs = [(out, (n, wg), f32), (out, (n, wg), bf16)]
+    if fresh:
+        outs.append((whole(*rows), rows, f32))
+    outs.append((whole(HB, D, 2 * D), (HB, D, 2 * D), f32))
+    if last:
+        outs += [(whole(HB, D, 2 * D), (HB, D, 2 * D), bf16), (whole(HB, D, D), (HB, D, D), bf16)]
+    return pl.pallas_call(
+        functools.partial(local_body, HB=HB, NC=NC, first=g * HB, start=start, fresh=fresh, last=last),
+        grid=((stop - start) // NC,),
+        in_specs=[flat, pair, pair, *(whole(*x.shape) for x in small), *([whole(HB, D, 2 * D), any_, any_] if held else [])],
+        out_specs=[x[0] for x in outs],
+        out_shape=[jax.ShapeDtypeStruct(x[1], x[2]) for x in outs],
+        input_output_aliases={3 + len(small) + 1: 0, 3 + len(small) + 2: 1} if held else {},
+        scratch_shapes=[pltpu.VMEM((HB, D, 2 * D), f32)],
         cost_estimate=cost(HB * LOCAL), name="local", compiler_params=params(52),
-    )(queries, keys, values, betas, decay)
+    )(queries, keys, values, *small, *held)
 
 
 VMEM = pl.BlockSpec(memory_space=pltpu.VMEM)
@@ -339,7 +371,7 @@
         functools.partial(weigh_body, axis=axis, R=R, first=g * HB), grid=(HB,),
         in_specs=[flat, VMEM, flat], out_specs=pl.BlockSpec((1, n, 2 * n), lambda h: (h, 0, 0)),
         out_shape=jax.ShapeDtypeStruct((HB, n, 2 * n), bf16),
-        cost_estimate=cost(HB * 1.3), name="weigh", compiler_params=params(24))(q, kp, ko)
+        cost_estimate=cost(HB * 1), name="weigh", compiler_params=params(24))(q, kp, ko)
 
 
 def gather_body(o_ref, qe_ref, p_ref, vz_ref, *refs):
@@ -367,39 +399,41 @@
     return lax.ppermute(array, "ctx", pairs) if pairs else jnp.zeros_like(array)
 
 
-GROUPS = 2
-
-
 def per_device(queries, keys, values, betas, log_decay, attn_queries, attn_keys):
     n, w = queries.shape
-    HB = w // D // GROUPS
+    HB = w // D // 2
+    chunks = n // 64
     blocks = lax.axis_size("ctx")
     every = [(i, i + 1) for i in range(blocks - 1)]
-    G = range(GROUPS)
-    beta_rows = betas.transpose(1, 2, 0)
-    decay_rows = log_decay.transpose(1, 0)
     keys_behind = send(attn_keys, every)
-    parts, near, far, crossing = [], [], [], []
-    for g in G:
-        parts.append(local(queries, keys, values, beta_rows, decay_rows, g, HB, math.gcd(16 // HB, n // 64)))
-        am, a = parts[g][3:]
-        near.append(send(am, every[:2]))
-        far.append(send(a, [(0, 2)] if blocks > 2 else []))
-    for g in G:
-        if g < GROUPS - 1:
-            near[g], far[g], parts[-1], keys_behind = lax.optimization_barrier((near[g], far[g], parts[-1], keys_behind))
-        else:
-            weights = [weigh(attn_queries, keys_behind, attn_keys, h, HB) for h in G]
-            near[g], far[g], weights = lax.optimization_barrier((near[g], far[g], weights))
-        z = meet(near[g], far[g])
-        o, qe, y = parts[g][:3]
+
+    def pass_on(o, qe, y, near, far):
+        z = meet(near, far)
         for k in range(3, blocks - 1):
             z = z + send(hop(y, z), [(k - 1, k)])
-        crossing.append(send(leave(o, qe, y, z), every))
-    done = ()
-    for g in G:
-        done = gather(*parts[g][:2], weights[g], crossing[g], done, g, HB, w)
-    return tuple(done)
+        return leave(o, qe, y, z)
+
+    def round_one(am, a):
+        return send(am, every[:2]), send(a, [(0, 2)] if blocks > 2 else [])
+
+    small = (betas.transpose(1, 2, 0), log_decay.transpose(1, 0))
+    o0, qe0, rows, y0, am, a = local(queries, keys, values, small, 0, HB, 0, chunks)
+    near, far = round_one(am, a)
+    o1, qe1, y1 = local(queries, keys, values, (rows,), 1, HB, 0, chunks // 2)
+    near, far, y1 = lax.optimization_barrier((near, far, y1))
+    leaving = pass_on(o0, qe0, y0, near, far)
+    leaving, y1 = lax.optimization_barrier((leaving, y1))
+    crossing0 = send(leaving, every)
+    o1, qe1, y1, am, a = local(queries, keys, values, (rows,), 1, HB, chunks // 2, chunks, (y1, o1, qe1))
+    near, far = round_one(am, a)
+    keys_behind, y1 = lax.optimization_barrier((keys_behind, y1))
+    weights = [weigh(attn_queries, keys_behind, attn_keys, 0, HB)]
+    keys_behind, crossing0, weights = lax.optimization_barrier((keys_behind, crossing0, weights))
+    weights.append(weigh(attn_queries, keys_behind, attn_keys, 1, HB))
+    near, far, weights = lax.optimization_barrier((near, far, weights))
+    crossing1 = send(pass_on(o1, qe1, y1, near, far), every)
+    done = gather(o0, qe0, weights[0], crossing0, (), 0, HB, w)
+    return tuple(gather(o1, qe1, weights[1], crossing1, tuple(done), 1, HB, w))
 
 
 def solution(mesh):

time: 93 us -> 88.3 us (0.949)
  the two profiles are of different devices: /device:TPU:0 before, /device:TPU:16 now
where the time goes in v4:
time: 88.3 us; the launch traced here: 87.8 us
  Pallas kernels  53.7 us (61%)
  waiting for transfers between devices  18.2 us (21%)
  starting transfers between devices  12.9 us (15%)
  local copies, waits for them, and re-layouts  2.28 us (3%)
    pallas_call x3, Pallas kernels, local(): pl.pallas_call(functools.partial(local_body, HB=HB, NC=NC, first=g * HB,...  40.1 us
    ppermute x7, waiting for transfers between devices, send(): return lax.ppermute(array, 'ctx', pairs) if pairs else jnp.zeros_like(array)  18.2 us
    ppermute x7, starting transfers between devices, send(): return lax.ppermute(array, 'ctx', pairs) if pairs else jnp.zeros_like(array)  12.9 us
    pallas_call x2, Pallas kernels, weigh(): pl.pallas_call(functools.partial(weigh_body, axis=axis, R=R, first=g * HB...  6.66 us
    pallas_call x2, Pallas kernels, gather(): pl.pallas_call(gather_body, grid=(HB,), in_specs=[part, part, pl.BlockSpe...  5.85 us
    unnamed x14, local copies, waits for them, and re-layouts  2.28 us
  transfers between devices with their start and end apart: 7, of which 3 were waited for; matrix products, arithmetic and copies ran while one was open for 0% of the time, Pallas kernels for 57%

profile of v4, /device:TPU:16, one launch (start us, length us, event | category | flops | bytes accessed | tf_op | source)
XLA Modules:
  0.0 87.8 jit_solution(8408086804640551309)
XLA Ops:
  0.6 3.5 %collective-permute-start.4 = (bf16[512,1024]{1,0:T(8,128)(2,1)}, bf16[512,1024]{1,0:T(8,128)(2,1)S(1)}, u32[]{:S(2)}, u32[]{:S(2)}) collective-permute-start(bf16[512,1024]{1,0:T(8,128)(2,1)} %ko_ref.3), channel_id=1, source_target_pairs={{0,4},{4,8},{8,12},{1,5},{5,9},{9,13},{2,6},{6,10},{10,14},{3,7},{... | collective-permute-start | bytes 3145736 | tf_op jit(solution)/shard_map/ppermute | solution.py:399
  4.1 0.7 copy-done.4
  4.9 0.7 copy-done.5
  5.6 19.3 %local.3 = (f32[512,512]{1,0:T(8,128)}, bf16[512,512]{1,0:T(8,128)(2,1)S(1)}, f32[8,24,128]{2,1,0:T(8,128)S(1)}, f32[4,128,256]{2,1,0:T(8,128)S(1)}, bf16[4,128,...) custom-call(bf16[512,1024]{1,0:T(8,128)(2,1)} %refs_0_.5, bf16[512,2,1024]{2,1,0:T(2,128)(2,1)} %refs_1_.5, ...), custom_call_target="tpu_custom_call" | custom-call | flops 4000000000 | bytes 1000000 | tf_op jit(solution)/shard_map/local/pallas_call | solution.py:288
  24.9 1.3 %collective-permute-start = (bf16[4,128,256]{2,1,0:T(8,128)(2,1)S(1)}, bf16[4,128,256]{2,1,0:T(8,128)(2,1)S(1)}, u32[]{:S(2)}, u32[]{:S(2)}) collective-permute-start(bf16[4,128,256]{2,1,0:T(8,128)(2,1)S(1)} %get-tuple-element.36), channel_id=1, source_target_pairs={{0,4},{4,8},{1,5},{5,9},{2,6},{6,10},{3,7},{7,11},{16,20},{20,24},... | collective-permute-start | bytes 786440 | tf_op jit(solution)/shard_map/ppermute | solution.py:399
  26.2 1.5 %collective-permute-start.1 = (bf16[4,128,128]{2,1,0:T(8,128)(2,1)S(1)}, bf16[4,128,128]{2,1,0:T(8,128)(2,1)S(1)}, u32[]{:S(2)}, u32[]{:S(2)}) collective-permute-start(bf16[4,128,128]{2,1,0:T(8,128)(2,1)S(1)} %get-tuple-element.37), channel_id=1, source_target_pairs={{0,8},{1,9},{2,10},{3,11},{16,24},{17,25},{18,26},{19,27}} | collective-permute-start | bytes 393224 | tf_op jit(solution)/shard_map/ppermute | solution.py:399
  27.7 0.0 copy-start.1
  27.7 10.3 %local.4 = (f32[512,512]{1,0:T(8,128)}, bf16[512,512]{1,0:T(8,128)(2,1)S(1)}, f32[4,128,256]{2,1,0:T(8,128)S(1)}) custom-call(bf16[512,1024]{1,0:T(8,128)(2,1)} %refs_0_.5, bf16[512,2,1024]{2,1,0:T(2,128)(2,1)} %refs_1_.5, bf16[512,2,1024]{2,1,0:T(2,128)(2,1)} %refs_2_.5, f32[8,24,128]{2,1,0:T(8,128)S(1)} %get-tuple-element.32.refs_3_), custom_call_target="tpu_custom_call" | custom-call | flops 4000000000 | bytes 1000000 | tf_op jit(solution)/shard_map/local/pallas_call | solution.py:288
  38.0 0.8 copy-done.6
  38.8 0.0 collective-permute-done.1.a_ref
  38.8 0.0 collective-permute-done.am_ref
  38.8 0.2 meet.2.z_ref
  39.0 0.4 leave.2
  39.3 2.1 %collective-permute-start.5 = (bf16[640,512]{1,0:T(8,128)(2,1)S(1)}, bf16[640,512]{1,0:T(8,128)(2,1)S(1)}, u32[]{:S(2)}, u32[]{:S(2)}) collective-permute-start(bf16[640,512]{1,0:T(8,128)(2,1)S(1)} %leave.2), channel_id=1, source_target_pairs={{0,4},{4,8},{8,12},{1,5},{5,9},{9,13},{2,6},{6,10},{10,14},{3,7},{... | collective-permute-start | bytes 1966088 | tf_op jit(solution)/shard_map/ppermute | solution.py:399
  41.5 0.0 copy-start.2
  41.5 0.0 copy-start.3
  41.5 10.5 %local.5 = (f32[512,512]{1,0:T(8,128)}, bf16[512,512]{1,0:T(8,128)(2,1)S(1)}, f32[4,128,256]{2,1,0:T(8,128)S(1)}, bf16[4,128,256]{2,1,0:T(8,128)(2,1)S(1)}, bf16[4,128,128]{2,1,0:T(8,128)(2,1)S(1)}) custom-call(bf16[512,1024]{1,0:T(8,128)(2,1)} %refs_0_.5, bf16[512,2,1024]{2,1,0:T(2,128)(2,1)} %refs_1_.5, ...), custom_call_target="tpu_custom_call", output_to_operand_aliasing={{0}: (5, {}), {1}: (6, {})} | custom-call | flops 4000000000 | bytes 1000000 | tf_op jit(solution)/shard_map/local/pallas_call | solution.py:288
  52.0 1.3 %collective-permute-start.2 = (bf16[4,128,256]{2,1,0:T(8,128)(2,1)S(1)}, bf16[4,128,256]{2,1,0:T(8,128)(2,1)S(1)}, u32[]{:S(2)}, u32[]{:S(2)}) collective-permute-start(bf16[4,128,256]{2,1,0:T(8,128)(2,1)S(1)} %get-tuple-element.47), channel_id=1, source_target_pairs={{0,4},{4,8},{1,5},{5,9},{2,6},{6,10},{3,7},{7,11},{16,20},{20,24},... | collective-permute-start | bytes 786440 | tf_op jit(solution)/shard_map/ppermute | solution.py:399
  53.3 1.3 %collective-permute-start.3 = (bf16[4,128,128]{2,1,0:T(8,128)(2,1)S(1)}, bf16[4,128,128]{2,1,0:T(8,128)(2,1)S(1)}, u32[]{:S(2)}, u32[]{:S(2)}) collective-permute-start(bf16[4,128,128]{2,1,0:T(8,128)(2,1)S(1)} %get-tuple-element.48), channel_id=1, source_target_pairs={{0,8},{1,9},{2,10},{3,11},{16,24},{17,25},{18,26},{19,27}} | collective-permute-start | bytes 393224 | tf_op jit(solution)/shard_map/ppermute | solution.py:399
  54.6 0.0 collective-permute-done.4.kp_ref
  54.6 3.3 %weigh.2.p_ref = bf16[4,512,1024]{2,1,0:T(8,128)(2,1)S(1)} custom-call(bf16[512,1024]{1,0:T(8,128)(2,1)S(1)} %copy-done.2, bf16[512,1024]{1,0:T(8,128)(2,1)S(1)} %collective-permute-done.4.kp_ref, bf16[512,1024]{1,0:T(8,128)(2,1)S(1)} %copy-done.3), custom_call_target="tpu_custom_call" | custom-call | flops 4000000000 | bytes 1000000 | tf_op jit(solution)/shard_map/weigh/pallas_call | solution.py:370
  58.0 0.0 copy-start
  58.0 0.8 collective-permute-done.5.vz_ref
  58.7 3.3 %weigh.3.p_ref = bf16[4,512,1024]{2,1,0:T(8,128)(2,1)S(1)} custom-call(bf16[512,1024]{1,0:T(8,128)(2,1)S(1)} %copy-done.2, bf16[512,1024]{1,0:T(8,128)(2,1)S(1)} %collective-permute-done.4.kp_ref, bf16[512,1024]{1,0:T(8,128)(2,1)S(1)} %copy-done.3), custom_call_target="tpu_custom_call" | custom-call | flops 4000000000 | bytes 1000000 | tf_op jit(solution)/shard_map/weigh/pallas_call | solution.py:370
  62.1 4.9 %collective-permute-done.3.a_ref = bf16[4,128,128]{2,1,0:T(8,128)(2,1)S(1)} collective-permute-done((bf16[4,128,128]{2,1,0:T(8,128)(2,1)S(1)}, bf16[4,128,128]{2,1,0:T(8,128)(2,1)S(1)}, u32[]{:S(2)}, u32[]{:S(2)}) %collective-permute-start.3) | collective-permute-done | bytes 131104 | tf_op jit(solution)/shard_map/ppermute | solution.py:399
  67.0 0.0 collective-permute-done.2.am_ref
  67.0 0.2 meet.3.z_ref
  67.2 0.4 leave.3
  67.6 1.9 %collective-permute-start.6 = (bf16[640,512]{1,0:T(8,128)(2,1)S(1)}, bf16[640,512]{1,0:T(8,128)(2,1)S(1)}, u32[]{:S(2)}, u32[]{:S(2)}) collective-permute-start(bf16[640,512]{1,0:T(8,128)(2,1)S(1)} %leave.3), channel_id=1, source_target_pairs={{0,4},{4,8},{8,12},{1,5},{5,9},{9,13},{2,6},{6,10},{10,14},{3,7},{... | collective-permute-start | bytes 1966088 | tf_op jit(solution)/shard_map/ppermute | solution.py:399
  69.5 2.9 %gather.2 = (bf16[512,1024]{1,0:T(8,128)(2,1)}, bf16[512,1024]{1,0:T(8,128)(2,1)}) custom-call(f32[512,512]{1,0:T(8,128)S(1)} %copy-done.1, bf16[512,512]{1,0:T(8,128)(2,1)S(1)} %get-tuple-element.34.qe_ref, bf16[4,512,1024]{2,1,0:T(8,128)(2,1)S(1)} %weigh.2.p_ref, bf16[640,512]{1,0:T(8,128)(2,1)S(1)} %collective-permute-done.5.vz_ref), custom_call_target="tpu_custom_call" | custom-call | flops 2000000000 | bytes 1000000 | tf_op jit(solution)/shard_map/gather/pallas_call | solution.py:391
  72.4 12.5 %collective-permute-done.6.vz_ref = bf16[640,512]{1,0:T(8,128)(2,1)S(1)} collective-permute-done((bf16[640,512]{1,0:T(8,128)(2,1)S(1)}, bf16[640,512]{1,0:T(8,128)(2,1)S(1)}, u32[]{:S(2)}, u32[]{:S(2)}) %collective-permute-start.6) | collective-permute-done | bytes 655392 | tf_op jit(solution)/shard_map/ppermute | solution.py:399
  84.9 2.9 %gather.3 = (bf16[512,1024]{1,0:T(8,128)(2,1)}, bf16[512,1024]{1,0:T(8,128)(2,1)}) custom-call(f32[512,512]{1,0:T(8,128)S(1)} %copy-done, bf16[512,512]{1,0:T(8,128)(2,1)S(1)} %get-tuple-element.46.qe_ref, bf16[4,512,1024]{2,1,0:T(8,128)(2,1)S(1)} %weigh.3.p_ref, ...), custom_call_target="tpu_custom_call", output_to_operand_aliasing={{0}: (4, {}), {1}: (5, {})} | custom-call | flops 2000000000 | bytes 1000000 | tf_op jit(solution)/shard_map/gather/pallas_call | solution.py:391
  (7 shorter events, 0.0 us)
Async XLA Ops:
  0.6 54.0 %collective-permute-start.4 = (bf16[512,1024]{1,0:T(8,128)(2,1)}, bf16[512,1024]{1,0:T(8,128)(2,1)S(1)}, u32[]{:S(2)}, u32[]{:S(2)}) collective-permute-start(bf16[512,1024]{1,0:T(8,128)(2,1)} %ko_ref.3), channel_id=1, source_target_pairs={{0,4},{4,8},{8,12},{1,5},{5,9},{9,13},{2,6},{6,10},{10,14},{3,7},{... | collective-permute-start | bytes 3145736 | tf_op jit(solution)/shard_map/ppermute | solution.py:399
  4.1 0.8 copy-start.4
  4.9 0.7 copy-start.5
  24.9 13.9 %collective-permute-start = (bf16[4,128,256]{2,1,0:T(8,128)(2,1)S(1)}, bf16[4,128,256]{2,1,0:T(8,128)(2,1)S(1)}, u32[]{:S(2)}, u32[]{:S(2)}) collective-permute-start(bf16[4,128,256]{2,1,0:T(8,128)(2,1)S(1)} %get-tuple-element.36), channel_id=1, source_target_pairs={{0,4},{4,8},{1,5},{5,9},{2,6},{6,10},{3,7},{7,11},{16,20},{20,24},... | collective-permute-start | bytes 786440 | tf_op jit(solution)/shard_map/ppermute | solution.py:399
  26.2 12.6 %collective-permute-start.1 = (bf16[4,128,128]{2,1,0:T(8,128)(2,1)S(1)}, bf16[4,128,128]{2,1,0:T(8,128)(2,1)S(1)}, u32[]{:S(2)}, u32[]{:S(2)}) collective-permute-start(bf16[4,128,128]{2,1,0:T(8,128)(2,1)S(1)} %get-tuple-element.37), channel_id=1, source_target_pairs={{0,8},{1,9},{2,10},{3,11},{16,24},{17,25},{18,26},{19,27}} | collective-permute-start | bytes 393224 | tf_op jit(solution)/shard_map/ppermute | solution.py:399
  27.7 11.3 %copy-start.1 = (f32[512,512]{1,0:T(8,128)S(1)}, f32[512,512]{1,0:T(8,128)}, u32[]{:S(2)}) copy-start(f32[512,512]{1,0:T(8,128)} %get-tuple-element.33.o_ref) | copy-start | bytes 3145732
  38.0 0.8 copy-start.6
  39.3 19.4 %collective-permute-start.5 = (bf16[640,512]{1,0:T(8,128)(2,1)S(1)}, bf16[640,512]{1,0:T(8,128)(2,1)S(1)}, u32[]{:S(2)}, u32[]{:S(2)}) collective-permute-start(bf16[640,512]{1,0:T(8,128)(2,1)S(1)} %leave.2), channel_id=1, source_target_pairs={{0,4},{4,8},{8,12},{1,5},{5,9},{9,13},{2,6},{6,10},{10,14},{3,7},{... | collective-permute-start | bytes 1966088 | tf_op jit(solution)/shard_map/ppermute | solution.py:399
  41.5 13.1 %copy-start.2 = (bf16[512,1024]{1,0:T(8,128)(2,1)S(1)}, bf16[512,1024]{1,0:T(8,128)(2,1)}, u32[]{:S(2)}) copy-start(bf16[512,1024]{1,0:T(8,128)(2,1)} %q_ref.3) | copy-start | bytes 3145732
  41.5 13.1 %copy-start.3 = (bf16[512,1024]{1,0:T(8,128)(2,1)S(1)}, bf16[512,1024]{1,0:T(8,128)(2,1)}, u32[]{:S(2)}) copy-start(bf16[512,1024]{1,0:T(8,128)(2,1)} %ko_ref.3) | copy-start | bytes 3145732
  52.0 15.0 %collective-permute-start.2 = (bf16[4,128,256]{2,1,0:T(8,128)(2,1)S(1)}, bf16[4,128,256]{2,1,0:T(8,128)(2,1)S(1)}, u32[]{:S(2)}, u32[]{:S(2)}) collective-permute-start(bf16[4,128,256]{2,1,0:T(8,128)(2,1)S(1)} %get-tuple-element.47), channel_id=1, source_target_pairs={{0,4},{4,8},{1,5},{5,9},{2,6},{6,10},{3,7},{7,11},{16,20},{20,24},... | collective-permute-start | bytes 786440 | tf_op jit(solution)/shard_map/ppermute | solution.py:399
  53.3 13.7 %collective-permute-start.3 = (bf16[4,128,128]{2,1,0:T(8,128)(2,1)S(1)}, bf16[4,128,128]{2,1,0:T(8,128)(2,1)S(1)}, u32[]{:S(2)}, u32[]{:S(2)}) collective-permute-start(bf16[4,128,128]{2,1,0:T(8,128)(2,1)S(1)} %get-tuple-element.48), channel_id=1, source_target_pairs={{0,8},{1,9},{2,10},{3,11},{16,24},{17,25},{18,26},{19,27}} | collective-permute-start | bytes 393224 | tf_op jit(solution)/shard_map/ppermute | solution.py:399
  58.0 9.3 %copy-start = (f32[512,512]{1,0:T(8,128)S(1)}, f32[512,512]{1,0:T(8,128)}, u32[]{:S(2)}) copy-start(f32[512,512]{1,0:T(8,128)} %get-tuple-element.45.o_ref) | copy-start | bytes 3145732
  67.6 17.3 %collective-permute-start.6 = (bf16[640,512]{1,0:T(8,128)(2,1)S(1)}, bf16[640,512]{1,0:T(8,128)(2,1)S(1)}, u32[]{:S(2)}, u32[]{:S(2)}) collective-permute-start(bf16[640,512]{1,0:T(8,128)(2,1)S(1)} %leave.3), channel_id=1, source_target_pairs={{0,4},{4,8},{8,12},{1,5},{5,9},{9,13},{2,6},{6,10},{10,14},{3,7},{... | collective-permute-start | bytes 1966088 | tf_op jit(solution)/shard_map/ppermute | solution.py:399

commit v5 on v4

--- a/solution.py
+++ b/solution.py
@@ -98,18 +98,35 @@
     As = [split(a) for a in A]
     X = base_inverses(A)
     Xs = [split(x) for x in X]
+    yield
     s = BASE
     while s < C:
         m = odd(masks[s], s)
         B = [split(product((odd(a[0], s) * m, odd(a[1], s) * m), x)) for a, x in zip(As, Xs)]
         B = [(weave(None, b[0], s), weave(None, b[1], s)) for b in B]
+        yield
         Xo = [odd(x, s) - product((odd(xs[0], s), odd(xs[1], s)), b) for x, xs, b in zip(X, Xs, B)]
         X = [weave(x, o, s) for x, o in zip(X, Xo)]
         if 2 * s < C:
             So = [split(o) for o in Xo]
             Xs = [(weave(x[0], o[0], s), weave(x[1], o[1], s)) for x, o in zip(Xs, So)]
+        yield
         s *= 2
     return X
+
+
+def staggered(runs, lag):
+    done = [None] * len(runs)
+    t = 0
+    while any(d is None for d in done):
+        for i, run in enumerate(runs):
+            if done[i] is None and t >= i * lag:
+                try:
+                    next(run)
+                except StopIteration as stop:
+                    done[i] = stop.value
+        t += 1
+    return done
 
 
 def two(parts):
@@ -130,6 +147,7 @@
         a, b = k[2 * p], k[2 * p + 1]
         r = dot_nt(both, cat([cat([a, nil], 1), cat([nil, b], 1)], 0))
         G += [r[:, :C], r[:, C:]]
+    yield
     Gd = [G[h][:C] * eye for h in H]
     nr = [lax.rsqrt(jnp.sum(Gd[h], axis=0, keepdims=True) + 1e-6) for h in H]
     nc = [lax.rsqrt(jnp.sum(Gd[h], axis=1, keepdims=True) + 1e-6) for h in H]
@@ -137,16 +155,19 @@
     lev = [cat([Lc[h], Lq[h]], 0) for h in H]
     rs = [cat([bc[h] * nc[h] * nc[h], qn[h]], 0) for h in H]
     M = [jnp.where(visible, jnp.exp(jnp.minimum(lev[h] - Lr[h], 0.0)) * G[h] * rs[h], 0.0) for h in H]
-    X = inverses([M[h][:C] for h in H], masks, eye)
+    yield
+    X = yield from inverses([M[h][:C] for h in H], masks, eye)
     bn = [br[h] * nr[h] for h in H]
     W = [dot(cat(split(X[h] * bn[h]), 1), cat([v[h], v[h]], 0)) for h in H]
     U = [dot(cat(split(X[h] * (bn[h] * nr[h] * jnp.exp(Lr[h]))), 1), cat([k[h], k[h]], 0)) for h in H]
+    yield
     last = [Lr[h][:, C - 1:C] for h in H]
     kt = [split(jnp.transpose(k[h].astype(f32)) * jnp.exp(last[h] - Lr[h])) for h in H]
     ws = [split(M[h][C:]) for h in H]
     right = [split(cat([U[h], W[h]], 1)) for h in H]
     R = [dot(two([kt[h][0], ws[h][0], kt[h][1], ws[h][1]]), cat(right[h], 0)) for h in H]
     R = [r[:d + T] + r[d + T:] for r in R]
+    yield
     left = [split(cat([R[h][:d, :d], (qn[h] * jnp.exp(Lq[h])) * q[h].astype(f32) - R[h][d:, :d]], 0)) for h in H]
     return left, [R[h][:, d:] for h in H], [jnp.exp(last[h]) for h in H]
 
@@ -164,6 +185,9 @@
 
 D = 128
 LOCAL = 1
+LIMIT = 40
+BATCH = 8
+LAG = 2
 
 
 def params(mib):
@@ -174,9 +198,9 @@
     return pl.CostEstimate(flops=int(us * 10**9), bytes_accessed=10**6, transcendentals=0)
 
 
-def levels_body(b_ref, l_ref, r_ref, *, T):
+def levels_body(x_ref, r_ref, *, T):
     C = 2 * T
-    heads = l_ref.shape[0]
+    heads = x_ref.shape[0] // 3
 
     def pick(x, m):
         a = x.astype(bf16)
@@ -186,9 +210,9 @@
     def full(x):
         return x if heads == 8 else cat([x, jnp.zeros((8 - heads, C), f32)], 0)
 
-    ld, b0, b1 = l_ref[...], b_ref[0], b_ref[1]
-    t = lax.broadcasted_iota(jnp.int32, (l_ref.shape[1], C), 0)
-    i = lax.broadcasted_iota(jnp.int32, (l_ref.shape[1], C), 1)
+    b0, b1, ld = (x_ref[r * heads:(r + 1) * heads] for r in range(3))
+    t = lax.broadcasted_iota(jnp.int32, (x_ref.shape[1], C), 0)
+    i = lax.broadcasted_iota(jnp.int32, (x_ref.shape[1], C), 1)
     for s in range(r_ref.shape[0]):
         u = t - s * T
         r_ref[s, 0:8] = full(pick(ld, (u >= 0) & (u <= i // 2)))
@@ -206,7 +230,7 @@
     d = D
     H = range(HB)
     if fresh:
-        o_ref, qe_ref, r_ref, *out = refs[5:]
+        o_ref, qe_ref, r_ref, *out = refs[4:]
     else:
         r_ref, *more = refs[3:]
         if start:
@@ -217,7 +241,7 @@
     @pl.when(c == 0)
     def _():
         if fresh:
-            levels_body(refs[3], refs[4], r_ref, T=T)
+            levels_body(refs[3], r_ref, T=T)
         if start:
             y_ref[...] = more[0][...]
         else:
@@ -246,7 +270,11 @@
             Lc.append(cols[:, at:at + 1])
             bc.append(cols[:, 8 + at:9 + at])
             Lq.append(cols[:T, 16 + at:17 + at])
-    left, add, decay = factors(kq, k, q, v, Lr, Lc, br, bc, Lq, masks, eye)
+    runs = []
+    for at in range(0, len(k), BATCH):
+        now = slice(at, at + BATCH)
+        runs.append(factors(kq[at // 2:(at + BATCH) // 2], *(x[now] for x in (k, q, v, Lr, Lc, br, bc, Lq)), masks, eye))
+    left, add, decay = (sum(x, []) for x in zip(*staggered(runs, LAG)))
     Y = [y_ref[h] for h in H]
     for s in range(NC):
         now = slice(s * HB, (s + 1) * HB)
@@ -272,7 +300,7 @@
     NC = math.gcd(16 // HB, stop - start)
     B = NC * T
     at = start // NC
-    fresh, last = len(small) == 2, stop == n // T
+    fresh, last = small.ndim == 2, stop == n // T
     flat = pl.BlockSpec((B, wg), lambda c: (at + c, g))
     pair = pl.BlockSpec((B, 2, wg), lambda c: (at + c, 0, g))
     out = pl.BlockSpec((B, wg), lambda c: (at + c, 0))
@@ -288,13 +316,13 @@
     return pl.pallas_call(
         functools.partial(local_body, HB=HB, NC=NC, first=g * HB, start=start, fresh=fresh, last=last),
         grid=((stop - start) // NC,),
-        in_specs=[flat, pair, pair, *(whole(*x.shape) for x in small), *([whole(HB, D, 2 * D), any_, any_] if held else [])],
+        in_specs=[flat, pair, pair, whole(*small.shape), *([whole(HB, D, 2 * D), any_, any_] if held else [])],
         out_specs=[x[0] for x in outs],
         out_shape=[jax.ShapeDtypeStruct(x[1], x[2]) for x in outs],
-        input_output_aliases={3 + len(small) + 1: 0, 3 + len(small) + 2: 1} if held else {},
+        input_output_aliases={5: 0, 6: 1} if held else {},
         scratch_shapes=[pltpu.VMEM((HB, D, 2 * D), f32)],
-        cost_estimate=cost(HB * LOCAL), name="local", compiler_params=params(52),
-    )(queries, keys, values, *small, *held)
+        cost_estimate=cost(HB * LOCAL), name="local", compiler_params=params(LIMIT),
+    )(queries, keys, values, small, *held)
 
 
 VMEM = pl.BlockSpec(memory_space=pltpu.VMEM)
@@ -371,7 +399,7 @@
         functools.partial(weigh_body, axis=axis, R=R, first=g * HB), grid=(HB,),
         in_specs=[flat, VMEM, flat], out_specs=pl.BlockSpec((1, n, 2 * n), lambda h: (h, 0, 0)),
         out_shape=jax.ShapeDtypeStruct((HB, n, 2 * n), bf16),
-        cost_estimate=cost(HB * 1), name="weigh", compiler_params=params(24))(q, kp, ko)
+        cost_estimate=cost(HB * 1.3), name="weigh", compiler_params=params(24))(q, kp, ko)
 
 
 def gather_body(o_ref, qe_ref, p_ref, vz_ref, *refs):
@@ -380,7 +408,7 @@
     vz = vz_ref[:, pl.ds(pl.multiple_of(pl.program_id(0) * D, D), D)]
     ret = (o_ref[...] + dot(qe_ref[...], vz[n:])).astype(bf16)
     ret_ref[...] = ret
-    out_ref[...] = dot(p_ref[0], cat([vz[:n], ret], 0)).astype(bf16)
+    out_ref[...] = dot(p_ref[pl.program_id(0)], cat([vz[:n], ret], 0)).astype(bf16)
 
 
 def gather(o, qe, p, vz, carry, g, HB, w):
@@ -389,7 +417,7 @@
     flat = pl.BlockSpec((n, D), lambda h: (0, g * HB + h))
     held = [pl.BlockSpec(memory_space=pl.ANY)] * len(carry)
     return pl.pallas_call(
-        gather_body, grid=(HB,), in_specs=[part, part, pl.BlockSpec((1, n, 2 * n), lambda h: (h, 0, 0)), VMEM] + held,
+        gather_body, grid=(HB,), in_specs=[part, part, VMEM, VMEM] + held,
         out_specs=[flat, flat], out_shape=[jax.ShapeDtypeStruct((n, w), bf16)] * 2,
         input_output_aliases={4 + i: i for i in range(len(carry))},
         cost_estimate=cost(HB * 0.5), name="gather", compiler_params=params(24))(o, qe, p, vz, *carry)
@@ -414,17 +442,18 @@
         return leave(o, qe, y, z)
 
     def round_one(am, a):
-        return send(am, every[:2]), send(a, [(0, 2)] if blocks > 2 else [])
-
-    small = (betas.transpose(1, 2, 0), log_decay.transpose(1, 0))
+        far = send(a, [(0, 2)] if blocks > 2 else [])
+        return send(am, every[:2]), far
+
+    small = cat([betas[:, 0], betas[:, 1], log_decay], 1).transpose(1, 0)
     o0, qe0, rows, y0, am, a = local(queries, keys, values, small, 0, HB, 0, chunks)
     near, far = round_one(am, a)
-    o1, qe1, y1 = local(queries, keys, values, (rows,), 1, HB, 0, chunks // 2)
+    o1, qe1, y1 = local(queries, keys, values, rows, 1, HB, 0, chunks // 2)
     near, far, y1 = lax.optimization_barrier((near, far, y1))
     leaving = pass_on(o0, qe0, y0, near, far)
     leaving, y1 = lax.optimization_barrier((leaving, y1))
     crossing0 = send(leaving, every)
-    o1, qe1, y1, am, a = local(queries, keys, values, (rows,), 1, HB, chunks // 2, chunks, (y1, o1, qe1))
+    o1, qe1, y1, am, a = local(queries, keys, values, rows, 1, HB, chunks // 2, chunks, (y1, o1, qe1))
     near, far = round_one(am, a)
     keys_behind, y1 = lax.optimization_barrier((keys_behind, y1))
     weights = [weigh(attn_queries, keys_behind, attn_keys, 0, HB)]

time: 88.3 us -> 86.5 us (0.980)
  Pallas kernels: 53.7 us -> 46.2 us
  local copies, waits for them, and re-layouts: 2.28 us -> 5.16 us
  waiting for transfers between devices: 18.2 us -> 20.1 us
    pallas_call x3, Pallas kernels: 40.1 us -> 32.7 us  [local(): pl.pallas_call(functools.partial(local_body, HB=HB, NC=NC, first=g * HB,...]
    unnamed x14 -> x10, local copies, waits for them, and re-layouts: 2.28 us -> 4.42 us
    ppermute x7, waiting for transfers between devices: 18.2 us -> 20.1 us  [send(): return lax.ppermute(array, 'ctx', pairs) if pairs else jnp.zeros_like(array)]
  transfers between devices with their start and end apart: 7 -> 7, of which waited for: 3 -> 4; matrix products, arithmetic and copies ran while one was open for 0% -> 2% of each run, Pallas kernels for 57% -> 50%
where the time goes in v5:
time: 86.5 us; the launch traced here: 85.9 us
  Pallas kernels  46.2 us (53%)
  waiting for transfers between devices  20.1 us (23%)
  starting transfers between devices  12.9 us (15%)
  local copies, waits for them, and re-layouts  5.16 us (6%)
    pallas_call x3, Pallas kernels, local(): pl.pallas_call(functools.partial(local_body, HB=HB, NC=NC, first=g * HB,...  32.7 us
    ppermute x7, waiting for transfers between devices, send(): return lax.ppermute(array, 'ctx', pairs) if pairs else jnp.zeros_like(array)  20.1 us
    ppermute x7, starting transfers between devices, send(): return lax.ppermute(array, 'ctx', pairs) if pairs else jnp.zeros_like(array)  12.9 us
    pallas_call x2, Pallas kernels, weigh(): pl.pallas_call(functools.partial(weigh_body, axis=axis, R=R, first=g * HB...  6.66 us
    pallas_call x2, Pallas kernels, gather(): pl.pallas_call(gather_body, grid=(HB,), in_specs=[part, part, VMEM, VMEM]...  5.84 us
    unnamed x10, local copies, waits for them, and re-layouts  4.42 us
  transfers between devices with their start and end apart: 7, of which 4 were waited for; matrix products, arithmetic and copies ran while one was open for 2% of the time, Pallas kernels for 50%

profile of v5, /device:TPU:16, one launch (start us, length us, event | category | flops | bytes accessed | tf_op | source)
XLA Modules:
  0.0 85.9 jit_solution(6003579215609181721)
XLA Ops:
  0.6 3.5 %collective-permute-start.4 = (bf16[512,1024]{1,0:T(8,128)(2,1)}, bf16[512,1024]{1,0:T(8,128)(2,1)S(1)}, u32[]{:S(2)}, u32[]{:S(2)}) collective-permute-start(bf16[512,1024]{1,0:T(8,128)(2,1)} %ko_ref.3), channel_id=1, source_target_pairs={{0,4},{4,8},{8,12},{1,5},{5,9},{9,13},{2,6},{6,10},{10,14},{3,7},{... | collective-permute-start | bytes 3145736 | tf_op jit(solution)/shard_map/ppermute | solution.py:427
  4.1 0.7 slice_bitcast_fusion.1
  4.9 0.7 maximum_bitcast_fusion.refs_3_
  5.6 1.6 %copy-done = bf16[512,2,1024]{2,1,0:T(2,128)(2,1)S(1)} copy-done((bf16[512,2,1024]{2,1,0:T(2,128)(2,1)S(1)}, bf16[512,2,1024]{2,1,0:T(2,128)(2,1)}, u32[]{:S(2)}) %copy-start) | copy-done | bytes 2097176
  7.2 1.6 %copy-done.1 = bf16[512,2,1024]{2,1,0:T(2,128)(2,1)S(1)} copy-done((bf16[512,2,1024]{2,1,0:T(2,128)(2,1)S(1)}, bf16[512,2,1024]{2,1,0:T(2,128)(2,1)}, u32[]{:S(2)}) %copy-start.1) | copy-done | bytes 2097176
  8.8 1.2 %copy-done.2 = bf16[512,1024]{1,0:T(8,128)(2,1)S(1)} copy-done((bf16[512,1024]{1,0:T(8,128)(2,1)S(1)}, bf16[512,1024]{1,0:T(8,128)(2,1)}, u32[]{:S(2)}) %copy-start.2) | copy-done | bytes 1048600
  10.0 17.0 %local.3 = (f32[512,512]{1,0:T(8,128)S(1)}, bf16[512,512]{1,0:T(8,128)(2,1)S(1)}, f32[8,24,128]{2,1,0:T(8,128)S(1)}, f32[4,128,256]{2,1,0:T(8,128)S(1)}, bf16[4,...) custom-call(bf16[512,1024]{1,0:T(8,128)(2,1)S(1)} %copy-done.2, bf16[512,2,1024]{2,1,0:T(2,128)(2,1)S(1)} %copy-done, ...), custom_call_target="tpu_custom_call" | custom-call | flops 4000000000 | bytes 1000000 | tf_op jit(solution)/shard_map/local/pallas_call | solution.py:316
  27.0 1.3 %collective-permute-start = (bf16[4,128,256]{2,1,0:T(8,128)(2,1)S(1)}, bf16[4,128,256]{2,1,0:T(8,128)(2,1)S(1)}, u32[]{:S(2)}, u32[]{:S(2)}) collective-permute-start(bf16[4,128,256]{2,1,0:T(8,128)(2,1)S(1)} %get-tuple-element.36), channel_id=1, source_target_pairs={{0,4},{4,8},{1,5},{5,9},{2,6},{6,10},{3,7},{7,11},{16,20},{20,24},... | collective-permute-start | bytes 786440 | tf_op jit(solution)/shard_map/ppermute | solution.py:427
  28.3 1.5 %collective-permute-start.1 = (bf16[4,128,128]{2,1,0:T(8,128)(2,1)S(1)}, bf16[4,128,128]{2,1,0:T(8,128)(2,1)S(1)}, u32[]{:S(2)}, u32[]{:S(2)}) collective-permute-start(bf16[4,128,128]{2,1,0:T(8,128)(2,1)S(1)} %get-tuple-element.37), channel_id=1, source_target_pairs={{0,8},{1,9},{2,10},{3,11},{16,24},{17,25},{18,26},{19,27}} | collective-permute-start | bytes 393224 | tf_op jit(solution)/shard_map/ppermute | solution.py:427
  29.8 7.8 %local.4 = (f32[512,512]{1,0:T(8,128)S(1)}, bf16[512,512]{1,0:T(8,128)(2,1)S(1)}, f32[4,128,256]{2,1,0:T(8,128)S(1)}) custom-call(bf16[512,1024]{1,0:T(8,128)(2,1)S(1)} %copy-done.2, bf16[512,2,1024]{2,1,0:T(2,128)(2,1)S(1)} %copy-done, bf16[512,2,1024]{2,1,0:T(2,128)(2,1)S(1)} %copy-done.1, f32[8,24,128]{2,1,0:T(8,128)S(1)} %get-tuple-element.32.refs_3_), custom_call_target="tpu_custom_call" | custom-call | flops 4000000000 | bytes 1000000 | tf_op jit(solution)/shard_map/local/pallas_call | solution.py:316
  37.6 1.9 %collective-permute-done.1.a_ref = bf16[4,128,128]{2,1,0:T(8,128)(2,1)S(1)} collective-permute-done((bf16[4,128,128]{2,1,0:T(8,128)(2,1)S(1)}, bf16[4,128,128]{2,1,0:T(8,128)(2,1)S(1)}, u32[]{:S(2)}, u32[]{:S(2)}) %collective-permute-start.1) | collective-permute-done | bytes 131104 | tf_op jit(solution)/shard_map/ppermute | solution.py:427
  39.4 0.0 collective-permute-done.am_ref
  39.5 0.2 meet.2.z_ref
  39.6 0.4 leave.2
  40.0 2.1 %collective-permute-start.5 = (bf16[640,512]{1,0:T(8,128)(2,1)S(1)}, bf16[640,512]{1,0:T(8,128)(2,1)S(1)}, u32[]{:S(2)}, u32[]{:S(2)}) collective-permute-start(bf16[640,512]{1,0:T(8,128)(2,1)S(1)} %leave.2), channel_id=1, source_target_pairs={{0,4},{4,8},{8,12},{1,5},{5,9},{9,13},{2,6},{6,10},{10,14},{3,7},{... | collective-permute-start | bytes 1966088 | tf_op jit(solution)/shard_map/ppermute | solution.py:427
  42.1 0.0 copy-start.3
  42.2 0.0 copy-start.4
  42.2 7.9 %local.5 = (f32[512,512]{1,0:T(8,128)S(1)}, bf16[512,512]{1,0:T(8,128)(2,1)S(1)}, f32[4,128,256]{2,1,0:T(8,128)S(1)}, bf16[4,128,256]{2,1,0:T(8,128)(2,1)S(1)}, bf16[4,128,128]{2,1,0:T(8,128)(2,1)S(1)}) custom-call(bf16[512,1024]{1,0:T(8,128)(2,1)S(1)} %copy-done.2, bf16[512,2,1024]{2,1,0:T(2,128)(2,1)S(1)} %copy-done, ...), custom_call_target="tpu_custom_call", output_to_operand_aliasing={{0}: (5, {}), {1}: (6, {})} | custom-call | flops 4000000000 | bytes 1000000 | tf_op jit(solution)/shard_map/local/pallas_call | solution.py:316
  50.0 1.3 %collective-permute-start.2 = (bf16[4,128,256]{2,1,0:T(8,128)(2,1)S(1)}, bf16[4,128,256]{2,1,0:T(8,128)(2,1)S(1)}, u32[]{:S(2)}, u32[]{:S(2)}) collective-permute-start(bf16[4,128,256]{2,1,0:T(8,128)(2,1)S(1)} %get-tuple-element.47), channel_id=1, source_target_pairs={{0,4},{4,8},{1,5},{5,9},{2,6},{6,10},{3,7},{7,11},{16,20},{20,24},... | collective-permute-start | bytes 786440 | tf_op jit(solution)/shard_map/ppermute | solution.py:427
  51.3 1.3 %collective-permute-start.3 = (bf16[4,128,128]{2,1,0:T(8,128)(2,1)S(1)}, bf16[4,128,128]{2,1,0:T(8,128)(2,1)S(1)}, u32[]{:S(2)}, u32[]{:S(2)}) collective-permute-start(bf16[4,128,128]{2,1,0:T(8,128)(2,1)S(1)} %get-tuple-element.48), channel_id=1, source_target_pairs={{0,8},{1,9},{2,10},{3,11},{16,24},{17,25},{18,26},{19,27}} | collective-permute-start | bytes 393224 | tf_op jit(solution)/shard_map/ppermute | solution.py:427
  52.6 0.0 collective-permute-done.4.kp_ref
  52.7 3.3 %weigh.2.p_ref = bf16[4,512,1024]{2,1,0:T(8,128)(2,1)S(1)} custom-call(bf16[512,1024]{1,0:T(8,128)(2,1)S(1)} %copy-done.3, bf16[512,1024]{1,0:T(8,128)(2,1)S(1)} %collective-permute-done.4.kp_ref, bf16[512,1024]{1,0:T(8,128)(2,1)S(1)} %copy-done.4), custom_call_target="tpu_custom_call" | custom-call | flops 5200000000 | bytes 1000000 | tf_op jit(solution)/shard_map/weigh/pallas_call | solution.py:398
  56.0 3.6 %collective-permute-done.5.vz_ref = bf16[640,512]{1,0:T(8,128)(2,1)S(1)} collective-permute-done((bf16[640,512]{1,0:T(8,128)(2,1)S(1)}, bf16[640,512]{1,0:T(8,128)(2,1)S(1)}, u32[]{:S(2)}, u32[]{:S(2)}) %collective-permute-start.5) | collective-permute-done | bytes 655392 | tf_op jit(solution)/shard_map/ppermute | solution.py:427
  59.6 3.3 %weigh.3.p_ref = bf16[4,512,1024]{2,1,0:T(8,128)(2,1)S(1)} custom-call(bf16[512,1024]{1,0:T(8,128)(2,1)S(1)} %copy-done.3, bf16[512,1024]{1,0:T(8,128)(2,1)S(1)} %collective-permute-done.4.kp_ref, bf16[512,1024]{1,0:T(8,128)(2,1)S(1)} %copy-done.4), custom_call_target="tpu_custom_call" | custom-call | flops 5200000000 | bytes 1000000 | tf_op jit(solution)/shard_map/weigh/pallas_call | solution.py:398
  62.9 3.0 %collective-permute-done.3.a_ref = bf16[4,128,128]{2,1,0:T(8,128)(2,1)S(1)} collective-permute-done((bf16[4,128,128]{2,1,0:T(8,128)(2,1)S(1)}, bf16[4,128,128]{2,1,0:T(8,128)(2,1)S(1)}, u32[]{:S(2)}, u32[]{:S(2)}) %collective-permute-start.3) | collective-permute-done | bytes 131104 | tf_op jit(solution)/shard_map/ppermute | solution.py:427
  65.8 0.0 collective-permute-done.2.am_ref
  65.8 0.2 meet.3.z_ref
  66.0 0.4 leave.3
  66.4 1.9 %collective-permute-start.6 = (bf16[640,512]{1,0:T(8,128)(2,1)S(1)}, bf16[640,512]{1,0:T(8,128)(2,1)S(1)}, u32[]{:S(2)}, u32[]{:S(2)}) collective-permute-start(bf16[640,512]{1,0:T(8,128)(2,1)S(1)} %leave.3), channel_id=1, source_target_pairs={{0,4},{4,8},{8,12},{1,5},{5,9},{9,13},{2,6},{6,10},{10,14},{3,7},{... | collective-permute-start | bytes 1966088 | tf_op jit(solution)/shard_map/ppermute | solution.py:427
  68.3 2.9 %gather.2 = (bf16[512,1024]{1,0:T(8,128)(2,1)}, bf16[512,1024]{1,0:T(8,128)(2,1)}) custom-call(f32[512,512]{1,0:T(8,128)S(1)} %get-tuple-element.33.o_ref, bf16[512,512]{1,0:T(8,128)(2,1)S(1)} %get-tuple-element.34.qe_ref, bf16[4,512,1024]{2,1,0:T(8,128)(2,1)S(1)} %weigh.2.p_ref, bf16[640,512]{1,0:T(8,128)(2,1)S(1)} %collective-permute-done.5.vz_ref), custom_call_target="tpu_custom_call" | custom-call | flops 2000000000 | bytes 1000000 | tf_op jit(solution)/shard_map/gather/pallas_call | solution.py:419
  71.2 11.7 %collective-permute-done.6.vz_ref = bf16[640,512]{1,0:T(8,128)(2,1)S(1)} collective-permute-done((bf16[640,512]{1,0:T(8,128)(2,1)S(1)}, bf16[640,512]{1,0:T(8,128)(2,1)S(1)}, u32[]{:S(2)}, u32[]{:S(2)}) %collective-permute-start.6) | collective-permute-done | bytes 655392 | tf_op jit(solution)/shard_map/ppermute | solution.py:427
  83.0 2.9 %gather.3 = (bf16[512,1024]{1,0:T(8,128)(2,1)}, bf16[512,1024]{1,0:T(8,128)(2,1)}) custom-call(f32[512,512]{1,0:T(8,128)S(1)} %get-tuple-element.45.o_ref, bf16[512,512]{1,0:T(8,128)(2,1)S(1)} %get-tuple-element.46.qe_ref, bf16[4,512,1024]{2,1,0:T(8,128)(2,1)S(1)} %weigh.3.p_ref, ...), custom_call_target="tpu_custom_call", output_to_operand_aliasing={{0}: (4, {}), {1}: (5, {})} | custom-call | flops 2000000000 | bytes 1000000 | tf_op jit(solution)/shard_map/gather/pallas_call | solution.py:419
  (5 shorter events, 0.0 us)
Async XLA Ops:
  0.6 52.0 %collective-permute-start.4 = (bf16[512,1024]{1,0:T(8,128)(2,1)}, bf16[512,1024]{1,0:T(8,128)(2,1)S(1)}, u32[]{:S(2)}, u32[]{:S(2)}) collective-permute-start(bf16[512,1024]{1,0:T(8,128)(2,1)} %ko_ref.3), channel_id=1, source_target_pairs={{0,4},{4,8},{8,12},{1,5},{5,9},{9,13},{2,6},{6,10},{10,14},{3,7},{... | collective-permute-start | bytes 3145736 | tf_op jit(solution)/shard_map/ppermute | solution.py:427
  5.6 1.6 %copy-start = (bf16[512,2,1024]{2,1,0:T(2,128)(2,1)S(1)}, bf16[512,2,1024]{2,1,0:T(2,128)(2,1)}, u32[]{:S(2)}) copy-start(bf16[512,2,1024]{2,1,0:T(2,128)(2,1)} %refs_1_.5) | copy-start | bytes 6291460
  7.2 1.6 %copy-start.1 = (bf16[512,2,1024]{2,1,0:T(2,128)(2,1)S(1)}, bf16[512,2,1024]{2,1,0:T(2,128)(2,1)}, u32[]{:S(2)}) copy-start(bf16[512,2,1024]{2,1,0:T(2,128)(2,1)} %refs_2_.5) | copy-start | bytes 6291460
  8.8 1.2 %copy-start.2 = (bf16[512,1024]{1,0:T(8,128)(2,1)S(1)}, bf16[512,1024]{1,0:T(8,128)(2,1)}, u32[]{:S(2)}) copy-start(bf16[512,1024]{1,0:T(8,128)(2,1)} %refs_0_.5) | copy-start | bytes 3145732
  27.0 12.5 %collective-permute-start = (bf16[4,128,256]{2,1,0:T(8,128)(2,1)S(1)}, bf16[4,128,256]{2,1,0:T(8,128)(2,1)S(1)}, u32[]{:S(2)}, u32[]{:S(2)}) collective-permute-start(bf16[4,128,256]{2,1,0:T(8,128)(2,1)S(1)} %get-tuple-element.36), channel_id=1, source_target_pairs={{0,4},{4,8},{1,5},{5,9},{2,6},{6,10},{3,7},{7,11},{16,20},{20,24},... | collective-permute-start | bytes 786440 | tf_op jit(solution)/shard_map/ppermute | solution.py:427
  28.3 11.2 %collective-permute-start.1 = (bf16[4,128,128]{2,1,0:T(8,128)(2,1)S(1)}, bf16[4,128,128]{2,1,0:T(8,128)(2,1)S(1)}, u32[]{:S(2)}, u32[]{:S(2)}) collective-permute-start(bf16[4,128,128]{2,1,0:T(8,128)(2,1)S(1)} %get-tuple-element.37), channel_id=1, source_target_pairs={{0,8},{1,9},{2,10},{3,11},{16,24},{17,25},{18,26},{19,27}} | collective-permute-start | bytes 393224 | tf_op jit(solution)/shard_map/ppermute | solution.py:427
  40.0 19.6 %collective-permute-start.5 = (bf16[640,512]{1,0:T(8,128)(2,1)S(1)}, bf16[640,512]{1,0:T(8,128)(2,1)S(1)}, u32[]{:S(2)}, u32[]{:S(2)}) collective-permute-start(bf16[640,512]{1,0:T(8,128)(2,1)S(1)} %leave.2), channel_id=1, source_target_pairs={{0,4},{4,8},{8,12},{1,5},{5,9},{9,13},{2,6},{6,10},{10,14},{3,7},{... | collective-permute-start | bytes 1966088 | tf_op jit(solution)/shard_map/ppermute | solution.py:427
  42.1 10.5 %copy-start.3 = (bf16[512,1024]{1,0:T(8,128)(2,1)S(1)}, bf16[512,1024]{1,0:T(8,128)(2,1)}, u32[]{:S(2)}) copy-start(bf16[512,1024]{1,0:T(8,128)(2,1)} %q_ref.3) | copy-start | bytes 3145732
  42.2 10.5 %copy-start.4 = (bf16[512,1024]{1,0:T(8,128)(2,1)S(1)}, bf16[512,1024]{1,0:T(8,128)(2,1)}, u32[]{:S(2)}) copy-start(bf16[512,1024]{1,0:T(8,128)(2,1)} %ko_ref.3) | copy-start | bytes 3145732
  50.0 15.8 %collective-permute-start.2 = (bf16[4,128,256]{2,1,0:T(8,128)(2,1)S(1)}, bf16[4,128,256]{2,1,0:T(8,128)(2,1)S(1)}, u32[]{:S(2)}, u32[]{:S(2)}) collective-permute-start(bf16[4,128,256]{2,1,0:T(8,128)(2,1)S(1)} %get-tuple-element.47), channel_id=1, source_target_pairs={{0,4},{4,8},{1,5},{5,9},{2,6},{6,10},{3,7},{7,11},{16,20},{20,24},... | collective-permute-start | bytes 786440 | tf_op jit(solution)/shard_map/ppermute | solution.py:427
  51.3 14.5 %collective-permute-start.3 = (bf16[4,128,128]{2,1,0:T(8,128)(2,1)S(1)}, bf16[4,128,128]{2,1,0:T(8,128)(2,1)S(1)}, u32[]{:S(2)}, u32[]{:S(2)}) collective-permute-start(bf16[4,128,128]{2,1,0:T(8,128)(2,1)S(1)} %get-tuple-element.48), channel_id=1, source_target_pairs={{0,8},{1,9},{2,10},{3,11},{16,24},{17,25},{18,26},{19,27}} | collective-permute-start | bytes 393224 | tf_op jit(solution)/shard_map/ppermute | solution.py:427
  66.4 16.6 %collective-permute-start.6 = (bf16[640,512]{1,0:T(8,128)(2,1)S(1)}, bf16[640,512]{1,0:T(8,128)(2,1)S(1)}, u32[]{:S(2)}, u32[]{:S(2)}) collective-permute-start(bf16[640,512]{1,0:T(8,128)(2,1)S(1)} %leave.3), channel_id=1, source_target_pairs={{0,4},{4,8},{8,12},{1,5},{5,9},{9,13},{2,6},{6,10},{10,14},{3,7},{... | collective-permute-start | bytes 1966088 | tf_op jit(solution)/shard_map/ppermute | solution.py:427

commit v6 on v5

--- a/solution.py
+++ b/solution.py
@@ -185,9 +185,11 @@
 
 D = 128
 LOCAL = 1
-LIMIT = 40
+LIMIT = 24
+FIRST = 48
 BATCH = 8
 LAG = 2
+STEP = 2
 
 
 def params(mib):
@@ -220,44 +222,22 @@
         r_ref[s, 16:24] = full(pick(ld, (u >= 0) & (u <= i)))
 
 
-def local_body(*refs, HB, NC, first, start, fresh, last):
-    refs = list(refs)
-    q_ref, k_ref, v_ref = refs[:3]
-    y_ref = refs.pop()
-    c = pl.program_id(0)
-    T = q_ref.shape[0] // NC
-    C = 2 * T
+VMEM = pl.BlockSpec(memory_space=pltpu.VMEM)
+
+
+def run_chunks(keys, queries, values, r_ref, y_ref, o_ref, qe_ref, HB, NC, first, chunk_at, out_at):
+    C = keys.shape[0] // NC
+    T = C // 2
     d = D
     H = range(HB)
-    if fresh:
-        o_ref, qe_ref, r_ref, *out = refs[4:]
-    else:
-        r_ref, *more = refs[3:]
-        if start:
-            o_ref, qe_ref, *out = more[3:]
-        else:
-            o_ref, qe_ref, *out = more
-
-    @pl.when(c == 0)
-    def _():
-        if fresh:
-            levels_body(refs[3], r_ref, T=T)
-        if start:
-            y_ref[...] = more[0][...]
-        else:
-            i = lax.broadcasted_iota(jnp.int32, (d, 2 * d), 0)
-            j = lax.broadcasted_iota(jnp.int32, (d, 2 * d), 1)
-            for h in H:
-                y_ref[h] = (j == i + d).astype(f32)
-
     masks, eye = block_masks(C)
     kq, k, q, v, Lr, Lc, br, bc, Lq = ([] for _ in range(9))
     for s in range(NC):
-        rows = r_ref[start + c * NC + s]
+        rows = r_ref[chunk_at + s]
         cols = jnp.transpose(cat([rows, jnp.zeros((C - 24, C), f32)], 0))
-        ks = k_ref[s * T:(s + 1) * T].reshape(C, HB * d)
-        vs = v_ref[s * T:(s + 1) * T].reshape(C, HB * d)
-        qs = q_ref[s * T:(s + 1) * T]
+        ks = keys[s * C:(s + 1) * C]
+        vs = values[s * C:(s + 1) * C]
+        qs = queries[s * T:(s + 1) * T]
         both = cat([ks, qs], 0)
         kq += [both[:, p * d:(p + 2) * d] for p in range(0, HB, 2)]
         for h in H:
@@ -280,52 +260,107 @@
         now = slice(s * HB, (s + 1) * HB)
         Y, o = advance(Y, left[now], add[now], decay[now])
         for h in H:
-            o_ref[s * T:(s + 1) * T, h * d:(h + 1) * d] = o[h][:, :d]
-            qe_ref[s * T:(s + 1) * T, h * d:(h + 1) * d] = o[h][:, d:].astype(bf16)
+            rows = pl.ds(out_at + s * T, T)
+            o_ref[rows, h * d:(h + 1) * d] = o[h][:, :d]
+            qe_ref[rows, h * d:(h + 1) * d] = o[h][:, d:].astype(bf16)
     for h in H:
         y_ref[h] = Y[h]
+    return Y
+
+
+def put(Y, refs):
+    for h, y in enumerate(Y):
+        refs[0][h] = y
+        refs[1][h] = y.astype(bf16)
+        refs[2][h] = y[:, :D].astype(bf16)
+
+
+def open_body(q_ref, k_ref, v_ref, x_ref, o_ref, qe_ref, r_ref, qk_ref, kk_ref, vk_ref, yo_ref, am_ref, a_ref, y_ref, *, HB, NC):
+    c = pl.program_id(0)
+    T = q_ref.shape[0] // NC
+    wg = HB * D
+
+    @pl.when(c == 0)
+    def _():
+        levels_body(x_ref, r_ref, T=T)
+        i = lax.broadcasted_iota(jnp.int32, (D, 2 * D), 0)
+        j = lax.broadcasted_iota(jnp.int32, (D, 2 * D), 1)
+        for h in range(HB):
+            y_ref[h] = (j == i + D).astype(f32)
+
+    flat = lambda ref, at: ref[:, :, at:at + wg].reshape(2 * NC * T, wg)
+    here = pl.multiple_of(c * NC * T, NC * T)
+    double = pl.multiple_of(2 * c * NC * T, 2 * NC * T)
+    qk_ref[pl.ds(here, NC * T)] = q_ref[:, wg:]
+    kk_ref[pl.ds(double, 2 * NC * T)] = flat(k_ref, wg)
+    vk_ref[pl.ds(double, 2 * NC * T)] = flat(v_ref, wg)
+    Y = run_chunks(flat(k_ref, 0), q_ref[:, :wg], flat(v_ref, 0), r_ref, y_ref, o_ref, qe_ref, HB, NC, 0, c * NC, 0)
 
     @pl.when(c == pl.num_programs(0) - 1)
     def _():
-        for h in H:
-            out[0][h] = Y[h]
-            if last:
-                out[1][h] = Y[h].astype(bf16)
-                out[2][h] = Y[h][:, :d].astype(bf16)
-
-
-def local(queries, keys, values, small, g, HB, start, stop, held=(), T=64):
+        put(Y, (yo_ref, am_ref, a_ref))
+
+
+def local_open(queries, keys, values, small, HB, T=64):
     n, w = queries.shape
     wg = HB * D
-    NC = math.gcd(16 // HB, stop - start)
+    NC = math.gcd(16 // HB, n // T)
     B = NC * T
-    at = start // NC
-    fresh, last = small.ndim == 2, stop == n // T
-    flat = pl.BlockSpec((B, wg), lambda c: (at + c, g))
-    pair = pl.BlockSpec((B, 2, wg), lambda c: (at + c, 0, g))
-    out = pl.BlockSpec((B, wg), lambda c: (at + c, 0))
+    flat = pl.BlockSpec((B, w), lambda c: (c, 0))
+    pair = pl.BlockSpec((B, 2, w), lambda c: (c, 0, 0))
+    out = pl.BlockSpec((B, wg), lambda c: (c, 0))
     whole = lambda *s: pl.BlockSpec(s, lambda c: (0,) * len(s))
-    rows = (n // T, 24, 2 * T)
-    any_ = pl.BlockSpec(memory_space=pl.ANY)
-    outs = [(out, (n, wg), f32), (out, (n, wg), bf16)]
-    if fresh:
-        outs.append((whole(*rows), rows, f32))
-    outs.append((whole(HB, D, 2 * D), (HB, D, 2 * D), f32))
-    if last:
-        outs += [(whole(HB, D, 2 * D), (HB, D, 2 * D), bf16), (whole(HB, D, D), (HB, D, D), bf16)]
-    return pl.pallas_call(
-        functools.partial(local_body, HB=HB, NC=NC, first=g * HB, start=start, fresh=fresh, last=last),
-        grid=((stop - start) // NC,),
-        in_specs=[flat, pair, pair, whole(*small.shape), *([whole(HB, D, 2 * D), any_, any_] if held else [])],
-        out_specs=[x[0] for x in outs],
-        out_shape=[jax.ShapeDtypeStruct(x[1], x[2]) for x in outs],
-        input_output_aliases={5: 0, 6: 1} if held else {},
-        scratch_shapes=[pltpu.VMEM((HB, D, 2 * D), f32)],
-        cost_estimate=cost(HB * LOCAL), name="local", compiler_params=params(LIMIT),
-    )(queries, keys, values, small, *held)
-
-
-VMEM = pl.BlockSpec(memory_space=pltpu.VMEM)
+    rows, state = (n // T, 24, 2 * T), (HB, D, 2 * D)
+    outs = [
+        (out, (n, wg), f32), (out, (n, wg), bf16), (whole(*rows), rows, f32),
+        (VMEM, (n, wg), bf16), (VMEM, (2 * n, wg), bf16), (VMEM, (2 * n, wg), bf16),
+        (whole(*state), state, f32), (whole(*state), state, bf16), (whole(HB, D, D), (HB, D, D), bf16),
+    ]
+    return pl.pallas_call(
+        functools.partial(open_body, HB=HB, NC=NC), grid=(n // B,),
+        in_specs=[flat, pair, pair, whole(*small.shape)],
+        out_specs=[x[0] for x in outs], out_shape=[jax.ShapeDtypeStruct(x[1], x[2]) for x in outs],
+        scratch_shapes=[pltpu.VMEM(state, f32)],
+        cost_estimate=cost(HB * LOCAL), name="local_open", compiler_params=params(FIRST),
+    )(queries, keys, values, small)
+
+
+def half_body(q_ref, k_ref, v_ref, r_ref, *refs, HB, NC, start):
+    n = q_ref.shape[0]
+    T = 64
+    if start:
+        y_in, o_ref, qe_ref, yo_ref, am_ref, a_ref, y_ref = refs
+        y_ref[...] = y_in[...]
+    else:
+        o_ref, qe_ref, yo_ref, y_ref = refs
+        i = lax.broadcasted_iota(jnp.int32, (D, 2 * D), 0)
+        j = lax.broadcasted_iota(jnp.int32, (D, 2 * D), 1)
+        for h in range(HB):
+            y_ref[h] = (j == i + D).astype(f32)
+    for s in range(0, o_ref.shape[0] // T, NC):
+        at = start + s
+        token, double = slice(at * T, (at + NC) * T), slice(2 * at * T, 2 * (at + NC) * T)
+        Y = run_chunks(k_ref[double], q_ref[token], v_ref[double], r_ref, y_ref, o_ref, qe_ref, HB, NC, HB, at, s * T)
+    if start:
+        put(Y, (yo_ref, am_ref, a_ref))
+    else:
+        yo_ref[...] = y_ref[...]
+
+
+def local_half(q, k, v, rows, HB, start, stop, state=None, T=64):
+    n, wg = q.shape
+    m = (stop - start) * T
+    shape = (HB, D, 2 * D)
+    outs = [((m, wg), f32), ((m, wg), bf16), (shape, f32)]
+    if start:
+        outs += [(shape, bf16), ((HB, D, D), bf16)]
+    args = (q, k, v, rows) + ((state,) if start else ())
+    return pl.pallas_call(
+        functools.partial(half_body, HB=HB, NC=math.gcd(16 // HB, stop - start), start=start),
+        in_specs=[VMEM] * len(args), out_specs=[VMEM] * len(outs), out_shape=[jax.ShapeDtypeStruct(*x) for x in outs],
+        scratch_shapes=[pltpu.VMEM(shape, f32)],
+        cost_estimate=cost(HB * LOCAL), name="local_half", compiler_params=params(LIMIT),
+    )(*args)
 
 
 def meet_body(am_ref, a_ref, z_ref):
@@ -352,21 +387,27 @@
         cost_estimate=cost(0.3), name="hop", compiler_params=params(8))(y, z)
 
 
-def leave_body(o_ref, qe_ref, y_ref, z_ref, out_ref):
-    n = o_ref.shape[0]
+def leave_body(*refs):
+    parts, (y_ref, z_ref, out_ref) = refs[:-3], refs[-3:]
+    at = 0
+    for o_ref, qe_ref in zip(parts[::2], parts[1::2]):
+        m = o_ref.shape[0]
+        for h in range(z_ref.shape[0]):
+            s = slice(h * D, h * D + D)
+            out_ref[at:at + m, s] = (o_ref[:, s] + dot(qe_ref[:, s], z_ref[h])).astype(bf16)
+        at += m
     for h in range(z_ref.shape[0]):
-        s = slice(h * D, h * D + D)
         z = z_ref[h]
         hi, lo = split(y_ref[h, :, D:])
-        out_ref[:n, s] = (o_ref[:, s] + dot(qe_ref[:, s], z)).astype(bf16)
-        out_ref[n:, s] = (y_ref[h, :, :D] + dot(cat([hi, lo], 1), cat([z, z], 0))).astype(bf16)
-
-
-def leave(o, qe, y, z):
-    n, w = o.shape
-    return pl.pallas_call(
-        leave_body, in_specs=[VMEM] * 4, out_specs=VMEM, out_shape=jax.ShapeDtypeStruct((n + D, w), bf16),
-        cost_estimate=cost(0.5), name="leave", compiler_params=params(8))(o, qe, y, z)
+        out_ref[at:, h * D:h * D + D] = (y_ref[h, :, :D] + dot(cat([hi, lo], 1), cat([z, z], 0))).astype(bf16)
+
+
+def leave(parts, y, z):
+    n = sum(x[0].shape[0] for x in parts)
+    args = [x for p in parts for x in p] + [y, z]
+    return pl.pallas_call(
+        leave_body, in_specs=[VMEM] * len(args), out_specs=VMEM, out_shape=jax.ShapeDtypeStruct((n + D, y.shape[0] * D), bf16),
+        cost_estimate=cost(0.5), name="leave", compiler_params=params(8))(*args)
 
 
 def weigh_body(q_ref, kp_ref, ko_ref, p_ref, *, axis, R, first):
@@ -402,25 +443,30 @@
         cost_estimate=cost(HB * 1.3), name="weigh", compiler_params=params(24))(q, kp, ko)
 
 
-def gather_body(o_ref, qe_ref, p_ref, vz_ref, *refs):
+def gather_body(*refs, step, count):
+    parts, (p_ref, vz_ref) = refs[:2 * count], refs[2 * count:2 * count + 2]
     ret_ref, out_ref = refs[-2:]
-    n = o_ref.shape[0]
-    vz = vz_ref[:, pl.ds(pl.multiple_of(pl.program_id(0) * D, D), D)]
-    ret = (o_ref[...] + dot(qe_ref[...], vz[n:])).astype(bf16)
-    ret_ref[...] = ret
-    out_ref[...] = dot(p_ref[pl.program_id(0)], cat([vz[:n], ret], 0)).astype(bf16)
-
-
-def gather(o, qe, p, vz, carry, g, HB, w):
-    n = o.shape[0]
-    part = pl.BlockSpec((n, D), lambda h: (0, h))
-    flat = pl.BlockSpec((n, D), lambda h: (0, g * HB + h))
+    n = ret_ref.shape[0]
+    for h in range(step):
+        s = slice(h * D, h * D + D)
+        vz = vz_ref[:, pl.ds(pl.multiple_of((pl.program_id(0) * step + h) * D, D), D)]
+        ret = cat([(o[:, s] + dot(qe[:, s], vz[n:])).astype(bf16) for o, qe in zip(parts[::2], parts[1::2])], 0)
+        ret_ref[:, s] = ret
+        out_ref[:, s] = dot(p_ref[pl.program_id(0) * step + h], cat([vz[:n], ret], 0)).astype(bf16)
+
+
+def gather(parts, p, vz, carry, g, HB, w):
+    n = p.shape[1]
+    step = math.gcd(STEP, HB)
+    args = [x for pair in parts for x in pair]
+    flat = pl.BlockSpec((n, step * D), lambda h: (0, g * (HB // step) + h))
     held = [pl.BlockSpec(memory_space=pl.ANY)] * len(carry)
     return pl.pallas_call(
-        gather_body, grid=(HB,), in_specs=[part, part, VMEM, VMEM] + held,
+        functools.partial(gather_body, step=step, count=len(parts)), grid=(HB // step,),
+        in_specs=[pl.BlockSpec((x.shape[0], step * D), lambda h: (0, h)) for x in args] + [VMEM, VMEM] + held,
         out_specs=[flat, flat], out_shape=[jax.ShapeDtypeStruct((n, w), bf16)] * 2,
-        input_output_aliases={4 + i: i for i in range(len(carry))},
-        cost_estimate=cost(HB * 0.5), name="gather", compiler_params=params(24))(o, qe, p, vz, *carry)
+        input_output_aliases={len(args) + 2 + i: i for i in range(len(carry))},
+        cost_estimate=cost(HB * 0.5), name="gather", compiler_params=params(24))(*args, p, vz, *carry)
 
 
 def send(array, pairs):
@@ -435,34 +481,36 @@
     every = [(i, i + 1) for i in range(blocks - 1)]
     keys_behind = send(attn_keys, every)
 
-    def pass_on(o, qe, y, near, far):
+    def pass_on(parts, y, near, far):
         z = meet(near, far)
         for k in range(3, blocks - 1):
             z = z + send(hop(y, z), [(k - 1, k)])
-        return leave(o, qe, y, z)
+        return leave(parts, y, z)
 
     def round_one(am, a):
         far = send(a, [(0, 2)] if blocks > 2 else [])
         return send(am, every[:2]), far
 
     small = cat([betas[:, 0], betas[:, 1], log_decay], 1).transpose(1, 0)
-    o0, qe0, rows, y0, am, a = local(queries, keys, values, small, 0, HB, 0, chunks)
+    o0, qe0, rows, q1, k1, v1, y0, am, a = local_open(queries, keys, values, small, HB)
     near, far = round_one(am, a)
-    o1, qe1, y1 = local(queries, keys, values, rows, 1, HB, 0, chunks // 2)
+    first = ((o0, qe0),)
+    oa, qa, y1 = local_half(q1, k1, v1, rows, HB, 0, chunks // 2)
     near, far, y1 = lax.optimization_barrier((near, far, y1))
-    leaving = pass_on(o0, qe0, y0, near, far)
+    leaving = pass_on(first, y0, near, far)
     leaving, y1 = lax.optimization_barrier((leaving, y1))
     crossing0 = send(leaving, every)
-    o1, qe1, y1, am, a = local(queries, keys, values, rows, 1, HB, chunks // 2, chunks, (y1, o1, qe1))
+    ob, qb, y1, am, a = local_half(q1, k1, v1, rows, HB, chunks // 2, chunks, y1)
+    second = ((oa, qa), (ob, qb))
     near, far = round_one(am, a)
     keys_behind, y1 = lax.optimization_barrier((keys_behind, y1))
     weights = [weigh(attn_queries, keys_behind, attn_keys, 0, HB)]
     keys_behind, crossing0, weights = lax.optimization_barrier((keys_behind, crossing0, weights))
     weights.append(weigh(attn_queries, keys_behind, attn_keys, 1, HB))
     near, far, weights = lax.optimization_barrier((near, far, weights))
-    crossing1 = send(pass_on(o1, qe1, y1, near, far), every)
-    done = gather(o0, qe0, weights[0], crossing0, (), 0, HB, w)
-    return tuple(gather(o1, qe1, weights[1], crossing1, tuple(done), 1, HB, w))
+    crossing1 = send(pass_on(second, y1, near, far), every)
+    done = gather(first, weights[0], crossing0, (), 0, HB, w)
+    return tuple(gather(second, weights[1], crossing1, tuple(done), 1, HB, w))
 
 
 def solution(mesh):

time: 86.5 us -> 83 us (0.960)
  local copies, waits for them, and re-layouts: 5.16 us -> 0.75 us
    unnamed x10 -> x4, local copies, waits for them, and re-layouts: 4.42 us -> 0.01 us
  transfers between devices with their start and end apart: 7 -> 7, of which waited for: 4 -> 4; matrix products, arithmetic and copies ran while one was open for 2% -> 2% of each run, Pallas kernels for 50% -> 53%
where the time goes in v6:
time: 83 us; the launch traced here: 82.5 us
  Pallas kernels  46.3 us (56%)
  waiting for transfers between devices  20.9 us (25%)
  starting transfers between devices  13 us (16%)
    ppermute x7, waiting for transfers between devices, send(): return lax.ppermute(array, 'ctx', pairs) if pairs else jnp.zeros_like(array)  20.9 us
    pallas_call x1, Pallas kernels, local_open(): pl.pallas_call(functools.partial(open_body, HB=HB, NC=NC), grid=(n // B,)...  18.6 us
    pallas_call x2, Pallas kernels, local_half(): pl.pallas_call(functools.partial(half_body, HB=HB, NC=math.gcd(16 // HB,...  15.2 us
    ppermute x7, starting transfers between devices, send(): return lax.ppermute(array, 'ctx', pairs) if pairs else jnp.zeros_like(array)  13 us
    pallas_call x2, Pallas kernels, weigh(): pl.pallas_call(functools.partial(weigh_body, axis=axis, R=R, first=g * HB...  6.63 us
    pallas_call x2, Pallas kernels, gather(): pl.pallas_call(functools.partial(gather_body, step=step, count=len(parts)...  4.79 us
  transfers between devices with their start and end apart: 7, of which 4 were waited for; matrix products, arithmetic and copies ran while one was open for 2% of the time, Pallas kernels for 53%

profile of v6, /device:TPU:16, one launch (start us, length us, event | category | flops | bytes accessed | tf_op | source)
XLA Modules:
  0.0 82.5 jit_solution(1258026415940655411)
XLA Ops:
  0.6 3.5 %collective-permute-start.4 = (bf16[512,1024]{1,0:T(8,128)(2,1)}, bf16[512,1024]{1,0:T(8,128)(2,1)S(1)}, u32[]{:S(2)}, u32[]{:S(2)}) collective-permute-start(bf16[512,1024]{1,0:T(8,128)(2,1)} %ko_ref.3), channel_id=1, source_target_pairs={{0,4},{4,8},{8,12},{1,5},{5,9},{9,13},{2,6},{6,10},{10,14},{3,7},{... | collective-permute-start | bytes 3145736 | tf_op jit(solution)/shard_map/ppermute | solution.py:473
  4.1 0.7 slice_bitcast_fusion.1
  4.9 0.7 maximum_bitcast_fusion.x_ref
  5.6 18.6 %local_open.1 = (f32[512,512]{1,0:T(8,128)S(1)}, bf16[512,512]{1,0:T(8,128)(2,1)S(1)}, f32[8,24,128]{2,1,0:T(8,128)S(1)}, bf16[512,512]{1,0:T(8,128)(2,1)S(1)}, ...) custom-call(bf16[512,1024]{1,0:T(8,128)(2,1)} %q_ref.3, ...), custom_call_target="tpu_custom_call" | custom-call | flops 4000000000 | bytes 1000000 | tf_op jit(solution)/shard_map/local_open/pallas_call | solution.py:319
  24.1 1.3 %collective-permute-start = (bf16[4,128,256]{2,1,0:T(8,128)(2,1)S(1)}, bf16[4,128,256]{2,1,0:T(8,128)(2,1)S(1)}, u32[]{:S(2)}, u32[]{:S(2)}) collective-permute-start(bf16[4,128,256]{2,1,0:T(8,128)(2,1)S(1)} %get-tuple-element.44), channel_id=1, source_target_pairs={{0,4},{4,8},{1,5},{5,9},{2,6},{6,10},{3,7},{7,11},{16,20},{20,24},... | collective-permute-start | bytes 786440 | tf_op jit(solution)/shard_map/ppermute | solution.py:473
  25.4 1.5 %collective-permute-start.1 = (bf16[4,128,128]{2,1,0:T(8,128)(2,1)S(1)}, bf16[4,128,128]{2,1,0:T(8,128)(2,1)S(1)}, u32[]{:S(2)}, u32[]{:S(2)}) collective-permute-start(bf16[4,128,128]{2,1,0:T(8,128)(2,1)S(1)} %get-tuple-element.45), channel_id=1, source_target_pairs={{0,8},{1,9},{2,10},{3,11},{16,24},{17,25},{18,26},{19,27}} | collective-permute-start | bytes 393224 | tf_op jit(solution)/shard_map/ppermute | solution.py:473
  26.9 7.6 %local_half.2 = (f32[256,512]{1,0:T(8,128)S(1)}, bf16[256,512]{1,0:T(8,128)(2,1)S(1)}, f32[4,128,256]{2,1,0:T(8,128)S(1)}) custom-call(bf16[512,512]{1,0:T(8,128)(2,1)S(1)} %get-tuple-element.35.q_ref, bf16[1024,512]{1,0:T(8,128)(2,1)S(1)} %get-tuple-element.36.k_ref, bf16[1024,512]{1,0:T(8,128)(2,1)S(1)} %get-tuple-element.37.v_ref, ...), custom_call_target="tpu_custom_call" | custom-call | flops 4000000000 | bytes 1000000 | tf_op jit(solution)/shard_map/local_half/pallas_call | solution.py:358
  34.6 2.1 %collective-permute-done.1.a_ref = bf16[4,128,128]{2,1,0:T(8,128)(2,1)S(1)} collective-permute-done((bf16[4,128,128]{2,1,0:T(8,128)(2,1)S(1)}, bf16[4,128,128]{2,1,0:T(8,128)(2,1)S(1)}, u32[]{:S(2)}, u32[]{:S(2)}) %collective-permute-start.1) | collective-permute-done | bytes 131104 | tf_op jit(solution)/shard_map/ppermute | solution.py:473
  36.6 0.0 collective-permute-done.am_ref
  36.6 0.2 meet.2.refs_3_
  36.8 0.4 leave.2
  37.2 0.0 copy-start
  37.2 0.0 copy-start.1
  37.2 2.3 %collective-permute-start.5 = (bf16[640,512]{1,0:T(8,128)(2,1)S(1)}, bf16[640,512]{1,0:T(8,128)(2,1)S(1)}, u32[]{:S(2)}, u32[]{:S(2)}) collective-permute-start(bf16[640,512]{1,0:T(8,128)(2,1)S(1)} %leave.2), channel_id=1, source_target_pairs={{0,4},{4,8},{8,12},{1,5},{5,9},{9,13},{2,6},{6,10},{10,14},{3,7},{... | collective-permute-start | bytes 1966088 | tf_op jit(solution)/shard_map/ppermute | solution.py:473
  39.5 7.6 %local_half.3 = (f32[256,512]{1,0:T(8,128)S(1)}, bf16[256,512]{1,0:T(8,128)(2,1)S(1)}, f32[4,128,256]{2,1,0:T(8,128)S(1)}, bf16[4,128,256]{2,1,0:T(8,128)(2,1)S(1)}, bf16[4,128,128]{2,1,0:T(8,128)(2,1)S(1)}) custom-call(bf16[512,512]{1,0:T(8,128)(2,1)S(1)} %get-tuple-element.35.q_ref, bf16[1024,512]{1,0:T(8,128)(2,1)S(1)} %get-tuple-element.36.k_ref, ...), custom_call_target="tpu_custom_call" | custom-call | flops 4000000000 | bytes 1000000 | tf_op jit(solution)/shard_map/local_half/pallas_call | solution.py:358
  47.1 1.3 %collective-permute-start.2 = (bf16[4,128,256]{2,1,0:T(8,128)(2,1)S(1)}, bf16[4,128,256]{2,1,0:T(8,128)(2,1)S(1)}, u32[]{:S(2)}, u32[]{:S(2)}) collective-permute-start(bf16[4,128,256]{2,1,0:T(8,128)(2,1)S(1)} %get-tuple-element.53), channel_id=1, source_target_pairs={{0,4},{4,8},{1,5},{5,9},{2,6},{6,10},{3,7},{7,11},{16,20},{20,24},... | collective-permute-start | bytes 786440 | tf_op jit(solution)/shard_map/ppermute | solution.py:473
  48.4 1.3 %collective-permute-start.3 = (bf16[4,128,128]{2,1,0:T(8,128)(2,1)S(1)}, bf16[4,128,128]{2,1,0:T(8,128)(2,1)S(1)}, u32[]{:S(2)}, u32[]{:S(2)}) collective-permute-start(bf16[4,128,128]{2,1,0:T(8,128)(2,1)S(1)} %get-tuple-element.54), channel_id=1, source_target_pairs={{0,8},{1,9},{2,10},{3,11},{16,24},{17,25},{18,26},{19,27}} | collective-permute-start | bytes 393224 | tf_op jit(solution)/shard_map/ppermute | solution.py:473
  49.7 0.0 collective-permute-done.4.kp_ref
  49.7 0.0 copy-done
  49.7 0.0 copy-done.1
  49.7 3.3 %weigh.2.refs_2_ = bf16[4,512,1024]{2,1,0:T(8,128)(2,1)S(1)} custom-call(bf16[512,1024]{1,0:T(8,128)(2,1)S(1)} %copy-done, bf16[512,1024]{1,0:T(8,128)(2,1)S(1)} %collective-permute-done.4.kp_ref, bf16[512,1024]{1,0:T(8,128)(2,1)S(1)} %copy-done.1), custom_call_target="tpu_custom_call" | custom-call | flops 5200000000 | bytes 1000000 | tf_op jit(solution)/shard_map/weigh/pallas_call | solution.py:439
  53.1 3.8 %collective-permute-done.5.refs_3_ = bf16[640,512]{1,0:T(8,128)(2,1)S(1)} collective-permute-done((bf16[640,512]{1,0:T(8,128)(2,1)S(1)}, bf16[640,512]{1,0:T(8,128)(2,1)S(1)}, u32[]{:S(2)}, u32[]{:S(2)}) %collective-permute-start.5) | collective-permute-done | bytes 655392 | tf_op jit(solution)/shard_map/ppermute | solution.py:473
  56.9 3.3 %weigh.3.refs_4_ = bf16[4,512,1024]{2,1,0:T(8,128)(2,1)S(1)} custom-call(bf16[512,1024]{1,0:T(8,128)(2,1)S(1)} %copy-done, bf16[512,1024]{1,0:T(8,128)(2,1)S(1)} %collective-permute-done.4.kp_ref, bf16[512,1024]{1,0:T(8,128)(2,1)S(1)} %copy-done.1), custom_call_target="tpu_custom_call" | custom-call | flops 5200000000 | bytes 1000000 | tf_op jit(solution)/shard_map/weigh/pallas_call | solution.py:439
  60.2 2.8 %collective-permute-done.3.a_ref = bf16[4,128,128]{2,1,0:T(8,128)(2,1)S(1)} collective-permute-done((bf16[4,128,128]{2,1,0:T(8,128)(2,1)S(1)}, bf16[4,128,128]{2,1,0:T(8,128)(2,1)S(1)}, u32[]{:S(2)}, u32[]{:S(2)}) %collective-permute-start.3) | collective-permute-done | bytes 131104 | tf_op jit(solution)/shard_map/ppermute | solution.py:473
  62.9 0.0 collective-permute-done.2.am_ref
  62.9 0.2 meet.3.refs_5_
  63.1 0.4 leave.3
  63.5 1.9 %collective-permute-start.6 = (bf16[640,512]{1,0:T(8,128)(2,1)S(1)}, bf16[640,512]{1,0:T(8,128)(2,1)S(1)}, u32[]{:S(2)}, u32[]{:S(2)}) collective-permute-start(bf16[640,512]{1,0:T(8,128)(2,1)S(1)} %leave.3), channel_id=1, source_target_pairs={{0,4},{4,8},{8,12},{1,5},{5,9},{9,13},{2,6},{6,10},{10,14},{3,7},{... | collective-permute-start | bytes 1966088 | tf_op jit(solution)/shard_map/ppermute | solution.py:473
  65.4 2.4 %gather.2 = (bf16[512,1024]{1,0:T(8,128)(2,1)}, bf16[512,1024]{1,0:T(8,128)(2,1)}) custom-call(f32[512,512]{1,0:T(8,128)S(1)} %get-tuple-element.41.refs_0_, bf16[512,512]{1,0:T(8,128)(2,1)S(1)} %get-tuple-element.42.refs_1_, bf16[4,512,1024]{2,1,0:T(8,128)(2,1)S(1)} %weigh.2.refs_2_, bf16[640,512]{1,0:T(8,128)(2,1)S(1)} %collective-permute-done.5.refs_3_), custom_call_target="tpu_custom_call" | custom-call | flops 2000000000 | bytes 1000000 | tf_op jit(solution)/shard_map/gather/pallas_call | solution.py:464
  67.8 12.2 %collective-permute-done.6.refs_5_ = bf16[640,512]{1,0:T(8,128)(2,1)S(1)} collective-permute-done((bf16[640,512]{1,0:T(8,128)(2,1)S(1)}, bf16[640,512]{1,0:T(8,128)(2,1)S(1)}, u32[]{:S(2)}, u32[]{:S(2)}) %collective-permute-start.6) | collective-permute-done | bytes 655392 | tf_op jit(solution)/shard_map/ppermute | solution.py:473
  80.1 2.4 %gather.3 = (bf16[512,1024]{1,0:T(8,128)(2,1)}, bf16[512,1024]{1,0:T(8,128)(2,1)}) custom-call(f32[256,512]{1,0:T(8,128)S(1)} %get-tuple-element.39.refs_0_, bf16[256,512]{1,0:T(8,128)(2,1)S(1)} %get-tuple-element.40.refs_1_, f32[256,512]{1,0:T(8,128)S(1)} %get-tuple-element.51.refs_2_, ...), custom_call_target="tpu_custom_call", output_to_operand_aliasing={{0}: (6, {}), {1}: (7, {})} | custom-call | flops 2000000000 | bytes 1000000 | tf_op jit(solution)/shard_map/gather/pallas_call | solution.py:464
Async XLA Ops:
  0.6 49.1 %collective-permute-start.4 = (bf16[512,1024]{1,0:T(8,128)(2,1)}, bf16[512,1024]{1,0:T(8,128)(2,1)S(1)}, u32[]{:S(2)}, u32[]{:S(2)}) collective-permute-start(bf16[512,1024]{1,0:T(8,128)(2,1)} %ko_ref.3), channel_id=1, source_target_pairs={{0,4},{4,8},{8,12},{1,5},{5,9},{9,13},{2,6},{6,10},{10,14},{3,7},{... | collective-permute-start | bytes 3145736 | tf_op jit(solution)/shard_map/ppermute | solution.py:473
  24.1 12.5 %collective-permute-start = (bf16[4,128,256]{2,1,0:T(8,128)(2,1)S(1)}, bf16[4,128,256]{2,1,0:T(8,128)(2,1)S(1)}, u32[]{:S(2)}, u32[]{:S(2)}) collective-permute-start(bf16[4,128,256]{2,1,0:T(8,128)(2,1)S(1)} %get-tuple-element.44), channel_id=1, source_target_pairs={{0,4},{4,8},{1,5},{5,9},{2,6},{6,10},{3,7},{7,11},{16,20},{20,24},... | collective-permute-start | bytes 786440 | tf_op jit(solution)/shard_map/ppermute | solution.py:473
  25.4 11.2 %collective-permute-start.1 = (bf16[4,128,128]{2,1,0:T(8,128)(2,1)S(1)}, bf16[4,128,128]{2,1,0:T(8,128)(2,1)S(1)}, u32[]{:S(2)}, u32[]{:S(2)}) collective-permute-start(bf16[4,128,128]{2,1,0:T(8,128)(2,1)S(1)} %get-tuple-element.45), channel_id=1, source_target_pairs={{0,8},{1,9},{2,10},{3,11},{16,24},{17,25},{18,26},{19,27}} | collective-permute-start | bytes 393224 | tf_op jit(solution)/shard_map/ppermute | solution.py:473
  37.2 12.5 %copy-start = (bf16[512,1024]{1,0:T(8,128)(2,1)S(1)}, bf16[512,1024]{1,0:T(8,128)(2,1)}, u32[]{:S(2)}) copy-start(bf16[512,1024]{1,0:T(8,128)(2,1)} %q_ref.5) | copy-start | bytes 3145732
  37.2 12.5 %copy-start.1 = (bf16[512,1024]{1,0:T(8,128)(2,1)S(1)}, bf16[512,1024]{1,0:T(8,128)(2,1)}, u32[]{:S(2)}) copy-start(bf16[512,1024]{1,0:T(8,128)(2,1)} %ko_ref.3) | copy-start | bytes 3145732
  37.2 19.7 %collective-permute-start.5 = (bf16[640,512]{1,0:T(8,128)(2,1)S(1)}, bf16[640,512]{1,0:T(8,128)(2,1)S(1)}, u32[]{:S(2)}, u32[]{:S(2)}) collective-permute-start(bf16[640,512]{1,0:T(8,128)(2,1)S(1)} %leave.2), channel_id=1, source_target_pairs={{0,4},{4,8},{8,12},{1,5},{5,9},{9,13},{2,6},{6,10},{10,14},{3,7},{... | collective-permute-start | bytes 1966088 | tf_op jit(solution)/shard_map/ppermute | solution.py:473
  47.1 15.9 %collective-permute-start.2 = (bf16[4,128,256]{2,1,0:T(8,128)(2,1)S(1)}, bf16[4,128,256]{2,1,0:T(8,128)(2,1)S(1)}, u32[]{:S(2)}, u32[]{:S(2)}) collective-permute-start(bf16[4,128,256]{2,1,0:T(8,128)(2,1)S(1)} %get-tuple-element.53), channel_id=1, source_target_pairs={{0,4},{4,8},{1,5},{5,9},{2,6},{6,10},{3,7},{7,11},{16,20},{20,24},... | collective-permute-start | bytes 786440 | tf_op jit(solution)/shard_map/ppermute | solution.py:473
  48.4 14.6 %collective-permute-start.3 = (bf16[4,128,128]{2,1,0:T(8,128)(2,1)S(1)}, bf16[4,128,128]{2,1,0:T(8,128)(2,1)S(1)}, u32[]{:S(2)}, u32[]{:S(2)}) collective-permute-start(bf16[4,128,128]{2,1,0:T(8,128)(2,1)S(1)} %get-tuple-element.54), channel_id=1, source_target_pairs={{0,8},{1,9},{2,10},{3,11},{16,24},{17,25},{18,26},{19,27}} | collective-permute-start | bytes 393224 | tf_op jit(solution)/shard_map/ppermute | solution.py:473
  63.5 16.6 %collective-permute-start.6 = (bf16[640,512]{1,0:T(8,128)(2,1)S(1)}, bf16[640,512]{1,0:T(8,128)(2,1)S(1)}, u32[]{:S(2)}, u32[]{:S(2)}) collective-permute-start(bf16[640,512]{1,0:T(8,128)(2,1)S(1)} %leave.3), channel_id=1, source_target_pairs={{0,4},{4,8},{8,12},{1,5},{5,9},{9,13},{2,6},{6,10},{10,14},{3,7},{... | collective-permute-start | bytes 1966088 | tf_op jit(solution)/shard_map/ppermute | solution.py:473

commit v7 on v6

--- a/solution.py
+++ b/solution.py
@@ -189,7 +189,7 @@
 FIRST = 48
 BATCH = 8
 LAG = 2
-STEP = 2
+STEP = 4
 
 
 def params(mib):
@@ -450,7 +450,8 @@
     for h in range(step):
         s = slice(h * D, h * D + D)
         vz = vz_ref[:, pl.ds(pl.multiple_of((pl.program_id(0) * step + h) * D, D), D)]
-        ret = cat([(o[:, s] + dot(qe[:, s], vz[n:])).astype(bf16) for o, qe in zip(parts[::2], parts[1::2])], 0)
+        mine = pl.ds(pl.multiple_of((pl.program_id(0) * step + h) * D, D), D)
+        ret = cat([(o[:, mine] + dot(qe[:, mine], vz[n:])).astype(bf16) for o, qe in zip(parts[::2], parts[1::2])], 0)
         ret_ref[:, s] = ret
         out_ref[:, s] = dot(p_ref[pl.program_id(0) * step + h], cat([vz[:n], ret], 0)).astype(bf16)
 
@@ -463,7 +464,7 @@
     held = [pl.BlockSpec(memory_space=pl.ANY)] * len(carry)
     return pl.pallas_call(
         functools.partial(gather_body, step=step, count=len(parts)), grid=(HB // step,),
-        in_specs=[pl.BlockSpec((x.shape[0], step * D), lambda h: (0, h)) for x in args] + [VMEM, VMEM] + held,
+        in_specs=[VMEM] * (len(args) + 2) + held,
         out_specs=[flat, flat], out_shape=[jax.ShapeDtypeStruct((n, w), bf16)] * 2,
         input_output_aliases={len(args) + 2 + i: i for i in range(len(carry))},
         cost_estimate=cost(HB * 0.5), name="gather", compiler_params=params(24))(*args, p, vz, *carry)

time: 83 us -> 82.8 us (level)
  no operation moved by 1% of the time
where the time goes in v7:
time: 82.8 us; the launch traced here: 82.2 us
  Pallas kernels  45.9 us (55%)
  waiting for transfers between devices  21.1 us (25%)
  starting transfers between devices  13 us (16%)
    ppermute x7, waiting for transfers between devices, send(): return lax.ppermute(array, 'ctx', pairs) if pairs else jnp.zeros_like(array)  21.1 us
    pallas_call x1, Pallas kernels, local_open(): pl.pallas_call(functools.partial(open_body, HB=HB, NC=NC), grid=(n // B,)...  18.6 us
    pallas_call x2, Pallas kernels, local_half(): pl.pallas_call(functools.partial(half_body, HB=HB, NC=math.gcd(16 // HB,...  15.2 us
    ppermute x7, starting transfers between devices, send(): return lax.ppermute(array, 'ctx', pairs) if pairs else jnp.zeros_like(array)  13 us
    pallas_call x2, Pallas kernels, weigh(): pl.pallas_call(functools.partial(weigh_body, axis=axis, R=R, first=g * HB...  6.63 us
    pallas_call x2, Pallas kernels, gather(): pl.pallas_call(functools.partial(gather_body, step=step, count=len(parts)...  4.37 us
  transfers between devices with their start and end apart: 7, of which 4 were waited for; matrix products, arithmetic and copies ran while one was open for 2% of the time, Pallas kernels for 53%

profile of v7, /device:TPU:16, one launch (start us, length us, event | category | flops | bytes accessed | tf_op | source)
XLA Modules:
  0.0 82.2 jit_solution(7795463534212500957)
XLA Ops:
  0.6 3.5 %collective-permute-start.4 = (bf16[512,1024]{1,0:T(8,128)(2,1)}, bf16[512,1024]{1,0:T(8,128)(2,1)S(1)}, u32[]{:S(2)}, u32[]{:S(2)}) collective-permute-start(bf16[512,1024]{1,0:T(8,128)(2,1)} %ko_ref.3), channel_id=1, source_target_pairs={{0,4},{4,8},{8,12},{1,5},{5,9},{9,13},{2,6},{6,10},{10,14},{3,7},{... | collective-permute-start | bytes 3145736 | tf_op jit(solution)/shard_map/ppermute | solution.py:474
  4.1 0.7 slice_bitcast_fusion.1
  4.9 0.7 maximum_bitcast_fusion.x_ref
  5.6 18.6 %local_open.1 = (f32[512,512]{1,0:T(8,128)S(1)}, bf16[512,512]{1,0:T(8,128)(2,1)S(1)}, f32[8,24,128]{2,1,0:T(8,128)S(1)}, bf16[512,512]{1,0:T(8,128)(2,1)S(1)}, ...) custom-call(bf16[512,1024]{1,0:T(8,128)(2,1)} %q_ref.3, ...), custom_call_target="tpu_custom_call" | custom-call | flops 4000000000 | bytes 1000000 | tf_op jit(solution)/shard_map/local_open/pallas_call | solution.py:319
  24.1 1.3 %collective-permute-start = (bf16[4,128,256]{2,1,0:T(8,128)(2,1)S(1)}, bf16[4,128,256]{2,1,0:T(8,128)(2,1)S(1)}, u32[]{:S(2)}, u32[]{:S(2)}) collective-permute-start(bf16[4,128,256]{2,1,0:T(8,128)(2,1)S(1)} %get-tuple-element.44), channel_id=1, source_target_pairs={{0,4},{4,8},{1,5},{5,9},{2,6},{6,10},{3,7},{7,11},{16,20},{20,24},... | collective-permute-start | bytes 786440 | tf_op jit(solution)/shard_map/ppermute | solution.py:474
  25.4 1.5 %collective-permute-start.1 = (bf16[4,128,128]{2,1,0:T(8,128)(2,1)S(1)}, bf16[4,128,128]{2,1,0:T(8,128)(2,1)S(1)}, u32[]{:S(2)}, u32[]{:S(2)}) collective-permute-start(bf16[4,128,128]{2,1,0:T(8,128)(2,1)S(1)} %get-tuple-element.45), channel_id=1, source_target_pairs={{0,8},{1,9},{2,10},{3,11},{16,24},{17,25},{18,26},{19,27}} | collective-permute-start | bytes 393224 | tf_op jit(solution)/shard_map/ppermute | solution.py:474
  26.9 7.6 %local_half.2 = (f32[256,512]{1,0:T(8,128)S(1)}, bf16[256,512]{1,0:T(8,128)(2,1)S(1)}, f32[4,128,256]{2,1,0:T(8,128)S(1)}) custom-call(bf16[512,512]{1,0:T(8,128)(2,1)S(1)} %get-tuple-element.35.q_ref, bf16[1024,512]{1,0:T(8,128)(2,1)S(1)} %get-tuple-element.36.k_ref, bf16[1024,512]{1,0:T(8,128)(2,1)S(1)} %get-tuple-element.37.v_ref, ...), custom_call_target="tpu_custom_call" | custom-call | flops 4000000000 | bytes 1000000 | tf_op jit(solution)/shard_map/local_half/pallas_call | solution.py:358
  34.6 2.1 %collective-permute-done.1.a_ref = bf16[4,128,128]{2,1,0:T(8,128)(2,1)S(1)} collective-permute-done((bf16[4,128,128]{2,1,0:T(8,128)(2,1)S(1)}, bf16[4,128,128]{2,1,0:T(8,128)(2,1)S(1)}, u32[]{:S(2)}, u32[]{:S(2)}) %collective-permute-start.1) | collective-permute-done | bytes 131104 | tf_op jit(solution)/shard_map/ppermute | solution.py:474
  36.6 0.0 collective-permute-done.am_ref
  36.6 0.2 meet.2.refs_3_
  36.8 0.4 leave.2
  37.2 0.0 copy-start
  37.2 0.0 copy-start.1
  37.2 2.3 %collective-permute-start.5 = (bf16[640,512]{1,0:T(8,128)(2,1)S(1)}, bf16[640,512]{1,0:T(8,128)(2,1)S(1)}, u32[]{:S(2)}, u32[]{:S(2)}) collective-permute-start(bf16[640,512]{1,0:T(8,128)(2,1)S(1)} %leave.2), channel_id=1, source_target_pairs={{0,4},{4,8},{8,12},{1,5},{5,9},{9,13},{2,6},{6,10},{10,14},{3,7},{... | collective-permute-start | bytes 1966088 | tf_op jit(solution)/shard_map/ppermute | solution.py:474
  39.5 7.6 %local_half.3 = (f32[256,512]{1,0:T(8,128)S(1)}, bf16[256,512]{1,0:T(8,128)(2,1)S(1)}, f32[4,128,256]{2,1,0:T(8,128)S(1)}, bf16[4,128,256]{2,1,0:T(8,128)(2,1)S(1)}, bf16[4,128,128]{2,1,0:T(8,128)(2,1)S(1)}) custom-call(bf16[512,512]{1,0:T(8,128)(2,1)S(1)} %get-tuple-element.35.q_ref, bf16[1024,512]{1,0:T(8,128)(2,1)S(1)} %get-tuple-element.36.k_ref, ...), custom_call_target="tpu_custom_call" | custom-call | flops 4000000000 | bytes 1000000 | tf_op jit(solution)/shard_map/local_half/pallas_call | solution.py:358
  47.1 1.3 %collective-permute-start.2 = (bf16[4,128,256]{2,1,0:T(8,128)(2,1)S(1)}, bf16[4,128,256]{2,1,0:T(8,128)(2,1)S(1)}, u32[]{:S(2)}, u32[]{:S(2)}) collective-permute-start(bf16[4,128,256]{2,1,0:T(8,128)(2,1)S(1)} %get-tuple-element.53), channel_id=1, source_target_pairs={{0,4},{4,8},{1,5},{5,9},{2,6},{6,10},{3,7},{7,11},{16,20},{20,24},... | collective-permute-start | bytes 786440 | tf_op jit(solution)/shard_map/ppermute | solution.py:474
  48.4 1.3 %collective-permute-start.3 = (bf16[4,128,128]{2,1,0:T(8,128)(2,1)S(1)}, bf16[4,128,128]{2,1,0:T(8,128)(2,1)S(1)}, u32[]{:S(2)}, u32[]{:S(2)}) collective-permute-start(bf16[4,128,128]{2,1,0:T(8,128)(2,1)S(1)} %get-tuple-element.54), channel_id=1, source_target_pairs={{0,8},{1,9},{2,10},{3,11},{16,24},{17,25},{18,26},{19,27}} | collective-permute-start | bytes 393224 | tf_op jit(solution)/shard_map/ppermute | solution.py:474
  49.7 0.0 collective-permute-done.4.kp_ref
  49.7 0.0 copy-done
  49.7 0.0 copy-done.1
  49.7 3.3 %weigh.2.refs_2_ = bf16[4,512,1024]{2,1,0:T(8,128)(2,1)S(1)} custom-call(bf16[512,1024]{1,0:T(8,128)(2,1)S(1)} %copy-done, bf16[512,1024]{1,0:T(8,128)(2,1)S(1)} %collective-permute-done.4.kp_ref, bf16[512,1024]{1,0:T(8,128)(2,1)S(1)} %copy-done.1), custom_call_target="tpu_custom_call" | custom-call | flops 5200000000 | bytes 1000000 | tf_op jit(solution)/shard_map/weigh/pallas_call | solution.py:439
  53.1 3.8 %collective-permute-done.5.refs_3_ = bf16[640,512]{1,0:T(8,128)(2,1)S(1)} collective-permute-done((bf16[640,512]{1,0:T(8,128)(2,1)S(1)}, bf16[640,512]{1,0:T(8,128)(2,1)S(1)}, u32[]{:S(2)}, u32[]{:S(2)}) %collective-permute-start.5) | collective-permute-done | bytes 655392 | tf_op jit(solution)/shard_map/ppermute | solution.py:474
  56.9 3.3 %weigh.3.refs_4_ = bf16[4,512,1024]{2,1,0:T(8,128)(2,1)S(1)} custom-call(bf16[512,1024]{1,0:T(8,128)(2,1)S(1)} %copy-done, bf16[512,1024]{1,0:T(8,128)(2,1)S(1)} %collective-permute-done.4.kp_ref, bf16[512,1024]{1,0:T(8,128)(2,1)S(1)} %copy-done.1), custom_call_target="tpu_custom_call" | custom-call | flops 5200000000 | bytes 1000000 | tf_op jit(solution)/shard_map/weigh/pallas_call | solution.py:439
  60.2 2.8 %collective-permute-done.3.a_ref = bf16[4,128,128]{2,1,0:T(8,128)(2,1)S(1)} collective-permute-done((bf16[4,128,128]{2,1,0:T(8,128)(2,1)S(1)}, bf16[4,128,128]{2,1,0:T(8,128)(2,1)S(1)}, u32[]{:S(2)}, u32[]{:S(2)}) %collective-permute-start.3) | collective-permute-done | bytes 131104 | tf_op jit(solution)/shard_map/ppermute | solution.py:474
  62.9 0.0 collective-permute-done.2.am_ref
  62.9 0.2 meet.3.refs_5_
  63.1 0.4 leave.3
  63.5 1.9 %collective-permute-start.6 = (bf16[640,512]{1,0:T(8,128)(2,1)S(1)}, bf16[640,512]{1,0:T(8,128)(2,1)S(1)}, u32[]{:S(2)}, u32[]{:S(2)}) collective-permute-start(bf16[640,512]{1,0:T(8,128)(2,1)S(1)} %leave.3), channel_id=1, source_target_pairs={{0,4},{4,8},{8,12},{1,5},{5,9},{9,13},{2,6},{6,10},{10,14},{3,7},{... | collective-permute-start | bytes 1966088 | tf_op jit(solution)/shard_map/ppermute | solution.py:474
  65.4 2.2 %gather.2 = (bf16[512,1024]{1,0:T(8,128)(2,1)}, bf16[512,1024]{1,0:T(8,128)(2,1)}) custom-call(f32[512,512]{1,0:T(8,128)S(1)} %get-tuple-element.41.refs_0_, bf16[512,512]{1,0:T(8,128)(2,1)S(1)} %get-tuple-element.42.refs_1_, bf16[4,512,1024]{2,1,0:T(8,128)(2,1)S(1)} %weigh.2.refs_2_, bf16[640,512]{1,0:T(8,128)(2,1)S(1)} %collective-permute-done.5.refs_3_), custom_call_target="tpu_custom_call" | custom-call | flops 2000000000 | bytes 1000000 | tf_op jit(solution)/shard_map/gather/pallas_call | solution.py:465
  67.6 12.4 %collective-permute-done.6.refs_5_ = bf16[640,512]{1,0:T(8,128)(2,1)S(1)} collective-permute-done((bf16[640,512]{1,0:T(8,128)(2,1)S(1)}, bf16[640,512]{1,0:T(8,128)(2,1)S(1)}, u32[]{:S(2)}, u32[]{:S(2)}) %collective-permute-start.6) | collective-permute-done | bytes 655392 | tf_op jit(solution)/shard_map/ppermute | solution.py:474
  80.1 2.2 %gather.3 = (bf16[512,1024]{1,0:T(8,128)(2,1)}, bf16[512,1024]{1,0:T(8,128)(2,1)}) custom-call(f32[256,512]{1,0:T(8,128)S(1)} %get-tuple-element.39.refs_0_, bf16[256,512]{1,0:T(8,128)(2,1)S(1)} %get-tuple-element.40.refs_1_, f32[256,512]{1,0:T(8,128)S(1)} %get-tuple-element.51.refs_2_, ...), custom_call_target="tpu_custom_call", output_to_operand_aliasing={{0}: (6, {}), {1}: (7, {})} | custom-call | flops 2000000000 | bytes 1000000 | tf_op jit(solution)/shard_map/gather/pallas_call | solution.py:465
Async XLA Ops:
  0.6 49.1 %collective-permute-start.4 = (bf16[512,1024]{1,0:T(8,128)(2,1)}, bf16[512,1024]{1,0:T(8,128)(2,1)S(1)}, u32[]{:S(2)}, u32[]{:S(2)}) collective-permute-start(bf16[512,1024]{1,0:T(8,128)(2,1)} %ko_ref.3), channel_id=1, source_target_pairs={{0,4},{4,8},{8,12},{1,5},{5,9},{9,13},{2,6},{6,10},{10,14},{3,7},{... | collective-permute-start | bytes 3145736 | tf_op jit(solution)/shard_map/ppermute | solution.py:474
  24.1 12.5 %collective-permute-start = (bf16[4,128,256]{2,1,0:T(8,128)(2,1)S(1)}, bf16[4,128,256]{2,1,0:T(8,128)(2,1)S(1)}, u32[]{:S(2)}, u32[]{:S(2)}) collective-permute-start(bf16[4,128,256]{2,1,0:T(8,128)(2,1)S(1)} %get-tuple-element.44), channel_id=1, source_target_pairs={{0,4},{4,8},{1,5},{5,9},{2,6},{6,10},{3,7},{7,11},{16,20},{20,24},... | collective-permute-start | bytes 786440 | tf_op jit(solution)/shard_map/ppermute | solution.py:474
  25.4 11.2 %collective-permute-start.1 = (bf16[4,128,128]{2,1,0:T(8,128)(2,1)S(1)}, bf16[4,128,128]{2,1,0:T(8,128)(2,1)S(1)}, u32[]{:S(2)}, u32[]{:S(2)}) collective-permute-start(bf16[4,128,128]{2,1,0:T(8,128)(2,1)S(1)} %get-tuple-element.45), channel_id=1, source_target_pairs={{0,8},{1,9},{2,10},{3,11},{16,24},{17,25},{18,26},{19,27}} | collective-permute-start | bytes 393224 | tf_op jit(solution)/shard_map/ppermute | solution.py:474
  37.2 12.5 %copy-start = (bf16[512,1024]{1,0:T(8,128)(2,1)S(1)}, bf16[512,1024]{1,0:T(8,128)(2,1)}, u32[]{:S(2)}) copy-start(bf16[512,1024]{1,0:T(8,128)(2,1)} %q_ref.5) | copy-start | bytes 3145732
  37.2 12.5 %copy-start.1 = (bf16[512,1024]{1,0:T(8,128)(2,1)S(1)}, bf16[512,1024]{1,0:T(8,128)(2,1)}, u32[]{:S(2)}) copy-start(bf16[512,1024]{1,0:T(8,128)(2,1)} %ko_ref.3) | copy-start | bytes 3145732
  37.2 19.7 %collective-permute-start.5 = (bf16[640,512]{1,0:T(8,128)(2,1)S(1)}, bf16[640,512]{1,0:T(8,128)(2,1)S(1)}, u32[]{:S(2)}, u32[]{:S(2)}) collective-permute-start(bf16[640,512]{1,0:T(8,128)(2,1)S(1)} %leave.2), channel_id=1, source_target_pairs={{0,4},{4,8},{8,12},{1,5},{5,9},{9,13},{2,6},{6,10},{10,14},{3,7},{... | collective-permute-start | bytes 1966088 | tf_op jit(solution)/shard_map/ppermute | solution.py:474
  47.1 15.9 %collective-permute-start.2 = (bf16[4,128,256]{2,1,0:T(8,128)(2,1)S(1)}, bf16[4,128,256]{2,1,0:T(8,128)(2,1)S(1)}, u32[]{:S(2)}, u32[]{:S(2)}) collective-permute-start(bf16[4,128,256]{2,1,0:T(8,128)(2,1)S(1)} %get-tuple-element.53), channel_id=1, source_target_pairs={{0,4},{4,8},{1,5},{5,9},{2,6},{6,10},{3,7},{7,11},{16,20},{20,24},... | collective-permute-start | bytes 786440 | tf_op jit(solution)/shard_map/ppermute | solution.py:474
  48.4 14.6 %collective-permute-start.3 = (bf16[4,128,128]{2,1,0:T(8,128)(2,1)S(1)}, bf16[4,128,128]{2,1,0:T(8,128)(2,1)S(1)}, u32[]{:S(2)}, u32[]{:S(2)}) collective-permute-start(bf16[4,128,128]{2,1,0:T(8,128)(2,1)S(1)} %get-tuple-element.54), channel_id=1, source_target_pairs={{0,8},{1,9},{2,10},{3,11},{16,24},{17,25},{18,26},{19,27}} | collective-permute-start | bytes 393224 | tf_op jit(solution)/shard_map/ppermute | solution.py:474
  63.5 16.6 %collective-permute-start.6 = (bf16[640,512]{1,0:T(8,128)(2,1)S(1)}, bf16[640,512]{1,0:T(8,128)(2,1)S(1)}, u32[]{:S(2)}, u32[]{:S(2)}) collective-permute-start(bf16[640,512]{1,0:T(8,128)(2,1)S(1)} %leave.3), channel_id=1, source_target_pairs={{0,4},{4,8},{8,12},{1,5},{5,9},{9,13},{2,6},{6,10},{10,14},{3,7},{... | collective-permute-start | bytes 1966088 | tf_op jit(solution)/shard_map/ppermute | solution.py:474

commit v8 on v7

--- a/solution.py
+++ b/solution.py
@@ -188,7 +188,7 @@
 LIMIT = 24
 FIRST = 48
 BATCH = 8
-LAG = 2
+LAG = 3
 STEP = 4
 
 

time: 82.8 us -> 83.3 us (level)
  no operation moved by 1% of the time
where the time goes in v8:
time: 83.3 us; the launch traced here: 82.8 us
  Pallas kernels  46.5 us (56%)
  waiting for transfers between devices  20.9 us (25%)
  starting transfers between devices  13 us (16%)
    ppermute x7, waiting for transfers between devices, send(): return lax.ppermute(array, 'ctx', pairs) if pairs else jnp.zeros_like(array)  20.9 us
    pallas_call x1, Pallas kernels, local_open(): pl.pallas_call(functools.partial(open_body, HB=HB, NC=NC), grid=(n // B,)...  18.9 us
    pallas_call x2, Pallas kernels, local_half(): pl.pallas_call(functools.partial(half_body, HB=HB, NC=math.gcd(16 // HB,...  15.6 us
    ppermute x7, starting transfers between devices, send(): return lax.ppermute(array, 'ctx', pairs) if pairs else jnp.zeros_like(array)  13 us
    pallas_call x2, Pallas kernels, weigh(): pl.pallas_call(functools.partial(weigh_body, axis=axis, R=R, first=g * HB...  6.65 us
    pallas_call x2, Pallas kernels, gather(): pl.pallas_call(functools.partial(gather_body, step=step, count=len(parts)...  4.37 us
  transfers between devices with their start and end apart: 7, of which 4 were waited for; matrix products, arithmetic and copies ran while one was open for 2% of the time, Pallas kernels for 53%

profile of v8, /device:TPU:16, one launch (start us, length us, event | category | flops | bytes accessed | tf_op | source)
XLA Modules:
  0.0 82.8 jit_solution(7267497227577499262)
XLA Ops:
  0.6 3.5 %collective-permute-start.4 = (bf16[512,1024]{1,0:T(8,128)(2,1)}, bf16[512,1024]{1,0:T(8,128)(2,1)S(1)}, u32[]{:S(2)}, u32[]{:S(2)}) collective-permute-start(bf16[512,1024]{1,0:T(8,128)(2,1)} %ko_ref.3), channel_id=1, source_target_pairs={{0,4},{4,8},{8,12},{1,5},{5,9},{9,13},{2,6},{6,10},{10,14},{3,7},{... | collective-permute-start | bytes 3145736 | tf_op jit(solution)/shard_map/ppermute | solution.py:474
  4.1 0.7 slice_bitcast_fusion.1
  4.9 0.7 maximum_bitcast_fusion.x_ref
  5.6 18.9 %local_open.1 = (f32[512,512]{1,0:T(8,128)S(1)}, bf16[512,512]{1,0:T(8,128)(2,1)S(1)}, f32[8,24,128]{2,1,0:T(8,128)S(1)}, bf16[512,512]{1,0:T(8,128)(2,1)S(1)}, ...) custom-call(bf16[512,1024]{1,0:T(8,128)(2,1)} %q_ref.3, ...), custom_call_target="tpu_custom_call" | custom-call | flops 4000000000 | bytes 1000000 | tf_op jit(solution)/shard_map/local_open/pallas_call | solution.py:319
  24.5 1.3 %collective-permute-start = (bf16[4,128,256]{2,1,0:T(8,128)(2,1)S(1)}, bf16[4,128,256]{2,1,0:T(8,128)(2,1)S(1)}, u32[]{:S(2)}, u32[]{:S(2)}) collective-permute-start(bf16[4,128,256]{2,1,0:T(8,128)(2,1)S(1)} %get-tuple-element.44), channel_id=1, source_target_pairs={{0,4},{4,8},{1,5},{5,9},{2,6},{6,10},{3,7},{7,11},{16,20},{20,24},... | collective-permute-start | bytes 786440 | tf_op jit(solution)/shard_map/ppermute | solution.py:474
  25.8 1.5 %collective-permute-start.1 = (bf16[4,128,128]{2,1,0:T(8,128)(2,1)S(1)}, bf16[4,128,128]{2,1,0:T(8,128)(2,1)S(1)}, u32[]{:S(2)}, u32[]{:S(2)}) collective-permute-start(bf16[4,128,128]{2,1,0:T(8,128)(2,1)S(1)} %get-tuple-element.45), channel_id=1, source_target_pairs={{0,8},{1,9},{2,10},{3,11},{16,24},{17,25},{18,26},{19,27}} | collective-permute-start | bytes 393224 | tf_op jit(solution)/shard_map/ppermute | solution.py:474
  27.3 7.8 %local_half.2 = (f32[256,512]{1,0:T(8,128)S(1)}, bf16[256,512]{1,0:T(8,128)(2,1)S(1)}, f32[4,128,256]{2,1,0:T(8,128)S(1)}) custom-call(bf16[512,512]{1,0:T(8,128)(2,1)S(1)} %get-tuple-element.35.q_ref, bf16[1024,512]{1,0:T(8,128)(2,1)S(1)} %get-tuple-element.36.k_ref, bf16[1024,512]{1,0:T(8,128)(2,1)S(1)} %get-tuple-element.37.v_ref, ...), custom_call_target="tpu_custom_call" | custom-call | flops 4000000000 | bytes 1000000 | tf_op jit(solution)/shard_map/local_half/pallas_call | solution.py:358
  35.0 1.9 %collective-permute-done.1.a_ref = bf16[4,128,128]{2,1,0:T(8,128)(2,1)S(1)} collective-permute-done((bf16[4,128,128]{2,1,0:T(8,128)(2,1)S(1)}, bf16[4,128,128]{2,1,0:T(8,128)(2,1)S(1)}, u32[]{:S(2)}, u32[]{:S(2)}) %collective-permute-start.1) | collective-permute-done | bytes 131104 | tf_op jit(solution)/shard_map/ppermute | solution.py:474
  36.9 0.0 collective-permute-done.am_ref
  37.0 0.2 meet.2.refs_3_
  37.1 0.4 leave.2
  37.5 0.0 copy-start
  37.5 0.0 copy-start.1
  37.5 2.3 %collective-permute-start.5 = (bf16[640,512]{1,0:T(8,128)(2,1)S(1)}, bf16[640,512]{1,0:T(8,128)(2,1)S(1)}, u32[]{:S(2)}, u32[]{:S(2)}) collective-permute-start(bf16[640,512]{1,0:T(8,128)(2,1)S(1)} %leave.2), channel_id=1, source_target_pairs={{0,4},{4,8},{8,12},{1,5},{5,9},{9,13},{2,6},{6,10},{10,14},{3,7},{... | collective-permute-start | bytes 1966088 | tf_op jit(solution)/shard_map/ppermute | solution.py:474
  39.8 7.8 %local_half.3 = (f32[256,512]{1,0:T(8,128)S(1)}, bf16[256,512]{1,0:T(8,128)(2,1)S(1)}, f32[4,128,256]{2,1,0:T(8,128)S(1)}, bf16[4,128,256]{2,1,0:T(8,128)(2,1)S(1)}, bf16[4,128,128]{2,1,0:T(8,128)(2,1)S(1)}) custom-call(bf16[512,512]{1,0:T(8,128)(2,1)S(1)} %get-tuple-element.35.q_ref, bf16[1024,512]{1,0:T(8,128)(2,1)S(1)} %get-tuple-element.36.k_ref, ...), custom_call_target="tpu_custom_call" | custom-call | flops 4000000000 | bytes 1000000 | tf_op jit(solution)/shard_map/local_half/pallas_call | solution.py:358
  47.6 1.3 %collective-permute-start.2 = (bf16[4,128,256]{2,1,0:T(8,128)(2,1)S(1)}, bf16[4,128,256]{2,1,0:T(8,128)(2,1)S(1)}, u32[]{:S(2)}, u32[]{:S(2)}) collective-permute-start(bf16[4,128,256]{2,1,0:T(8,128)(2,1)S(1)} %get-tuple-element.53), channel_id=1, source_target_pairs={{0,4},{4,8},{1,5},{5,9},{2,6},{6,10},{3,7},{7,11},{16,20},{20,24},... | collective-permute-start | bytes 786440 | tf_op jit(solution)/shard_map/ppermute | solution.py:474
  48.9 1.3 %collective-permute-start.3 = (bf16[4,128,128]{2,1,0:T(8,128)(2,1)S(1)}, bf16[4,128,128]{2,1,0:T(8,128)(2,1)S(1)}, u32[]{:S(2)}, u32[]{:S(2)}) collective-permute-start(bf16[4,128,128]{2,1,0:T(8,128)(2,1)S(1)} %get-tuple-element.54), channel_id=1, source_target_pairs={{0,8},{1,9},{2,10},{3,11},{16,24},{17,25},{18,26},{19,27}} | collective-permute-start | bytes 393224 | tf_op jit(solution)/shard_map/ppermute | solution.py:474
  50.2 0.0 collective-permute-done.4.kp_ref
  50.2 0.0 copy-done
  50.2 0.0 copy-done.1
  50.2 3.3 %weigh.2.refs_2_ = bf16[4,512,1024]{2,1,0:T(8,128)(2,1)S(1)} custom-call(bf16[512,1024]{1,0:T(8,128)(2,1)S(1)} %copy-done, bf16[512,1024]{1,0:T(8,128)(2,1)S(1)} %collective-permute-done.4.kp_ref, bf16[512,1024]{1,0:T(8,128)(2,1)S(1)} %copy-done.1), custom_call_target="tpu_custom_call" | custom-call | flops 5200000000 | bytes 1000000 | tf_op jit(solution)/shard_map/weigh/pallas_call | solution.py:439
  53.6 3.7 %collective-permute-done.5.refs_3_ = bf16[640,512]{1,0:T(8,128)(2,1)S(1)} collective-permute-done((bf16[640,512]{1,0:T(8,128)(2,1)S(1)}, bf16[640,512]{1,0:T(8,128)(2,1)S(1)}, u32[]{:S(2)}, u32[]{:S(2)}) %collective-permute-start.5) | collective-permute-done | bytes 655392 | tf_op jit(solution)/shard_map/ppermute | solution.py:474
  57.2 3.3 %weigh.3.refs_4_ = bf16[4,512,1024]{2,1,0:T(8,128)(2,1)S(1)} custom-call(bf16[512,1024]{1,0:T(8,128)(2,1)S(1)} %copy-done, bf16[512,1024]{1,0:T(8,128)(2,1)S(1)} %collective-permute-done.4.kp_ref, bf16[512,1024]{1,0:T(8,128)(2,1)S(1)} %copy-done.1), custom_call_target="tpu_custom_call" | custom-call | flops 5200000000 | bytes 1000000 | tf_op jit(solution)/shard_map/weigh/pallas_call | solution.py:439
  60.5 2.9 %collective-permute-done.3.a_ref = bf16[4,128,128]{2,1,0:T(8,128)(2,1)S(1)} collective-permute-done((bf16[4,128,128]{2,1,0:T(8,128)(2,1)S(1)}, bf16[4,128,128]{2,1,0:T(8,128)(2,1)S(1)}, u32[]{:S(2)}, u32[]{:S(2)}) %collective-permute-start.3) | collective-permute-done | bytes 131104 | tf_op jit(solution)/shard_map/ppermute | solution.py:474
  63.5 0.0 collective-permute-done.2.am_ref
  63.5 0.2 meet.3.refs_5_
  63.6 0.4 leave.3
  64.0 1.9 %collective-permute-start.6 = (bf16[640,512]{1,0:T(8,128)(2,1)S(1)}, bf16[640,512]{1,0:T(8,128)(2,1)S(1)}, u32[]{:S(2)}, u32[]{:S(2)}) collective-permute-start(bf16[640,512]{1,0:T(8,128)(2,1)S(1)} %leave.3), channel_id=1, source_target_pairs={{0,4},{4,8},{8,12},{1,5},{5,9},{9,13},{2,6},{6,10},{10,14},{3,7},{... | collective-permute-start | bytes 1966088 | tf_op jit(solution)/shard_map/ppermute | solution.py:474
  65.9 2.2 %gather.2 = (bf16[512,1024]{1,0:T(8,128)(2,1)}, bf16[512,1024]{1,0:T(8,128)(2,1)}) custom-call(f32[512,512]{1,0:T(8,128)S(1)} %get-tuple-element.41.refs_0_, bf16[512,512]{1,0:T(8,128)(2,1)S(1)} %get-tuple-element.42.refs_1_, bf16[4,512,1024]{2,1,0:T(8,128)(2,1)S(1)} %weigh.2.refs_2_, bf16[640,512]{1,0:T(8,128)(2,1)S(1)} %collective-permute-done.5.refs_3_), custom_call_target="tpu_custom_call" | custom-call | flops 2000000000 | bytes 1000000 | tf_op jit(solution)/shard_map/gather/pallas_call | solution.py:465
  68.1 12.5 %collective-permute-done.6.refs_5_ = bf16[640,512]{1,0:T(8,128)(2,1)S(1)} collective-permute-done((bf16[640,512]{1,0:T(8,128)(2,1)S(1)}, bf16[640,512]{1,0:T(8,128)(2,1)S(1)}, u32[]{:S(2)}, u32[]{:S(2)}) %collective-permute-start.6) | collective-permute-done | bytes 655392 | tf_op jit(solution)/shard_map/ppermute | solution.py:474
  80.6 2.2 %gather.3 = (bf16[512,1024]{1,0:T(8,128)(2,1)}, bf16[512,1024]{1,0:T(8,128)(2,1)}) custom-call(f32[256,512]{1,0:T(8,128)S(1)} %get-tuple-element.39.refs_0_, bf16[256,512]{1,0:T(8,128)(2,1)S(1)} %get-tuple-element.40.refs_1_, f32[256,512]{1,0:T(8,128)S(1)} %get-tuple-element.51.refs_2_, ...), custom_call_target="tpu_custom_call", output_to_operand_aliasing={{0}: (6, {}), {1}: (7, {})} | custom-call | flops 2000000000 | bytes 1000000 | tf_op jit(solution)/shard_map/gather/pallas_call | solution.py:465
Async XLA Ops:
  0.6 49.6 %collective-permute-start.4 = (bf16[512,1024]{1,0:T(8,128)(2,1)}, bf16[512,1024]{1,0:T(8,128)(2,1)S(1)}, u32[]{:S(2)}, u32[]{:S(2)}) collective-permute-start(bf16[512,1024]{1,0:T(8,128)(2,1)} %ko_ref.3), channel_id=1, source_target_pairs={{0,4},{4,8},{8,12},{1,5},{5,9},{9,13},{2,6},{6,10},{10,14},{3,7},{... | collective-permute-start | bytes 3145736 | tf_op jit(solution)/shard_map/ppermute | solution.py:474
  24.5 12.5 %collective-permute-start = (bf16[4,128,256]{2,1,0:T(8,128)(2,1)S(1)}, bf16[4,128,256]{2,1,0:T(8,128)(2,1)S(1)}, u32[]{:S(2)}, u32[]{:S(2)}) collective-permute-start(bf16[4,128,256]{2,1,0:T(8,128)(2,1)S(1)} %get-tuple-element.44), channel_id=1, source_target_pairs={{0,4},{4,8},{1,5},{5,9},{2,6},{6,10},{3,7},{7,11},{16,20},{20,24},... | collective-permute-start | bytes 786440 | tf_op jit(solution)/shard_map/ppermute | solution.py:474
  25.8 11.2 %collective-permute-start.1 = (bf16[4,128,128]{2,1,0:T(8,128)(2,1)S(1)}, bf16[4,128,128]{2,1,0:T(8,128)(2,1)S(1)}, u32[]{:S(2)}, u32[]{:S(2)}) collective-permute-start(bf16[4,128,128]{2,1,0:T(8,128)(2,1)S(1)} %get-tuple-element.45), channel_id=1, source_target_pairs={{0,8},{1,9},{2,10},{3,11},{16,24},{17,25},{18,26},{19,27}} | collective-permute-start | bytes 393224 | tf_op jit(solution)/shard_map/ppermute | solution.py:474
  37.5 12.7 %copy-start = (bf16[512,1024]{1,0:T(8,128)(2,1)S(1)}, bf16[512,1024]{1,0:T(8,128)(2,1)}, u32[]{:S(2)}) copy-start(bf16[512,1024]{1,0:T(8,128)(2,1)} %q_ref.5) | copy-start | bytes 3145732
  37.5 12.7 %copy-start.1 = (bf16[512,1024]{1,0:T(8,128)(2,1)S(1)}, bf16[512,1024]{1,0:T(8,128)(2,1)}, u32[]{:S(2)}) copy-start(bf16[512,1024]{1,0:T(8,128)(2,1)} %ko_ref.3) | copy-start | bytes 3145732
  37.5 19.7 %collective-permute-start.5 = (bf16[640,512]{1,0:T(8,128)(2,1)S(1)}, bf16[640,512]{1,0:T(8,128)(2,1)S(1)}, u32[]{:S(2)}, u32[]{:S(2)}) collective-permute-start(bf16[640,512]{1,0:T(8,128)(2,1)S(1)} %leave.2), channel_id=1, source_target_pairs={{0,4},{4,8},{8,12},{1,5},{5,9},{9,13},{2,6},{6,10},{10,14},{3,7},{... | collective-permute-start | bytes 1966088 | tf_op jit(solution)/shard_map/ppermute | solution.py:474
  47.6 15.9 %collective-permute-start.2 = (bf16[4,128,256]{2,1,0:T(8,128)(2,1)S(1)}, bf16[4,128,256]{2,1,0:T(8,128)(2,1)S(1)}, u32[]{:S(2)}, u32[]{:S(2)}) collective-permute-start(bf16[4,128,256]{2,1,0:T(8,128)(2,1)S(1)} %get-tuple-element.53), channel_id=1, source_target_pairs={{0,4},{4,8},{1,5},{5,9},{2,6},{6,10},{3,7},{7,11},{16,20},{20,24},... | collective-permute-start | bytes 786440 | tf_op jit(solution)/shard_map/ppermute | solution.py:474
  48.9 14.6 %collective-permute-start.3 = (bf16[4,128,128]{2,1,0:T(8,128)(2,1)S(1)}, bf16[4,128,128]{2,1,0:T(8,128)(2,1)S(1)}, u32[]{:S(2)}, u32[]{:S(2)}) collective-permute-start(bf16[4,128,128]{2,1,0:T(8,128)(2,1)S(1)} %get-tuple-element.54), channel_id=1, source_target_pairs={{0,8},{1,9},{2,10},{3,11},{16,24},{17,25},{18,26},{19,27}} | collective-permute-start | bytes 393224 | tf_op jit(solution)/shard_map/ppermute | solution.py:474
  64.0 16.6 %collective-permute-start.6 = (bf16[640,512]{1,0:T(8,128)(2,1)S(1)}, bf16[640,512]{1,0:T(8,128)(2,1)S(1)}, u32[]{:S(2)}, u32[]{:S(2)}) collective-permute-start(bf16[640,512]{1,0:T(8,128)(2,1)S(1)} %leave.3), channel_id=1, source_target_pairs={{0,4},{4,8},{8,12},{1,5},{5,9},{9,13},{2,6},{6,10},{10,14},{3,7},{... | collective-permute-start | bytes 1966088 | tf_op jit(solution)/shard_map/ppermute | solution.py:474
